TPU v7x, 128 devices: a whole 4x4x4 slice. The times are simulated.
128 devices in a mesh: seq: 16 (over y, x), dp: 8 (over z, core).
Axes of the slice: x: 4, y: 4, z: 4, core: 2. Of those that a mesh axis runs over, the one named last changes fastest.
Arguments:
- block_in: bfloat16 [16, 2048, 1536], P('dp', 'seq'), may hold values from -6 to 6
- cotangent: bfloat16 [16, 2048, 1536], P('dp', 'seq'), may hold values from -6 to 6
- in_master: float32 [1536, 6448], P(('seq', 'dp')), may hold values from -0.15625 to 0.15625
- in_moment1: float32 [1536, 6448], P(('seq', 'dp')), may hold values from -64 to 64
- in_moment2: float32 [1536, 6448], P(('seq', 'dp')), may hold values from 216.2688 to 3440.64
- out_master: float32 [3072, 1536], P(('seq', 'dp')), may hold values from -0.109375 to 0.109375
- out_moment1: float32 [3072, 1536], P(('seq', 'dp')), may hold values from -128 to 128
- out_moment2: float32 [3072, 1536], P(('seq', 'dp')), may hold values from 851.968 to 13762.56
- conv_master: float32 [5, 3328], P(None, ('seq', 'dp')), may hold values from -3 to 3
- conv_moment1: float32 [5, 3328], P(None, ('seq', 'dp')), may hold values from -64 to 64
- conv_moment2: float32 [5, 3328], P(None, ('seq', 'dp')), may hold values from 216.2688 to 3440.64
- gain_master: float32 [4608], P(('seq', 'dp')), may hold values from 0.1 to 1.9
- gain_moment1: float32 [4608], P(('seq', 'dp')), may hold values from -128 to 128
- gain_moment2: float32 [4608], P(('seq', 'dp')), may hold values from 851.968 to 13762.56
- head_master: float32 [3, 48], replicated, may hold values from -9.5 to 1.5
- head_moment1: float32 [3, 48], replicated, may hold values from -256 to 256
- head_moment2: float32 [3, 48], replicated, may hold values from 5033.165 to 79691.77
Outputs:
- block_out: bfloat16 [16, 2048, 1536], P('dp', 'seq')
- input_grad: float32 [16, 2048, 1536], P('dp', 'seq')
- in_moment1_next: float32 [1536, 6448], P(('seq', 'dp'))
- in_moment2_next: float32 [1536, 6448], P(('seq', 'dp'))
- in_master_next: float32 [1536, 6448], P(('seq', 'dp'))
- out_moment1_next: float32 [3072, 1536], P(('seq', 'dp'))
- out_moment2_next: float32 [3072, 1536], P(('seq', 'dp'))
- out_master_next: float32 [3072, 1536], P(('seq', 'dp'))
- conv_moment1_next: float32 [5, 3328], P(None, ('seq', 'dp'))
- conv_moment2_next: float32 [5, 3328], P(None, ('seq', 'dp'))
- conv_master_next: float32 [5, 3328], P(None, ('seq', 'dp'))
- gain_moment1_next: float32 [4608], P(('seq', 'dp'))
- gain_moment2_next: float32 [4608], P(('seq', 'dp'))
- gain_master_next: float32 [4608], P(('seq', 'dp'))
- head_moment1_next: float32 [3, 48], replicated
- head_moment2_next: float32 [3, 48], replicated
- head_master_next: float32 [3, 48], replicated
All inputs are finite; a program needn't handle non-finite values.
Results may differ from a plain program's by a relative error of at most 0.012.
The roundings to bfloat16 on the way count: a program that leaves them out, or rounds other values in their place, can miss the bound.
Values may be sent and summed in bfloat16 or wider, within the bound.
No kernel may reach another device: no remote copies, remote signals or barrier semaphores. Data moves between devices by JAX's collectives and lax.ppermute only.
A program may use at most 256 MiB of HBM per device.

v0:
```python
import jax
import jax.numpy as jnp
from jax import lax
from jax.sharding import PartitionSpec as P

INNER = 3072
STATE = 128
HEADDIM = 64
KERNEL = 4
STEP = 5
HEADS = 48
CONV = 3328


NORM_EPS = 1e-05
PRECISE = lax.Precision.HIGHEST
BETA_ONE = 0.9
BETA_TWO = 0.95
ADAM_EPS = 1e-08
MATRIX_RATE = 0.05
SMALL_RATE = 0.5
MATRIX_DECAY = 0.1


def from_behind(value, axis, steps):
    count = lax.axis_size(axis)
    leading, last = (max(0, -steps), min(count, count - steps))
    return lax.ppermute(value, axis, [(source, source + steps) for source in range(leading, last)])


def for_sending(x):

    def short(part):
        return part.astype(jnp.bfloat16) if part.dtype == jnp.float32 else part

    return jax.tree.map(short, x)


def rms_scale(values, gain):
    return values * lax.rsqrt(jnp.mean(values * values, axis=-1, keepdims=True) + NORM_EPS) * gain


def gate_norm(mixed_out, gate_proj, gain):
    return rms_scale(mixed_out * jax.nn.silu(gate_proj), gain)


def prepare(conv_input, dt_raw, edge_rows, conv_weights, head_params):
    sequences, length = conv_input.shape[:2]
    extended = jnp.concatenate([edge_rows, conv_input], axis=1)
    preact = conv_weights[KERNEL] + conv_weights[0] * extended[:, 0:length]
    for offset in range(1, KERNEL):
        preact = preact + conv_weights[offset] * extended[:, offset : offset + length]
    activated = jax.nn.silu(preact)
    head_x = activated[:, :, :INNER].reshape(sequences, length, HEADS, HEADDIM)
    b_proj = activated[:, :, INNER : INNER + STATE]
    c_proj = activated[:, :, INNER + STATE :]
    step_size = jax.nn.softplus(dt_raw + head_params[1])
    cumulative = jnp.cumsum(step_size * -jnp.exp(head_params[0]), axis=1)
    return (head_x, step_size, b_proj, c_proj, cumulative)


def ssd_local(head_x, step_size, b_proj, c_proj, cumulative, skip_gain, incoming):
    sequences, length = step_size.shape[:2]
    row_ids = lax.broadcasted_iota(jnp.int32, (length, length), 0)
    col_ids = lax.broadcasted_iota(jnp.int32, (length, length), 1)
    causal = row_ids >= col_ids
    by_head = jnp.transpose(cumulative, (0, 2, 1))
    differ = by_head[:, :, :, None] - by_head[:, :, None, :]
    decay_mask = jnp.where(causal, jnp.exp(jnp.where(causal, differ, 0.0)), 0.0)
    scores = jnp.einsum("sln,smn->slm", c_proj, b_proj, precision=PRECISE)
    mixing = scores[:, None] * decay_mask * jnp.transpose(step_size, (0, 2, 1))[:, :, None, :]
    within = jnp.einsum("shlm,smhp->slhp", mixing, head_x, precision=PRECISE)
    carried = (
        jnp.einsum("sln,shpn->slhp", c_proj, incoming, precision=PRECISE)
        * jnp.exp(cumulative)[:, :, :, None]
    )
    outputs = within + carried + skip_gain[:, None] * head_x
    return outputs.reshape(sequences, length, INNER)


def end_state(head_x, step_size, b_proj, cumulative):
    tail_weight = jnp.exp(cumulative[:, -1:] - cumulative) * step_size
    return jnp.einsum("smh,smhp,smn->shpn", tail_weight, head_x, b_proj, precision=PRECISE)


def pass_states(decay_total, local_end):

    def one_turn(turn, arriving):
        return from_behind(decay_total[:, :, None, None] * arriving + local_end, "seq", 1)

    return lax.fori_loop(0, lax.axis_size("seq") - 1, one_turn, jnp.zeros_like(local_end))


def pass_grads(decay_total, local_back):

    def one_turn(turn, arriving):
        return from_behind(decay_total[:, :, None, None] * arriving + local_back, "seq", -1)

    return lax.fori_loop(0, lax.axis_size("seq") - 1, one_turn, jnp.zeros_like(local_back))


def adamw_step(weight, gradient, moment_one, moment_two, step_rate, weight_decay):
    one_next = BETA_ONE * moment_one + (1.0 - BETA_ONE) * gradient
    two_next = BETA_TWO * moment_two + (1.0 - BETA_TWO) * gradient * gradient
    corrected = one_next / (1.0 - BETA_ONE**STEP)
    scale_next = jnp.sqrt(two_next / (1.0 - BETA_TWO**STEP)) + ADAM_EPS
    weight_next = weight - step_rate * (corrected / scale_next + weight_decay * weight)
    return (one_next, two_next, weight_next)


def on_device(
    block_in,
    cotangent,
    in_master,
    in_moment1,
    in_moment2,
    out_master,
    out_moment1,
    out_moment2,
    conv_master,
    conv_moment1,
    conv_moment2,
    gain_master,
    gain_moment1,
    gain_moment2,
    head_master,
    head_moment1,
    head_moment2,
):
    w_in, w_out, conv_low, gain_low = (
        lax.all_gather(in_master.astype(jnp.bfloat16), ("seq", "dp"), axis=0, tiled=True),
        lax.all_gather(out_master.astype(jnp.bfloat16), ("seq", "dp"), axis=0, tiled=True),
        lax.all_gather(conv_master.astype(jnp.bfloat16), ("seq", "dp"), axis=1, tiled=True),
        lax.all_gather(gain_master.astype(jnp.bfloat16), ("seq", "dp"), axis=0, tiled=True),
    )
    conv_weights = conv_low.astype(jnp.float32)
    gain_values = gain_low.astype(jnp.float32)
    sequences, length, width = block_in.shape
    tokens = block_in.astype(jnp.float32).reshape(sequences * length, width)
    normed, norm_pull = jax.vjp(rms_scale, tokens, gain_values[:width])
    normed_low = normed.astype(jnp.bfloat16)
    projected = jnp.dot(normed_low, w_in, preferred_element_type=jnp.float32)
    gate_proj = projected[:, :INNER]
    conv_input = projected[:, INNER : INNER + CONV].reshape(sequences, length, CONV)
    dt_raw = projected[:, INNER + CONV :].reshape(sequences, length, HEADS)
    edge_rows = from_behind(
        conv_input[:, length - KERNEL + 1 :].astype(jnp.bfloat16), "seq", 1
    ).astype(jnp.float32)
    prepared, prep_pull = jax.vjp(prepare, conv_input, dt_raw, edge_rows, conv_weights, head_master)
    head_x, step_size, b_proj, c_proj, cumulative = prepared
    decay_total = jnp.exp(cumulative[:, -1])
    local_end, end_pull = jax.vjp(end_state, head_x, step_size, b_proj, cumulative)
    incoming = pass_states(decay_total, local_end)
    mixed_out, ssd_pull = jax.vjp(
        ssd_local, head_x, step_size, b_proj, c_proj, cumulative, head_master[2], incoming
    )
    gated_out, gate_pull = jax.vjp(
        gate_norm, mixed_out.reshape(sequences * length, INNER), gate_proj, gain_values[width:]
    )
    gated_low = gated_out.astype(jnp.bfloat16)
    output = tokens + jnp.dot(gated_low, w_out, preferred_element_type=jnp.float32)
    block_out = output.astype(jnp.bfloat16).reshape(sequences, length, width)
    upstream = cotangent.reshape(sequences * length, width)
    out_grad = jnp.einsum("ti,td->id", gated_low, upstream, preferred_element_type=jnp.float32)
    d_gated = jnp.einsum("td,id->ti", upstream, w_out, preferred_element_type=jnp.float32)
    d_mixed, d_gate, d_gate_gain = gate_pull(d_gated)
    d_x1, d_step1, d_b1, d_c1, d_cum1, d_skip, local_back = ssd_pull(
        d_mixed.reshape(sequences, length, INNER)
    )
    leaving = pass_grads(decay_total, local_back)
    d_x2, d_step2, d_b2, d_cum2 = end_pull(leaving)
    d_total = jnp.sum(leaving * incoming, axis=(2, 3)) * decay_total
    d_cum = (d_cum1 + d_cum2).at[:, -1].add(d_total)
    d_input, d_dt, d_edge, d_conv, d_head = prep_pull(
        (d_x1 + d_x2, d_step1 + d_step2, d_b1 + d_b2, d_c1, d_cum)
    )
    back_edge = from_behind(for_sending(d_edge), "seq", -1).astype(d_edge.dtype)
    d_input = d_input.at[:, length - KERNEL + 1 :].add(back_edge)
    d_projected = jnp.concatenate(
        [
            d_gate,
            d_input.reshape(sequences * length, CONV),
            d_dt.reshape(sequences * length, HEADS),
        ],
        axis=1,
    ).astype(jnp.bfloat16)
    in_grad = jnp.einsum("td,tp->dp", normed_low, d_projected, preferred_element_type=jnp.float32)
    d_normed = jnp.einsum("tp,dp->td", d_projected, w_in, preferred_element_type=jnp.float32)
    d_tokens, d_norm_gain = norm_pull(d_normed)
    input_grad = (upstream.astype(jnp.float32) + d_tokens).reshape(sequences, length, width)
    gain_grad = jnp.concatenate([d_norm_gain, d_gate_gain])
    head_grad = d_head.at[2].add(d_skip)
    in_share, out_share, conv_share, gain_share = (
        lax.psum_scatter(in_grad, ("seq", "dp"), scatter_dimension=0, tiled=True),
        lax.psum_scatter(out_grad, ("seq", "dp"), scatter_dimension=0, tiled=True),
        lax.psum_scatter(d_conv, ("seq", "dp"), scatter_dimension=1, tiled=True),
        lax.psum_scatter(gain_grad, ("seq", "dp"), scatter_dimension=0, tiled=True),
    )
    head_share = lax.psum(head_grad, ("seq", "dp"))
    in_next = adamw_step(in_master, in_share, in_moment1, in_moment2, MATRIX_RATE, MATRIX_DECAY)
    out_next = adamw_step(
        out_master, out_share, out_moment1, out_moment2, MATRIX_RATE, MATRIX_DECAY
    )
    conv_next = adamw_step(conv_master, conv_share, conv_moment1, conv_moment2, SMALL_RATE, 0.0)
    gain_next = adamw_step(gain_master, gain_share, gain_moment1, gain_moment2, SMALL_RATE, 0.0)
    head_next = adamw_step(head_master, head_share, head_moment1, head_moment2, SMALL_RATE, 0.0)
    return (
        block_out,
        input_grad,
        in_next[0],
        in_next[1],
        in_next[2],
        out_next[0],
        out_next[1],
        out_next[2],
        conv_next[0],
        conv_next[1],
        conv_next[2],
        gain_next[0],
        gain_next[1],
        gain_next[2],
        head_next[0],
        head_next[1],
        head_next[2],
    )


def solution(mesh):
    return jax.shard_map(
        on_device,
        mesh=mesh,
        in_specs=(
            P("dp", "seq", None),
            P("dp", "seq", None),
            P(("seq", "dp"), None),
            P(("seq", "dp"), None),
            P(("seq", "dp"), None),
            P(("seq", "dp"), None),
            P(("seq", "dp"), None),
            P(("seq", "dp"), None),
            P(None, ("seq", "dp")),
            P(None, ("seq", "dp")),
            P(None, ("seq", "dp")),
            P(("seq", "dp")),
            P(("seq", "dp")),
            P(("seq", "dp")),
            P(),
            P(),
            P(),
        ),
        out_specs=(
            P("dp", "seq", None),
            P("dp", "seq", None),
            P(("seq", "dp"), None),
            P(("seq", "dp"), None),
            P(("seq", "dp"), None),
            P(("seq", "dp"), None),
            P(("seq", "dp"), None),
            P(("seq", "dp"), None),
            P(None, ("seq", "dp")),
            P(None, ("seq", "dp")),
            P(None, ("seq", "dp")),
            P(("seq", "dp")),
            P(("seq", "dp")),
            P(("seq", "dp")),
            P(),
            P(),
            P(),
        ),
        check_vma=False,
    )
```

profile of v0, /device:TPU:7, one launch (start us, length us, event | category | flops | bytes accessed | tf_op | source)
XLA Modules:
  0.0 3863.7 jit_solution(1297959317183135781)
XLA Ops:
  10.0 66.8 %all-reduce.15 = bf16[4608]{0:T(1024)(128)(2,1)S(1)} all-reduce(bf16[4608]{0:T(1024)(128)(2,1)S(1)} %dynamic-update-slice.9), channel_id=1, replica_groups=mesh['seq'=16,'dp'=8] {'seq','dp'}, use_global_device_ids=true, to_apply=%add.15 | all-reduce | flops 4608 | bytes 18432
  193.8 1054.5 %while.23 = (s32[]{:T(128)}, f32[2,48,64,128]{3,2,1,0:T(8,128)S(1)}, f32[2,48]{1,0:T(2,128)S(1)}, f32[2,48,64,128]{3,2,1,0:T(8,128)}, s32[]{:T(128)}) while((s32[]{:T(128)}, f32[2,48,64,128]{3,2,1,0:T(8,128)S(1)}, f32[2,48]{1,0:T(2,128)S(1)}, f32[2,48,64,128]{3,2,1,0:T(8,128)}, s32[]{:T(128)}) %tuple.100), condition=%wide.region_3.4_spmd, body=%wide.region_2.3_spmd.sunk | while | flops 1572866 | bytes 22020580 | solution.py:91
  201.1 68.1 %collective-permute-done = f32[2,48,64,128]{3,2,1,0:T(8,128)S(1)} collective-permute-done((f32[2,48,64,128]{3,2,1,0:T(8,128)}, f32[2,48,64,128]{3,2,1,0:T(8,128)S(1)}, u32[]{:S(2)}, u32[]{:S(2)}) %collective-permute-start) | collective-permute-done | bytes 3145760 | tf_op jit(solution)/shard_map/while/body/eval_jaxpr/ppermute | solution.py:28
  277.6 66.0 %collective-permute-done = f32[2,48,64,128]{3,2,1,0:T(8,128)S(1)} collective-permute-done((f32[2,48,64,128]{3,2,1,0:T(8,128)}, f32[2,48,64,128]{3,2,1,0:T(8,128)S(1)}, u32[]{:S(2)}, u32[]{:S(2)}) %collective-permute-start) | collective-permute-done | bytes 3145760 | tf_op jit(solution)/shard_map/while/body/eval_jaxpr/ppermute | solution.py:28
  353.2 64.5 %collective-permute-done = f32[2,48,64,128]{3,2,1,0:T(8,128)S(1)} collective-permute-done((f32[2,48,64,128]{3,2,1,0:T(8,128)}, f32[2,48,64,128]{3,2,1,0:T(8,128)S(1)}, u32[]{:S(2)}, u32[]{:S(2)}) %collective-permute-start) | collective-permute-done | bytes 3145760 | tf_op jit(solution)/shard_map/while/body/eval_jaxpr/ppermute | solution.py:28
  427.8 63.6 %collective-permute-done = f32[2,48,64,128]{3,2,1,0:T(8,128)S(1)} collective-permute-done((f32[2,48,64,128]{3,2,1,0:T(8,128)}, f32[2,48,64,128]{3,2,1,0:T(8,128)S(1)}, u32[]{:S(2)}, u32[]{:S(2)}) %collective-permute-start) | collective-permute-done | bytes 3145760 | tf_op jit(solution)/shard_map/while/body/eval_jaxpr/ppermute | solution.py:28
  501.6 62.7 %collective-permute-done = f32[2,48,64,128]{3,2,1,0:T(8,128)S(1)} collective-permute-done((f32[2,48,64,128]{3,2,1,0:T(8,128)}, f32[2,48,64,128]{3,2,1,0:T(8,128)S(1)}, u32[]{:S(2)}, u32[]{:S(2)}) %collective-permute-start) | collective-permute-done | bytes 3145760 | tf_op jit(solution)/shard_map/while/body/eval_jaxpr/ppermute | solution.py:28
  574.4 61.8 %collective-permute-done = f32[2,48,64,128]{3,2,1,0:T(8,128)S(1)} collective-permute-done((f32[2,48,64,128]{3,2,1,0:T(8,128)}, f32[2,48,64,128]{3,2,1,0:T(8,128)S(1)}, u32[]{:S(2)}, u32[]{:S(2)}) %collective-permute-start) | collective-permute-done | bytes 3145760 | tf_op jit(solution)/shard_map/while/body/eval_jaxpr/ppermute | solution.py:28
  646.3 60.8 %collective-permute-done = f32[2,48,64,128]{3,2,1,0:T(8,128)S(1)} collective-permute-done((f32[2,48,64,128]{3,2,1,0:T(8,128)}, f32[2,48,64,128]{3,2,1,0:T(8,128)S(1)}, u32[]{:S(2)}, u32[]{:S(2)}) %collective-permute-start) | collective-permute-done | bytes 3145760 | tf_op jit(solution)/shard_map/while/body/eval_jaxpr/ppermute | solution.py:28
  717.3 59.9 %collective-permute-done = f32[2,48,64,128]{3,2,1,0:T(8,128)S(1)} collective-permute-done((f32[2,48,64,128]{3,2,1,0:T(8,128)}, f32[2,48,64,128]{3,2,1,0:T(8,128)S(1)}, u32[]{:S(2)}, u32[]{:S(2)}) %collective-permute-start) | collective-permute-done | bytes 3145760 | tf_op jit(solution)/shard_map/while/body/eval_jaxpr/ppermute | solution.py:28
  1295.9 247.8 %reduce-scatter.5.cloned.1.call-done = f32[24,1536]{1,0:T(8,128)} async-done(((f32[3072,1536]{1,0:T(8,128)}), f32[24,1536]{1,0:T(8,128)}) %reduce-scatter.5.cloned.1.call-update) | async-done | bytes 147472 | tf_op jit(solution)/shard_map/reduce_scatter | solution.py:195
  1549.2 69.4 %all-gather.5.cloned.1.call-done = bf16[3072,1536]{1,0:T(8,128)(2,1)} async-done(((bf16[24,1536]{1,0:T(8,128)(2,1)}), bf16[3072,1536]{1,0:T(8,128)(2,1)}) %all-gather.5.cloned.1.call-update) | async-done | bytes 9437200 | tf_op jit(solution)/shard_map/all_gather | solution.py:132
  1665.4 1082.7 %while.24 = (s32[]{:T(128)}, f32[2,48,64,128]{3,2,1,0:T(8,128)}, f32[2,48]{1,0:T(2,128)S(1)}, f32[2,48,64,128]{3,2,1,0:T(8,128)}, s32[]{:T(128)}) while((s32[]{:T(128)}, f32[2,48,64,128]{3,2,1,0:T(8,128)}, f32[2,48]{1,0:T(2,128)S(1)}, f32[2,48,64,128]{3,2,1,0:T(8,128)}, s32[]{:T(128)}) %tuple.114), condition=%wide.region_8.9_spmd, body=%wide.region_7.8_spmd.sunk | while | flops 1572866 | bytes 22020580 | solution.py:99
  1672.7 71.3 %collective-permute-done.1 = f32[2,48,64,128]{3,2,1,0:T(8,128)} collective-permute-done((f32[2,48,64,128]{3,2,1,0:T(8,128)}, f32[2,48,64,128]{3,2,1,0:T(8,128)}, u32[]{:S(2)}, u32[]{:S(2)}) %collective-permute-start.1) | collective-permute-done | bytes 3145760 | tf_op jit(solution)/shard_map/while/body/eval_jaxpr/ppermute | solution.py:28
  1750.7 70.9 %collective-permute-done.1 = f32[2,48,64,128]{3,2,1,0:T(8,128)} collective-permute-done((f32[2,48,64,128]{3,2,1,0:T(8,128)}, f32[2,48,64,128]{3,2,1,0:T(8,128)}, u32[]{:S(2)}, u32[]{:S(2)}) %collective-permute-start.1) | collective-permute-done | bytes 3145760 | tf_op jit(solution)/shard_map/while/body/eval_jaxpr/ppermute | solution.py:28
  1828.3 70.0 %collective-permute-done.1 = f32[2,48,64,128]{3,2,1,0:T(8,128)} collective-permute-done((f32[2,48,64,128]{3,2,1,0:T(8,128)}, f32[2,48,64,128]{3,2,1,0:T(8,128)}, u32[]{:S(2)}, u32[]{:S(2)}) %collective-permute-start.1) | collective-permute-done | bytes 3145760 | tf_op jit(solution)/shard_map/while/body/eval_jaxpr/ppermute | solution.py:28
  1905.1 69.1 %collective-permute-done.1 = f32[2,48,64,128]{3,2,1,0:T(8,128)} collective-permute-done((f32[2,48,64,128]{3,2,1,0:T(8,128)}, f32[2,48,64,128]{3,2,1,0:T(8,128)}, u32[]{:S(2)}, u32[]{:S(2)}) %collective-permute-start.1) | collective-permute-done | bytes 3145760 | tf_op jit(solution)/shard_map/while/body/eval_jaxpr/ppermute | solution.py:28
  1980.9 68.1 %collective-permute-done.1 = f32[2,48,64,128]{3,2,1,0:T(8,128)} collective-permute-done((f32[2,48,64,128]{3,2,1,0:T(8,128)}, f32[2,48,64,128]{3,2,1,0:T(8,128)}, u32[]{:S(2)}, u32[]{:S(2)}) %collective-permute-start.1) | collective-permute-done | bytes 3145760 | tf_op jit(solution)/shard_map/while/body/eval_jaxpr/ppermute | solution.py:28
  2055.8 67.2 %collective-permute-done.1 = f32[2,48,64,128]{3,2,1,0:T(8,128)} collective-permute-done((f32[2,48,64,128]{3,2,1,0:T(8,128)}, f32[2,48,64,128]{3,2,1,0:T(8,128)}, u32[]{:S(2)}, u32[]{:S(2)}) %collective-permute-start.1) | collective-permute-done | bytes 3145760 | tf_op jit(solution)/shard_map/while/body/eval_jaxpr/ppermute | solution.py:28
  2129.7 66.3 %collective-permute-done.1 = f32[2,48,64,128]{3,2,1,0:T(8,128)} collective-permute-done((f32[2,48,64,128]{3,2,1,0:T(8,128)}, f32[2,48,64,128]{3,2,1,0:T(8,128)}, u32[]{:S(2)}, u32[]{:S(2)}) %collective-permute-start.1) | collective-permute-done | bytes 3145760 | tf_op jit(solution)/shard_map/while/body/eval_jaxpr/ppermute | solution.py:28
  2202.8 65.4 %collective-permute-done.1 = f32[2,48,64,128]{3,2,1,0:T(8,128)} collective-permute-done((f32[2,48,64,128]{3,2,1,0:T(8,128)}, f32[2,48,64,128]{3,2,1,0:T(8,128)}, u32[]{:S(2)}, u32[]{:S(2)}) %collective-permute-start.1) | collective-permute-done | bytes 3145760 | tf_op jit(solution)/shard_map/while/body/eval_jaxpr/ppermute | solution.py:28
  2274.9 64.4 %collective-permute-done.1 = f32[2,48,64,128]{3,2,1,0:T(8,128)} collective-permute-done((f32[2,48,64,128]{3,2,1,0:T(8,128)}, f32[2,48,64,128]{3,2,1,0:T(8,128)}, u32[]{:S(2)}, u32[]{:S(2)}) %collective-permute-start.1) | collective-permute-done | bytes 3145760 | tf_op jit(solution)/shard_map/while/body/eval_jaxpr/ppermute | solution.py:28
  2346.1 63.5 %collective-permute-done.1 = f32[2,48,64,128]{3,2,1,0:T(8,128)} collective-permute-done((f32[2,48,64,128]{3,2,1,0:T(8,128)}, f32[2,48,64,128]{3,2,1,0:T(8,128)}, u32[]{:S(2)}, u32[]{:S(2)}) %collective-permute-start.1) | collective-permute-done | bytes 3145760 | tf_op jit(solution)/shard_map/while/body/eval_jaxpr/ppermute | solution.py:28
  2416.4 62.6 %collective-permute-done.1 = f32[2,48,64,128]{3,2,1,0:T(8,128)} collective-permute-done((f32[2,48,64,128]{3,2,1,0:T(8,128)}, f32[2,48,64,128]{3,2,1,0:T(8,128)}, u32[]{:S(2)}, u32[]{:S(2)}) %collective-permute-start.1) | collective-permute-done | bytes 3145760 | tf_op jit(solution)/shard_map/while/body/eval_jaxpr/ppermute | solution.py:28
  2485.7 61.7 %collective-permute-done.1 = f32[2,48,64,128]{3,2,1,0:T(8,128)} collective-permute-done((f32[2,48,64,128]{3,2,1,0:T(8,128)}, f32[2,48,64,128]{3,2,1,0:T(8,128)}, u32[]{:S(2)}, u32[]{:S(2)}) %collective-permute-start.1) | collective-permute-done | bytes 3145760 | tf_op jit(solution)/shard_map/while/body/eval_jaxpr/ppermute | solution.py:28
  2554.2 60.8 %collective-permute-done.1 = f32[2,48,64,128]{3,2,1,0:T(8,128)} collective-permute-done((f32[2,48,64,128]{3,2,1,0:T(8,128)}, f32[2,48,64,128]{3,2,1,0:T(8,128)}, u32[]{:S(2)}, u32[]{:S(2)}) %collective-permute-start.1) | collective-permute-done | bytes 3145760 | tf_op jit(solution)/shard_map/while/body/eval_jaxpr/ppermute | solution.py:28
  2621.7 59.8 %collective-permute-done.1 = f32[2,48,64,128]{3,2,1,0:T(8,128)} collective-permute-done((f32[2,48,64,128]{3,2,1,0:T(8,128)}, f32[2,48,64,128]{3,2,1,0:T(8,128)}, u32[]{:S(2)}, u32[]{:S(2)}) %collective-permute-start.1) | collective-permute-done | bytes 3145760 | tf_op jit(solution)/shard_map/while/body/eval_jaxpr/ppermute | solution.py:28
  2688.3 59.8 %collective-permute-done.1 = f32[2,48,64,128]{3,2,1,0:T(8,128)} collective-permute-done((f32[2,48,64,128]{3,2,1,0:T(8,128)}, f32[2,48,64,128]{3,2,1,0:T(8,128)}, u32[]{:S(2)}, u32[]{:S(2)}) %collective-permute-start.1) | collective-permute-done | bytes 3145760 | tf_op jit(solution)/shard_map/while/body/eval_jaxpr/ppermute | solution.py:28
  2833.4 365.8 %fusion = f32[16,6448]{1,0:T(8,128)} fusion(f32[1536,6448]{1,0:T(8,128)} %fusion.62), kind=kCustom, calls=%all-reduce-scatter | all-reduce-scatter fusion | flops 13205505 | bytes 40029184
  3376.7 152.2 %all-reduce.23.cloned.1.call-done = f32[5,3328]{1,0:T(8,128)} async-done(((f32[5,3328]{1,0:T(8,128)}), f32[5,3328]{1,0:T(8,128)}) %all-reduce.23.cloned.1.call-update) | async-done | bytes 66576
  3560.2 75.7 %all-reduce.20 = (f32[4608]{0:T(1024)S(1)}, f32[3,48]{1,0:T(4,128)S(1)}) all-reduce(f32[4608]{0:T(1024)S(1)} %pad_maximum_fusion.4, f32[3,48]{1,0:T(4,128)S(1)} %scatter-add.14), channel_id=5, replica_groups=mesh['seq'=16,'dp'=8] {'seq','dp'}, use_global_device_ids=true, to_apply=%region_27.28.clone | all-reduce | flops 4752 | bytes 38016
  3714.7 139.7 %concatenate.19 = f32[524,6448]{1,0:T(8,128)} concatenate(f32[12,6448]{1,0:T(8,128)} %collective-permute-done.35, f32[16,6448]{1,0:T(8,128)} %copy-done.44, f32[16,6448]{1,0:T(8,128)} %copy-done.43, f32[16,6448]{1,0:T(8,128)} %copy-done.42, f32[16,6448]{1,0:T(8,128)} %copy-done.41, f32[16,6448]{1,0:T(8,128)} %collective-permute-done.30, f32[16,6448]{1,0:T(8,128)} %collective-permute-done.29, ...), dimensions={0} | concatenate | bytes 27030016
  (437 shorter events, 1241.6 us)
Async XLA Ops:
  7.2 109.3 %all-gather.7.cloned.1.call-start = ((), (), s32[]{:S(2)}) async-start(), calls=%async_computation.3 | async-start | bytes 26947584 | tf_op jit(solution)/shard_map/all_gather | solution.py:131
  9.1 1534.6 %reduce-scatter.5.cloned.1.call-start = ((), (), s32[]{:S(2)}) async-start(), calls=%async_computation.2 | async-start | bytes 19021824 | tf_op jit(solution)/shard_map/reduce_scatter | solution.py:195
  197.9 71.3 %collective-permute-start = (f32[2,48,64,128]{3,2,1,0:T(8,128)}, f32[2,48,64,128]{3,2,1,0:T(8,128)S(1)}, u32[]{:S(2)}, u32[]{:S(2)}) collective-permute-start(f32[2,48,64,128]{3,2,1,0:T(8,128)} %multiply_add_fusion.18), channel_id=1, source_target_pairs={{0,8},{8,16},{16,24},{24,32},{32,40},{40,48},{48,56},{56,64},{64,7... | collective-permute-start | bytes 9437192 | tf_op jit(solution)/shard_map/while/body/eval_jaxpr/ppermute | solution.py:28
  273.2 70.4 %collective-permute-start = (f32[2,48,64,128]{3,2,1,0:T(8,128)}, f32[2,48,64,128]{3,2,1,0:T(8,128)S(1)}, u32[]{:S(2)}, u32[]{:S(2)}) collective-permute-start(f32[2,48,64,128]{3,2,1,0:T(8,128)} %multiply_add_fusion.18), channel_id=1, source_target_pairs={{0,8},{8,16},{16,24},{24,32},{32,40},{40,48},{48,56},{56,64},{64,7... | collective-permute-start | bytes 9437192 | tf_op jit(solution)/shard_map/while/body/eval_jaxpr/ppermute | solution.py:28
  347.7 70.1 %collective-permute-start = (f32[2,48,64,128]{3,2,1,0:T(8,128)}, f32[2,48,64,128]{3,2,1,0:T(8,128)S(1)}, u32[]{:S(2)}, u32[]{:S(2)}) collective-permute-start(f32[2,48,64,128]{3,2,1,0:T(8,128)} %multiply_add_fusion.18), channel_id=1, source_target_pairs={{0,8},{8,16},{16,24},{24,32},{32,40},{40,48},{48,56},{56,64},{64,7... | collective-permute-start | bytes 9437192 | tf_op jit(solution)/shard_map/while/body/eval_jaxpr/ppermute | solution.py:28
  421.7 69.7 %collective-permute-start = (f32[2,48,64,128]{3,2,1,0:T(8,128)}, f32[2,48,64,128]{3,2,1,0:T(8,128)S(1)}, u32[]{:S(2)}, u32[]{:S(2)}) collective-permute-start(f32[2,48,64,128]{3,2,1,0:T(8,128)} %multiply_add_fusion.18), channel_id=1, source_target_pairs={{0,8},{8,16},{16,24},{24,32},{32,40},{40,48},{48,56},{56,64},{64,7... | collective-permute-start | bytes 9437192 | tf_op jit(solution)/shard_map/while/body/eval_jaxpr/ppermute | solution.py:28
  495.5 68.8 %collective-permute-start = (f32[2,48,64,128]{3,2,1,0:T(8,128)}, f32[2,48,64,128]{3,2,1,0:T(8,128)S(1)}, u32[]{:S(2)}, u32[]{:S(2)}) collective-permute-start(f32[2,48,64,128]{3,2,1,0:T(8,128)} %multiply_add_fusion.18), channel_id=1, source_target_pairs={{0,8},{8,16},{16,24},{24,32},{32,40},{40,48},{48,56},{56,64},{64,7... | collective-permute-start | bytes 9437192 | tf_op jit(solution)/shard_map/while/body/eval_jaxpr/ppermute | solution.py:28
  568.3 67.9 %collective-permute-start = (f32[2,48,64,128]{3,2,1,0:T(8,128)}, f32[2,48,64,128]{3,2,1,0:T(8,128)S(1)}, u32[]{:S(2)}, u32[]{:S(2)}) collective-permute-start(f32[2,48,64,128]{3,2,1,0:T(8,128)} %multiply_add_fusion.18), channel_id=1, source_target_pairs={{0,8},{8,16},{16,24},{24,32},{32,40},{40,48},{48,56},{56,64},{64,7... | collective-permute-start | bytes 9437192 | tf_op jit(solution)/shard_map/while/body/eval_jaxpr/ppermute | solution.py:28
  640.2 67.0 %collective-permute-start = (f32[2,48,64,128]{3,2,1,0:T(8,128)}, f32[2,48,64,128]{3,2,1,0:T(8,128)S(1)}, u32[]{:S(2)}, u32[]{:S(2)}) collective-permute-start(f32[2,48,64,128]{3,2,1,0:T(8,128)} %multiply_add_fusion.18), channel_id=1, source_target_pairs={{0,8},{8,16},{16,24},{24,32},{32,40},{40,48},{48,56},{56,64},{64,7... | collective-permute-start | bytes 9437192 | tf_op jit(solution)/shard_map/while/body/eval_jaxpr/ppermute | solution.py:28
  1295.9 322.7 %all-gather.5.cloned.1.call-start = ((), (), s32[]{:S(2)}) async-start(), calls=%async_computation.1 | async-start | bytes 9510912 | tf_op jit(solution)/shard_map/all_gather | solution.py:132
  1545.6 1983.3 %all-reduce.23.cloned.1.call-start = ((), (), s32[]{:S(2)}) async-start(), calls=%async_computation.4 | async-start | bytes 212992
  1670.2 73.7 %collective-permute-start.1 = (f32[2,48,64,128]{3,2,1,0:T(8,128)}, f32[2,48,64,128]{3,2,1,0:T(8,128)}, u32[]{:S(2)}, u32[]{:S(2)}) collective-permute-start(f32[2,48,64,128]{3,2,1,0:T(8,128)} %multiply_add_fusion.19), channel_id=1, source_target_pairs={{8,0},{16,8},{24,16},{32,24},{40,32},{48,40},{56,48},{64,56},{72,6... | collective-permute-start | bytes 9437192 | tf_op jit(solution)/shard_map/while/body/eval_jaxpr/ppermute | solution.py:28
  1748.8 72.8 %collective-permute-start.1 = (f32[2,48,64,128]{3,2,1,0:T(8,128)}, f32[2,48,64,128]{3,2,1,0:T(8,128)}, u32[]{:S(2)}, u32[]{:S(2)}) collective-permute-start(f32[2,48,64,128]{3,2,1,0:T(8,128)} %multiply_add_fusion.19), channel_id=1, source_target_pairs={{8,0},{16,8},{24,16},{32,24},{40,32},{48,40},{56,48},{64,56},{72,6... | collective-permute-start | bytes 9437192 | tf_op jit(solution)/shard_map/while/body/eval_jaxpr/ppermute | solution.py:28
  1826.4 71.9 %collective-permute-start.1 = (f32[2,48,64,128]{3,2,1,0:T(8,128)}, f32[2,48,64,128]{3,2,1,0:T(8,128)}, u32[]{:S(2)}, u32[]{:S(2)}) collective-permute-start(f32[2,48,64,128]{3,2,1,0:T(8,128)} %multiply_add_fusion.19), channel_id=1, source_target_pairs={{8,0},{16,8},{24,16},{32,24},{40,32},{48,40},{56,48},{64,56},{72,6... | collective-permute-start | bytes 9437192 | tf_op jit(solution)/shard_map/while/body/eval_jaxpr/ppermute | solution.py:28
  1903.1 71.0 %collective-permute-start.1 = (f32[2,48,64,128]{3,2,1,0:T(8,128)}, f32[2,48,64,128]{3,2,1,0:T(8,128)}, u32[]{:S(2)}, u32[]{:S(2)}) collective-permute-start(f32[2,48,64,128]{3,2,1,0:T(8,128)} %multiply_add_fusion.19), channel_id=1, source_target_pairs={{8,0},{16,8},{24,16},{32,24},{40,32},{48,40},{56,48},{64,56},{72,6... | collective-permute-start | bytes 9437192 | tf_op jit(solution)/shard_map/while/body/eval_jaxpr/ppermute | solution.py:28
  1979.0 70.1 %collective-permute-start.1 = (f32[2,48,64,128]{3,2,1,0:T(8,128)}, f32[2,48,64,128]{3,2,1,0:T(8,128)}, u32[]{:S(2)}, u32[]{:S(2)}) collective-permute-start(f32[2,48,64,128]{3,2,1,0:T(8,128)} %multiply_add_fusion.19), channel_id=1, source_target_pairs={{8,0},{16,8},{24,16},{32,24},{40,32},{48,40},{56,48},{64,56},{72,6... | collective-permute-start | bytes 9437192 | tf_op jit(solution)/shard_map/while/body/eval_jaxpr/ppermute | solution.py:28
  2053.8 69.1 %collective-permute-start.1 = (f32[2,48,64,128]{3,2,1,0:T(8,128)}, f32[2,48,64,128]{3,2,1,0:T(8,128)}, u32[]{:S(2)}, u32[]{:S(2)}) collective-permute-start(f32[2,48,64,128]{3,2,1,0:T(8,128)} %multiply_add_fusion.19), channel_id=1, source_target_pairs={{8,0},{16,8},{24,16},{32,24},{40,32},{48,40},{56,48},{64,56},{72,6... | collective-permute-start | bytes 9437192 | tf_op jit(solution)/shard_map/while/body/eval_jaxpr/ppermute | solution.py:28
  2127.8 68.2 %collective-permute-start.1 = (f32[2,48,64,128]{3,2,1,0:T(8,128)}, f32[2,48,64,128]{3,2,1,0:T(8,128)}, u32[]{:S(2)}, u32[]{:S(2)}) collective-permute-start(f32[2,48,64,128]{3,2,1,0:T(8,128)} %multiply_add_fusion.19), channel_id=1, source_target_pairs={{8,0},{16,8},{24,16},{32,24},{40,32},{48,40},{56,48},{64,56},{72,6... | collective-permute-start | bytes 9437192 | tf_op jit(solution)/shard_map/while/body/eval_jaxpr/ppermute | solution.py:28
  2200.9 67.3 %collective-permute-start.1 = (f32[2,48,64,128]{3,2,1,0:T(8,128)}, f32[2,48,64,128]{3,2,1,0:T(8,128)}, u32[]{:S(2)}, u32[]{:S(2)}) collective-permute-start(f32[2,48,64,128]{3,2,1,0:T(8,128)} %multiply_add_fusion.19), channel_id=1, source_target_pairs={{8,0},{16,8},{24,16},{32,24},{40,32},{48,40},{56,48},{64,56},{72,6... | collective-permute-start | bytes 9437192 | tf_op jit(solution)/shard_map/while/body/eval_jaxpr/ppermute | solution.py:28
  3201.0 72.3 %collective-permute-start.10 = (f32[16,6448]{1,0:T(8,128)}, f32[16,6448]{1,0:T(8,128)}, u32[]{:S(2)}, u32[]{:S(2)}) collective-permute-start(f32[16,6448]{1,0:T(8,128)} %fusion), channel_id=1, source_target_pairs={{0,7},{1,8},{2,9},{3,10},{4,11},{5,12},{6,13},{7,14},{8,15},{9,16}... | collective-permute-start | bytes 1238024
  3276.0 73.9 %collective-permute-start.16 = (f32[16,6448]{1,0:T(8,128)}, f32[16,6448]{1,0:T(8,128)S(1)}, u32[]{:S(2)}, u32[]{:S(2)}) collective-permute-start(f32[16,6448]{1,0:T(8,128)} %fusion), channel_id=1, source_target_pairs={{0,13},{1,14},{2,15},{3,16},{4,17},{5,18},{6,19},{7,20},{8,21},{9,... | collective-permute-start | bytes 1238024
  3297.3 75.6 %collective-permute-start.20 = (f32[16,6448]{1,0:T(8,128)}, f32[16,6448]{1,0:T(8,128)}, u32[]{:S(2)}, u32[]{:S(2)}) collective-permute-start(f32[16,6448]{1,0:T(8,128)} %fusion), channel_id=1, source_target_pairs={{0,17},{1,18},{2,19},{3,20},{4,21},{5,22},{6,23},{7,24},{8,25},{9,... | collective-permute-start | bytes 1238024
  3350.0 180.3 %collective-permute-start.21 = (f32[16,6448]{1,0:T(8,128)}, f32[16,6448]{1,0:T(8,128)}, u32[]{:S(2)}, u32[]{:S(2)}) collective-permute-start(f32[16,6448]{1,0:T(8,128)} %fusion), channel_id=1, source_target_pairs={{0,18},{1,19},{2,20},{3,21},{4,22},{5,23},{6,24},{7,25},{8,26},{9,... | collective-permute-start | bytes 1238024
  3353.2 179.6 %collective-permute-start.22 = (f32[16,6448]{1,0:T(8,128)}, f32[16,6448]{1,0:T(8,128)}, u32[]{:S(2)}, u32[]{:S(2)}) collective-permute-start(f32[16,6448]{1,0:T(8,128)} %fusion), channel_id=1, source_target_pairs={{0,19},{1,20},{2,21},{3,22},{4,23},{5,24},{6,25},{7,26},{8,27},{9,... | collective-permute-start | bytes 1238024
  3357.6 178.3 %collective-permute-start.23 = (f32[16,6448]{1,0:T(8,128)}, f32[16,6448]{1,0:T(8,128)}, u32[]{:S(2)}, u32[]{:S(2)}) collective-permute-start(f32[16,6448]{1,0:T(8,128)} %fusion), channel_id=1, source_target_pairs={{0,20},{1,21},{2,22},{3,23},{4,24},{5,25},{6,26},{7,27},{8,28},{9,... | collective-permute-start | bytes 1238024
  3359.5 182.2 %collective-permute-start.24 = (f32[16,6448]{1,0:T(8,128)}, f32[16,6448]{1,0:T(8,128)}, u32[]{:S(2)}, u32[]{:S(2)}) collective-permute-start(f32[16,6448]{1,0:T(8,128)} %fusion), channel_id=1, source_target_pairs={{0,21},{1,22},{2,23},{3,24},{4,25},{5,26},{6,27},{7,28},{8,29},{9,... | collective-permute-start | bytes 1238024
  3372.9 172.1 %collective-permute-start.25 = (f32[16,6448]{1,0:T(8,128)}, f32[16,6448]{1,0:T(8,128)}, u32[]{:S(2)}, u32[]{:S(2)}) collective-permute-start(f32[16,6448]{1,0:T(8,128)} %fusion), channel_id=1, source_target_pairs={{0,22},{1,23},{2,24},{3,25},{4,26},{5,27},{6,28},{7,29},{8,30},{9,... | collective-permute-start | bytes 1238024
  3530.3 105.6 %collective-permute-start.26 = (f32[16,6448]{1,0:T(8,128)}, f32[16,6448]{1,0:T(8,128)}, u32[]{:S(2)}, u32[]{:S(2)}) collective-permute-start(f32[16,6448]{1,0:T(8,128)} %fusion), channel_id=1, source_target_pairs={{0,23},{1,24},{2,25},{3,26},{4,27},{5,28},{6,29},{7,30},{8,31},{9,... | collective-permute-start | bytes 1238024
  3532.8 106.6 %collective-permute-start.27 = (f32[16,6448]{1,0:T(8,128)}, f32[16,6448]{1,0:T(8,128)}, u32[]{:S(2)}, u32[]{:S(2)}) collective-permute-start(f32[16,6448]{1,0:T(8,128)} %fusion), channel_id=1, source_target_pairs={{0,24},{1,25},{2,26},{3,27},{4,28},{5,29},{6,30},{7,31},{8,32},{9,... | collective-permute-start | bytes 1238024
  3536.0 108.3 %collective-permute-start.28 = (f32[16,6448]{1,0:T(8,128)}, f32[16,6448]{1,0:T(8,128)}, u32[]{:S(2)}, u32[]{:S(2)}) collective-permute-start(f32[16,6448]{1,0:T(8,128)} %fusion), channel_id=1, source_target_pairs={{0,25},{1,26},{2,27},{3,28},{4,29},{5,30},{6,31},{7,32},{8,33},{9,... | collective-permute-start | bytes 1238024
  3541.7 106.1 %collective-permute-start.29 = (f32[16,6448]{1,0:T(8,128)}, f32[16,6448]{1,0:T(8,128)}, u32[]{:S(2)}, u32[]{:S(2)}) collective-permute-start(f32[16,6448]{1,0:T(8,128)} %fusion), channel_id=1, source_target_pairs={{0,26},{1,27},{2,28},{3,29},{4,30},{5,31},{6,32},{7,33},{8,34},{9,... | collective-permute-start | bytes 1238024
  3545.1 104.1 %collective-permute-start.30 = (f32[16,6448]{1,0:T(8,128)}, f32[16,6448]{1,0:T(8,128)}, u32[]{:S(2)}, u32[]{:S(2)}) collective-permute-start(f32[16,6448]{1,0:T(8,128)} %fusion), channel_id=1, source_target_pairs={{0,27},{1,28},{2,29},{3,30},{4,31},{5,32},{6,33},{7,34},{8,35},{9,... | collective-permute-start | bytes 1238024
  (130 other events, 9240.8 us)
Sparse Core Ops, SparseCore 0:
  11.6 99.4 all-gather.6
  1296.0 247.6 reduce-scatter.4
  1547.7 70.7 all-gather.4
  3276.0 252.7 all-reduce.22
where the time goes:
time: 3910 us; the launch traced here: 3860 us
  waiting for transfers between devices  2370 us (61%)
  blocking collectives  542 us (14%)
  starting transfers between devices  369 us (9%)
  local copies, waits for them, and re-layouts  234 us (6%)
  other arithmetic  190 us (5%)
  matrix products  144 us (4%)
    ppermute x32, waiting for transfers between devices, from_behind(): lax.ppermute(value, axis, [(source, source + steps) for source in range(l...  1890 us
    unnamed x3, blocking collectives  508 us
    unnamed x33, starting transfers between devices  248 us
    reduce_scatter x1, waiting for transfers between devices, on_device(): lax.psum_scatter(out_grad, ('seq', 'dp'), scatter_dimension=0, tiled=True)  248 us
    unnamed x193, local copies, waits for them, and re-layouts  183 us
    unnamed x37, waiting for transfers between devices  161 us
    ppermute x32, starting transfers between devices, from_behind(): lax.ppermute(value, axis, [(source, source + steps) for source in range(l...  122 us
  transfers between devices with their start and end apart: 68, of which 36 were waited for; matrix products, arithmetic and copies ran while one was open for 1% of the time, Pallas kernels for 0%

commit v1 on v0

v1 whole, which is shorter than its diff:
```python
import jax
import jax.numpy as jnp
from jax import lax
from jax.sharding import Mesh
from jax.sharding import PartitionSpec as P

WIDTH = 1536
INNER = 3072
STATE = 128
HEADDIM = 64
KERNEL = 4
STEP = 5
HEADS = 48
CONV = 3328
PROJ = 6448

HALF = INNER // 2
HALF_HEADS = HEADS // 2
TOKENS = 512
OWN = TOKENS // 2
HALO = 16
ROWS_IN = TOKENS + HALO
CHUNK = 128
CHUNKS = TOKENS // CHUNK
LANES = 128
ACT = HALF + 2 * STATE
CRIT = ACT + LANES
PART = 1024
ROWS = 24

NORM_EPS = 1e-05
PRECISE = lax.Precision.HIGH
EXACT = lax.Precision.HIGHEST
BETA_ONE = 0.9
BETA_TWO = 0.95
ADAM_EPS = 1e-08
MATRIX_RATE = 0.05
SMALL_RATE = 0.5
MATRIX_DECAY = 0.1
BF16 = jnp.bfloat16
F32 = jnp.float32
CHIPS = ("y", "x", "z")
ALL = ("y", "x", "z", "c")


def mm(a, b, dims=((1,), (0,))):
    return lax.dot_general(
        a.astype(BF16), b.astype(BF16), (dims, ((), ())), preferred_element_type=F32
    )


def exact(a, b, dims=((1,), (0,))):
    return lax.dot_general(a, b, (dims, ((), ())), precision=PRECISE, preferred_element_type=F32)


NT = ((1,), (1,))
TN = ((0,), (0,))


def rounded(v):
    return lax.reduce_precision(v, 8, 7)


def iota(shape, dim):
    return lax.broadcasted_iota(jnp.int32, shape, dim)


def sigmoid(v):
    return 1.0 / (1.0 + jnp.exp(-v))


def spread_matrix():
    return (iota((LANES, HALF), 1) // HEADDIM == iota((LANES, HALF), 0)).astype(F32)


def adamw_step(weight, gradient, moment_one, moment_two, step_rate, weight_decay):
    one_next = BETA_ONE * moment_one + (1.0 - BETA_ONE) * gradient
    two_next = BETA_TWO * moment_two + (1.0 - BETA_TWO) * gradient * gradient
    corrected = one_next / (1.0 - BETA_ONE**STEP)
    scale_next = jnp.sqrt(two_next / (1.0 - BETA_TWO**STEP)) + ADAM_EPS
    weight_next = weight - step_rate * (corrected / scale_next + weight_decay * weight)
    return (one_next, two_next, weight_next)


def swap_cores(value):
    return lax.ppermute(value, "c", [(0, 1), (1, 0)])


def regroup(value, turn):
    pairs = [
        (x * 2 + c, (2 * c + (x + turn) % 2) * 2 + x // 2) for x in range(4) for c in range(2)
    ]
    return lax.ppermute(value, ("x", "c"), pairs)


def cross_halves(value):
    pairs = []
    for y in range(4):
        for c in range(2):
            to = (y, c) if y // 2 == c else (y ^ 2, 1 - c)
            pairs.append((y * 2 + c, to[0] * 2 + to[1]))
    return lax.ppermute(value, ("y", "c"), pairs)


def along_y(value, steps):
    return lax.ppermute(value, "y", [(y, y + steps) for y in range(4) if 0 <= y + steps < 4])


def partner(axis, turn):
    pairs = []
    for i in range(4):
        for c in range(2):
            pairs.append((i * 2 + c, (i ^ (1 if (turn + c) % 2 == 0 else 3)) * 2 + c))
    return (axis, "c"), pairs


def exchange(value, axis, turn):
    axes, pairs = partner(axis, turn)
    return lax.ppermute(value, axes, pairs)


def block_order(order):
    first = jnp.where(lax.axis_index("c") == 0, 1, 3)
    second = 4 - first
    block = jnp.arange(64)
    place = {a: lax.axis_index(a) for a in CHIPS}
    for at, axis in enumerate(order):
        high = (block >> (5 - 2 * at)) & 1
        low = (block >> (4 - 2 * at)) & 1
        place[axis] = place[axis] ^ (high * first) ^ (low * second)
    return [place[a] + jnp.zeros((64,), jnp.int32) for a in CHIPS]


def rows_of(blocks):
    return (blocks[:, None] * ROWS + jnp.arange(ROWS)[None, :]).reshape(-1)


def in_rows(order):
    y, x, z = block_order(order)
    return rows_of((y * 4 + x) * 4 + z)


def out_rows(order):
    y, x, z = block_order(order)
    return rows_of((((y % 2) * 4 + x) * 4 + z) * 2 + y // 2)


def pick(rows):
    return (rows[:, None] == iota((1536, 1536), 1)).astype(BF16)


def reduce_scatter(sends, keeps, orders):
    for step in range(6):
        arrived = []
        for send, order in zip(sends, orders):
            arrived.append(exchange(send.astype(BF16), order[step // 2], step % 2))
        totals = [keep.astype(F32) + got.astype(F32) for keep, got in zip(keeps, arrived)]
        half = totals[0].shape[0] // 2
        if step < 5:
            sends = [t[half:] for t in totals]
            keeps = [t[:half] for t in totals]
    return totals


PAIRS = HALF_HEADS // 2


def product(terms, a, b):
    return jnp.einsum(terms, a, b, preferred_element_type=F32)


def by_pair(value):
    return value.reshape(CHUNKS, CHUNK, PAIRS, LANES).transpose(0, 2, 1, 3)


def from_pairs(value):
    return value.transpose(0, 2, 1, 3).reshape(TOKENS, HALF)


def one_head(value):
    left = iota((2, 1, LANES), 2) // HEADDIM == iota((2, 1, LANES), 0)
    return jnp.where(left, value[:, :, None], jnp.zeros((), value.dtype))


def decays(cl):
    heads = cl[:, :HALF_HEADS].reshape(CHUNKS, CHUNK, PAIRS, 2).transpose(0, 2, 3, 1)
    causal = iota((CHUNK, CHUNK), 0) >= iota((CHUNK, CHUNK), 1)
    differ = jnp.where(causal, heads[..., :, None] - heads[..., None, :], 0.0)
    return jnp.where(causal, jnp.exp(differ), 0.0)


def pack_state(state, decay):
    high = rounded(decay)
    middle = rounded(decay - high)
    low = rounded(decay - high - middle)
    at = iota((16, LANES), 0)
    rows = jnp.where(at == 0, high, jnp.where(at == 1, middle, 0.0))
    rows = jnp.where(at == 2, low, rows)
    return jnp.concatenate([state, rows], axis=0).astype(BF16)


def unpack_state(packed):
    rows = packed[HALF : HALF + 3].astype(F32)
    return packed[:HALF].astype(F32), rows[0] + rows[1] + rows[2]


def per_row(head_values):
    heads = head_values[..., :HALF_HEADS, None]
    wide = jnp.broadcast_to(heads, heads.shape[:-1] + (HEADDIM,))
    return wide.reshape(head_values.shape[:-1] + (HALF, 1))


def combine(packed, way, unpack):
    near, far, farthest = [unpack(along_y(packed, way * k)) for k in (1, 2, 3)]
    return near[0] + per_row(near[1]) * (far[0] + per_row(far[1]) * farthest[0])


def pack_full(state, decay):
    return jnp.concatenate([state, jnp.broadcast_to(decay[None], (8, LANES))], axis=0)


def unpack_full(packed):
    return packed[:HALF], packed[HALF]


def chunked(value):
    return value.reshape(CHUNKS, CHUNK, value.shape[-1])


def flat(value):
    return value.reshape(TOKENS, value.shape[-1])


def sum_all_chips(value):
    for axis in CHIPS:
        for turn in range(2):
            value = value + exchange(value, axis, turn)
    return value


def on_device(
    block_in,
    cotangent,
    in_master,
    in_moment1,
    in_moment2,
    out_master,
    out_moment1,
    out_moment2,
    conv_master,
    conv_moment1,
    conv_moment2,
    gain_master,
    gain_moment1,
    gain_moment2,
    head_master,
    head_moment1,
    head_moment2,
):
    core = lax.axis_index("c")
    x_at = lax.axis_index("x")
    first_core = core == 0
    even_x = x_at % 2 == 0

    def ordered(flag, mine, other, axis=0):
        return jnp.where(
            flag, jnp.concatenate([mine, other], axis=axis), jnp.concatenate([other, mine], axis=axis)
        )

    def half_columns(c):
        return jnp.concatenate(
            [
                in_master[:, INNER + c * HALF : INNER + (c + 1) * HALF],
                in_master[:, 2 * INNER : INNER + CONV],
                in_master[:, INNER + CONV + c * HALF_HEADS : INNER + CONV + (c + 1) * HALF_HEADS],
                jnp.zeros((12, LANES - HALF_HEADS), F32),
                in_master[:, c * HALF : (c + 1) * HALF],
            ],
            axis=1,
        )

    halves = [half_columns(0), half_columns(1)]
    mine = jnp.where(first_core, halves[0], halves[1])
    theirs = jnp.where(first_core, halves[1], halves[0])
    in_rows_low = ordered(first_core, mine, swap_cores(theirs)).astype(BF16)
    out_rows_low = cross_halves(out_master).astype(BF16)
    small = jnp.zeros((8, LANES), F32)
    small = small.at[:5, :26].set(rounded(conv_master))
    small = small.at[5, :36].set(rounded(gain_master))
    small_all = lax.all_gather(small, ALL, axis=0, tiled=False)
    gathered = lax.all_gather(
        jnp.concatenate([in_rows_low, out_rows_low], axis=1), CHIPS, axis=0, tiled=True
    )
    w_crit = gathered[:, :CRIT]
    w_gate = gathered[:, CRIT : CRIT + HALF]
    w_out = (
        gathered[:, CRIT + HALF :]
        .reshape(2, 2, 16, ROWS, WIDTH)
        .transpose(1, 2, 0, 3, 4)
        .reshape(HALF, WIDTH)
    )
    conv_all = small_all[:, :5, :26].transpose(1, 0, 2).reshape(5, CONV)
    gain_all = small_all[:, 5, :36].reshape(-1)
    norm_gain = gain_all[:WIDTH]
    gate_gain = lax.dynamic_slice(gain_all, (WIDTH + core * HALF,), (HALF,))
    conv_weights = jnp.concatenate(
        [lax.dynamic_slice(conv_all, (0, core * HALF), (5, HALF)), conv_all[:, INNER:]], axis=1
    )
    head_half = jnp.pad(
        lax.dynamic_slice(head_master, (0, core * HALF_HEADS), (3, HALF_HEADS)),
        ((0, 0), (0, LANES - HALF_HEADS)),
    )
    decay_rate = -jnp.exp(head_half[0])

    both = jnp.stack([block_in, cotangent], axis=1)
    flipped = both[::-1]
    got = [regroup(jnp.where(even_x, both, flipped)[k], k) for k in range(2)]
    own_both = ordered(even_x, got[0], got[1], axis=1)
    all_both = ordered(first_core, own_both, swap_cores(own_both), axis=1)
    own_in, own_cot = own_both[0], own_both[1]
    tokens, cot = all_both[0], all_both[1]
    halo = along_y(tokens[TOKENS - HALO :], 1)
    extended = jnp.concatenate([tokens, halo], axis=0).astype(F32)
    inv = lax.rsqrt(jnp.mean(extended * extended, axis=1, keepdims=True) + NORM_EPS)
    normed = (extended * inv * norm_gain).astype(BF16)

    crit = mm(normed, w_crit)
    ext = jnp.concatenate([crit[TOKENS + 8 :, :ACT], crit[:TOKENS, :ACT]], axis=0)
    preact = conv_weights[KERNEL] + sum(
        conv_weights[k] * ext[5 + k : 5 + k + TOKENS] for k in range(KERNEL)
    )
    gate_of_act = sigmoid(preact)
    act = preact * gate_of_act
    head_x = act[:, :HALF]
    bc = act[:, HALF:]
    dt_in = crit[:TOKENS, ACT:] + head_half[1]
    real = iota((1, LANES), 1) < HALF_HEADS
    dt = jnp.where(real, jax.nn.softplus(dt_in), 0.0)
    log_decay = dt * decay_rate
    below = (iota((CHUNK, CHUNK), 0) >= iota((CHUNK, CHUNK), 1)).astype(F32)
    below = jnp.broadcast_to(below[None], (CHUNKS, CHUNK, CHUNK))
    cl = jnp.einsum("kts,ksh->kth", below, chunked(log_decay), precision=EXACT)
    spread = spread_matrix()
    u = head_x * exact(dt, spread)
    u_low = rounded(u)
    lasts = cl[:, -1]
    to_end = flat(jnp.exp(lasts[:, None] - cl))
    cl = flat(cl)
    to_end_wide = exact(to_end, spread)
    from_start_wide = exact(jnp.exp(cl), spread)
    u_wide = u * to_end_wide
    b_proj, c_proj = chunked(bc[:, :STATE]), chunked(bc[:, STATE:])
    b_low, c_low = b_proj.astype(BF16), c_proj.astype(BF16)
    own = jnp.einsum("ktr,ktn->krn", chunked(u_wide), b_proj, precision=PRECISE)
    def between(i, j):
        return per_row(jnp.exp(sum(lasts[i:j])) if j > i else jnp.ones((LANES,), F32))

    local = [jnp.zeros_like(own[0])]
    for k in range(CHUNKS):
        local.append(sum(between(i + 1, k + 1) * own[i] for i in range(k + 1)))
    piece_decay = jnp.exp(jnp.sum(lasts, axis=0))
    incoming = combine(pack_full(local[CHUNKS], piece_decay), 1, unpack_full)
    decay = decays(cl)
    scores = jnp.einsum("ktn,ksn->kts", c_proj, b_proj, precision=PRECISE)
    mixes = (scores[:, None, None] * decay).astype(BF16)
    u_pairs = one_head(by_pair(u_low.astype(BF16)))
    y_chunk = from_pairs(product("kpjts,kpjsc->kptc", mixes, u_pairs))

    starts = jnp.stack([between(0, k) * incoming + local[k] for k in range(CHUNKS)])
    state_end = between(0, CHUNKS) * incoming + local[CHUNKS]
    y_state = flat(jnp.einsum("ktn,krn->ktr", c_proj, starts, precision=PRECISE)) * from_start_wide
    y_ssd = y_chunk + y_state
    skip_wide = exact(head_half[2:3], spread)
    mixed = y_ssd + skip_wide * head_x

    gate = mm(normed[:TOKENS], w_gate)
    gate_sig = sigmoid(gate)
    gate_silu = gate * gate_sig
    d_gated = mm(cot, w_out, NT)
    g = mixed * gate_silu
    e = d_gated * gate_gain
    sums = jnp.concatenate(
        [jnp.sum(g * g, axis=1, keepdims=True), jnp.sum(e * g, axis=1, keepdims=True)], axis=1
    )
    sums = (sums + swap_cores(sums)) / INNER
    r = lax.rsqrt(sums[:, :1] + NORM_EPS)
    gated_low = (g * r * gate_gain).astype(BF16)
    d_g = r * e - (r * r * r) * g * sums[:, 1:]
    d_gate_gain = jnp.sum(d_gated * g * r, axis=0)
    dy = d_g * gate_silu
    d_gate = (d_g * mixed * (gate_sig * (1.0 + gate * (1.0 - gate_sig)))).astype(BF16)
    dy_low = rounded(dy)

    dy_start = chunked(dy * from_start_wide)
    chunk_backs = jnp.einsum("ktr,ktn->krn", dy_start, c_proj, precision=PRECISE)
    back = [None] * CHUNKS
    for k in range(CHUNKS):
        back[k] = sum((between(k + 1, i) * chunk_backs[i] for i in range(k + 1, CHUNKS)), jnp.zeros_like(own[0]))
    to_before = sum(between(0, i) * chunk_backs[i] for i in range(CHUNKS))
    leaving = combine(pack_state(to_before, piece_decay), -1, unpack_state)
    dy_pairs = by_pair(dy_low.astype(BF16))
    du_chunk = from_pairs(product("kpjts,kpjtc->kpsc", mixes, one_head(dy_pairs)))
    both = product("kptc,kpjsc->kpjts", dy_pairs, u_pairs)
    d_scores = jnp.sum(decay * both, axis=(1, 2)).astype(BF16)
    db_chunk = product("kts,ktn->ksn", d_scores, c_low)
    dc_chunk = product("kts,ksn->ktn", d_scores, b_low)

    part_out = mm(gated_low, w_out)

    def own_rows(value):
        return jnp.where(first_core, value[:OWN], value[OWN:]), jnp.where(
            first_core, value[OWN:], value[:OWN]
        )

    def to_owner(value):
        low, high = value[:CHUNK], value[CHUNK:]
        sent = [jnp.where(even_x, low, high), jnp.where(even_x, high, low)]
        back0, back1 = regroup(sent[0], 0), regroup(sent[1], 1)
        return jnp.where(even_x, jnp.stack([back0, back1]), jnp.stack([back1, back0]))

    kept, other = own_rows(part_out)
    own_out = own_in.astype(F32) + (kept + swap_cores(other))
    block_out = to_owner(own_out.astype(BF16))

    order_a, order_b = ("y", "x", "z"), ("x", "y", "z")
    pick_in_a, pick_in_b = pick(in_rows(order_a)), pick(in_rows(order_b))
    pick_out_b = pick(out_rows(order_b))
    normed_a = mm(pick_in_a, normed, NT).astype(BF16)
    normed_b = mm(pick_in_b, normed, NT).astype(BF16)
    gated_b = mm(pick_out_b, gated_low, NT).astype(BF16)
    middle = WIDTH // 2
    gate_rows, out_rows_grad = reduce_scatter(
        [mm(normed_a[middle:, :TOKENS], d_gate), mm(gated_b[middle:], cot)],
        [mm(normed_a[:middle, :TOKENS], d_gate), mm(gated_b[:middle], cot)],
        [order_a, order_b],
    )

    ends = jnp.stack([between(k + 1, CHUNKS) * leaving + back[k] for k in range(CHUNKS)])
    du = du_chunk + flat(jnp.einsum("ktn,krn->ktr", b_proj, ends, precision=PRECISE)) * to_end_wide
    d_b = flat(db_chunk + jnp.einsum("ktr,krn->ktn", chunked(u_wide), ends, precision=PRECISE))
    d_c = flat(dc_chunk + jnp.einsum("ktr,krn->ktn", dy_start, starts, precision=PRECISE))
    d_bc = jnp.concatenate([d_b, d_c], axis=1)
    nexts = jnp.concatenate([starts[1:], state_end[None]], axis=0)
    carries = exact(jnp.sum(ends * nexts, axis=2), spread, NT)
    d_cl = chunked(exact(dy_low * y_ssd - u_low * du, spread, NT))
    d_log_decay = flat(jnp.einsum("kts,kth->ksh", below, d_cl, precision=PRECISE) + carries[:, None])
    d_dt = exact(head_x * du, spread, NT) + d_log_decay * decay_rate
    d_dt_raw = jnp.where(real, d_dt * sigmoid(dt_in), 0.0)
    d_head = jnp.stack(
        [
            jnp.sum(d_log_decay * log_decay, axis=0),
            jnp.sum(d_dt_raw, axis=0),
            exact(jnp.sum(dy * head_x, axis=0, keepdims=True), spread, NT)[0],
        ]
    )
    d_x = exact(dt, spread) * du + skip_wide * dy
    d_act = jnp.concatenate([d_x, d_bc], axis=1)
    d_pre = d_act * (gate_of_act * (1.0 + preact * (1.0 - gate_of_act)))
    d_ext = sum(
        conv_weights[k] * jnp.pad(d_pre, ((5 + k, 3 - k), (0, 0))) for k in range(KERNEL)
    )
    d_conv = jnp.where(iota((8, ACT), 0) == KERNEL, jnp.sum(d_pre, axis=0)[None], 0.0)
    for k in range(KERNEL):
        tap = jnp.sum(d_pre * ext[5 + k : 5 + k + TOKENS], axis=0)
        d_conv = jnp.where(iota((8, ACT), 0) == k, tap[None], d_conv)
    d_ext = jnp.concatenate([d_ext[8:], jnp.zeros((8, ACT), F32), d_ext[:8]], axis=0)
    d_crit = jnp.concatenate(
        [d_ext, jnp.pad(d_dt_raw, ((0, HALO), (0, 0)))], axis=1
    ).astype(BF16)

    y_of, x_of, z_of = block_order(order_b)
    row_at = rows_of((y_of * 4 + x_of) * 4 + z_of)[:, None]
    device_of, slot_of = row_at // 12, row_at % 12
    conv_x = d_conv[:, :HALF]
    conv_full = jnp.concatenate(
        [ordered(first_core, conv_x, jnp.zeros_like(conv_x), axis=1), d_conv[:, HALF:]], axis=1
    )
    slot_pick = (slot_of == iota((1536, 8), 1)).astype(F32)
    conv_cols = iota((1536, CONV), 1)
    conv_spread = jnp.where(conv_cols // 26 == device_of, exact(slot_pick, conv_full), 0.0)
    fold = (iota((CONV, LANES), 0) % 26 + HALF_HEADS == iota((CONV, LANES), 1)).astype(BF16)
    gain_at = WIDTH + core * HALF + iota((1536, HALF), 1)
    gain_spread = jnp.where((gain_at // 36 == device_of) & (slot_of == 5), d_gate_gain[None, :], 0.0)
    gain_fold = (
        (WIDTH + core * HALF + iota((HALF, LANES), 0)) % 36 + HALF_HEADS == iota((HALF, LANES), 1)
    ).astype(BF16)
    riders = mm(conv_spread, fold) + mm(gain_spread, gain_fold)

    crit_b = jnp.concatenate([d_crit[:, PART:]], axis=1)

    def part_b(rows):
        with_riders = jnp.pad(riders[rows], ((0, 0), (CRIT - PART - LANES, 0)))
        return mm(normed_b[rows], crit_b) + with_riders

    rows_a, rows_b = reduce_scatter(
        [mm(normed_a[middle:], d_crit[:, :PART]), part_b(slice(middle, None))],
        [mm(normed_a[:middle], d_crit[:, :PART]), part_b(slice(0, middle))],
        [order_a, order_b],
    )
    head_own = sum_all_chips(jnp.pad(d_head, ((0, 5), (0, 0))))
    head_other = swap_cores(head_own)

    d_normed = mm(d_crit, w_crit, NT)
    d_halo = along_y(d_normed[TOKENS:], -1)
    d_normed = d_normed[:TOKENS] + mm(d_gate, w_gate, NT)
    d_normed = jnp.concatenate(
        [d_normed[: TOKENS - HALO], d_normed[TOKENS - HALO :] + d_halo], axis=0
    )
    kept, other = own_rows(d_normed)
    d_own = kept + swap_cores(other)
    own = own_in.astype(F32)
    own_inv = lax.rsqrt(jnp.mean(own * own, axis=1, keepdims=True) + NORM_EPS)
    d_own = d_own * norm_gain
    d_tokens = own_inv * d_own - (own_inv * own_inv * own_inv) * own * jnp.mean(
        own * d_own, axis=1, keepdims=True
    )
    input_grad = to_owner(own_cot.astype(F32) + d_tokens)

    rows = jnp.concatenate([rows_a, rows_b, gate_rows], axis=1)
    mine = jnp.where(first_core, rows[:12], rows[12:])
    theirs = jnp.where(first_core, rows[12:], rows[:12])
    theirs = swap_cores(theirs)
    h0 = jnp.where(first_core, mine, theirs)
    h1 = jnp.where(first_core, theirs, mine)
    in_share = jnp.concatenate(
        [
            h0[:, CRIT:],
            h1[:, CRIT:],
            h0[:, :HALF],
            h1[:, :HALF],
            h0[:, HALF:ACT] + h1[:, HALF:ACT],
            h0[:, ACT : ACT + HALF_HEADS],
            h1[:, ACT : ACT + HALF_HEADS],
        ],
        axis=1,
    )
    riding = h0[:, ACT + HALF_HEADS : CRIT] + h1[:, ACT + HALF_HEADS : CRIT]
    conv_share = riding[:5, :26]
    out_share = cross_halves(out_rows_grad)
    at_device = ((lax.axis_index("y") * 4 + x_at) * 4 + lax.axis_index("z")) * 2 + core
    w_own = rounded(in_master)
    own_gain = lax.dynamic_slice(norm_gain, (at_device * 12,), (12,))
    gain_rows = jnp.sum(w_own * in_share, axis=1) / own_gain
    thirds = [
        lax.ppermute(gain_rows, ALL, [(3 * d + k, d) for d in range(128) if 3 * d + k < 128])
        for k in range(3)
    ]
    gain_share = jnp.concatenate(thirds) + riding[5, :36]
    head_share = ordered(
        first_core, head_own[:3, :HALF_HEADS], head_other[:3, :HALF_HEADS], axis=1
    )

    in_next = adamw_step(in_master, in_share, in_moment1, in_moment2, MATRIX_RATE, MATRIX_DECAY)
    out_next = adamw_step(
        out_master, out_share, out_moment1, out_moment2, MATRIX_RATE, MATRIX_DECAY
    )
    conv_next = adamw_step(conv_master, conv_share, conv_moment1, conv_moment2, SMALL_RATE, 0.0)
    gain_next = adamw_step(gain_master, gain_share, gain_moment1, gain_moment2, SMALL_RATE, 0.0)
    head_next = adamw_step(head_master, head_share, head_moment1, head_moment2, SMALL_RATE, 0.0)
    return (
        block_out,
        input_grad,
        *in_next,
        *out_next,
        *conv_next,
        *gain_next,
        *head_next,
    )


def solution(mesh):
    fine = Mesh(mesh.devices.reshape(4, 4, 4, 2), ALL)
    tokens = P(("z", "c"), ("y", "x"), None)
    rows = P(ALL, None)
    columns = P(None, ALL)
    flat = P(ALL)
    return jax.shard_map(
        on_device,
        mesh=fine,
        in_specs=(tokens, tokens) + (rows,) * 6 + (columns,) * 3 + (flat,) * 3 + (P(),) * 3,
        out_specs=(tokens, tokens) + (rows,) * 6 + (columns,) * 3 + (flat,) * 3 + (P(),) * 3,
        check_vma=False,
    )
```

time: 3910 us -> 580 us (0.15)
  waiting for transfers between devices: 2370 us -> 118 us
  blocking collectives: 542 us -> 54.4 us
  starting transfers between devices: 369 us -> 82.8 us
  local copies, waits for them, and re-layouts: 234 us -> 85.8 us
  other arithmetic: 190 us -> 79.9 us
    ppermute x32 -> x56, waiting for transfers between devices: 1890 us -> 100 us  [the longest x30 79.4 us: exchange(): return lax.ppermute(value, axes, pairs)]
    unnamed x3 -> x0, blocking collectives: 508 us -> none
    unnamed x33 -> x0, starting transfers between devices: 248 us -> none
    reduce_scatter x1 -> x0, waiting for transfers between devices: 248 us -> none  [on_device(): lax.psum_scatter(out_grad, ('seq', 'dp'), scatter_dimension=0, tiled=True)]
    unnamed x193 -> x333, local copies, waits for them, and re-layouts: 183 us -> 9.43 us
    unnamed x37 -> x1, waiting for transfers between devices: 161 us -> 0.02 us
    add x35 -> x39, other arithmetic: 139 us -> 14.9 us  [the longest x1 10.2 us: on_device(): d_x = exact(dt, spread) * du + skip_wide * dy]
    all_gather x2 -> x1, waiting for transfers between devices: 69.4 us -> 17.5 us  [on_device(): lax.all_gather(jnp.concatenate([in_rows_low, out_rows_low], axis=1), CHIP...]
  transfers between devices with their start and end apart: 68 -> 57, of which waited for: 36 -> 25; matrix products, arithmetic and copies ran while one was open for 1% -> 32% of each run, Pallas kernels for 0% -> 0%
where the time goes in v1:
time: 580 us; the launch traced here: 572 us
  matrix products  134 us (23%)
  waiting for transfers between devices  118 us (20%)
  local copies, waits for them, and re-layouts  85.8 us (15%)
  starting transfers between devices  82.8 us (14%)
  other arithmetic  79.9 us (14%)
  blocking collectives  54.4 us (9%)
  between operations  17.2 us (3%)
    ppermute x30, waiting for transfers between devices, exchange(): return lax.ppermute(value, axes, pairs)  79.4 us
    dot_general x19, matrix products, mm(): lax.dot_general(a.astype(BF16), b.astype(BF16), (dims, ((), ())), preferr...  77.5 us
    all_gather x1, blocking collectives, on_device(): small_all = lax.all_gather(small, ALL, axis=0, tiled=False)  54.4 us
    ppermute x30, starting transfers between devices, exchange(): return lax.ppermute(value, axes, pairs)  32.9 us
    dot_general x9, matrix products, exact(): lax.dot_general(a, b, (dims, ((), ())), precision=PRECISE, preferred_elem...  22.9 us
    ppermute x8, starting transfers between devices, along_y(): lax.ppermute(value, 'y', [(y, y + steps) for y in range(4) if 0 <= y + st...  18.4 us
    all_gather x1, waiting for transfers between devices, on_device(): lax.all_gather(jnp.concatenate([in_rows_low, out_rows_low], axis=1), CHIP...  17.5 us
    dot_general x5, matrix products, product(): return jnp.einsum(terms, a, b, preferred_element_type=F32)  14.7 us
  transfers between devices with their start and end apart: 57, of which 25 were waited for; matrix products, arithmetic and copies ran while one was open for 32% of the time, Pallas kernels for 0%

profile of v1, /device:TPU:7, one launch (start us, length us, event | category | flops | bytes accessed | tf_op | source)
XLA Modules:
  0.0 571.9 jit_solution(16961723936643656010)
XLA Ops:
  12.7 4.7 collective-permute-start.5
  22.8 54.4 %all_gather.13 = f32[128,8,128]{2,1,0:T(8,128)S(1)} all-gather(f32[1,8,128]{2,1,0:T(8,128)S(1)} %scatter.9), channel_id=1, replica_groups=mesh['y'=4,'x'=4,'z'=4,'c'=2] {'y','x','z','c'}, dimensions={0}, use_global_device_ids=true | all-gather | bytes 528384 | tf_op jit(solution)/shard_map/all_gather | solution.py:290
  99.3 4.7 fusion.46
  104.0 4.3 fusion.47
  108.2 17.5 %all-gather.2.cloned.1.call-done = bf16[1536,4992]{1,0:T(8,128)(2,1)} async-done(((bf16[24,4992]{1,0:T(8,128)(2,1)}), bf16[1536,4992]{1,0:T(8,128)(2,1)}) %all-gather.2.cloned.1.call-update) | async-done | bytes 15335440 | tf_op jit(solution)/shard_map/all_gather | solution.py:291
  125.8 5.6 fusion.7
  143.4 4.8 reduce-precision_convert_fusion.1
  153.2 5.5 collective-permute-start.7
  178.3 7.2 %fusion.21 = f32[512,1536]{1,0:T(8,128)} fusion(bf16[1536,4992]{1,0:T(8,128)(2,1)} %all-gather.2.cloned.1.call-done, bf16[528,1536]{1,0:T(8,128)(2,1)} %copy-done.48), kind=kOutput, calls=%fused_computation.35 | convolution fusion | flops 2415919104 | bytes 9437184 | tf_op jit(solution)/shard_map/dot_general | solution.py:47
  185.6 5.4 fusion.57
  218.3 3.9 copy.94
  230.5 4.6 add_bitcast_fusion
  240.9 13.1 %multiply_reduce_fusion.7 = (f32[512]{0:T(512)S(1)}, f32[512]{0:T(512)S(1)}, f32[512,1536]{1,0:T(8,128)}, f32[512,1536]{1,0:T(8,128)}, f32[512,1536]{1,0:T(8,128)}) fusion(f32[1536]{0:T(1024)S(1)} %copy-done.99, f32[512,1536]{1,0:T(8,128)} %fusion.21, f32[512,1792]{1,0:T(8,128)S(1)} %copy-done.1, f32[1536]{0:T(1024)S(1)} %copy-done.96, ...), kind=kOutput, calls=%fused_computation.84 | convolution fusion | flops 2426928128 | bytes 32522240 | tf_op jit(solution)/shard_map/dot_general | solution.py:47
  256.2 4.7 fusion.233
  261.8 4.9 multiply_reduce_fusion.4
  278.7 4.1 fusion.48
  291.4 4.5 fusion.4
  305.2 3.9 copy.95
  328.8 10.2 %multiply_add_fusion = (f32[512,1536]{1,0:T(8,128)}, f32[512,1536]{1,0:T(8,128)}) fusion(f32[512,1536]{1,0:T(8,128)S(1)} %get-tuple-element.59, f32[512,1536]{1,0:T(8,128)} %get-tuple-element.147, f32[1536]{0:T(1024)S(1)} %copy-done.98, f32[512,1536]{1,0:T(8,128)} %copy-done.13, f32[4,128,1536]{2,1,0:T(8,128)} %fusion.127, f32[64,8,12,128]{3,2,1,0:T(8,128)} %bitcast.323), kind=kLoop, calls=%fused_computation.78 | loop fusion | flops 3932160 | bytes 22026240 | tf_op jit(solution)/shard_map/add | solution.py:456
  339.1 6.2 %multiply_reduce_fusion.2 = (f32[1792]{0:T(1024)S(1)}, f32[1792]{0:T(1024)S(1)}, f32[1792]{0:T(1024)S(1)}, f32[1792]{0:T(1024)S(1)}, f32[1792]{0:T(1024)S(1)}, /*index=5*/f32[512,1792]{1,0:T(8,128)S(1)}) fusion(f32[512,1792]{1,0:T(8,128)S(1)} %copy-done.6, f32[8,1792]{1,0:T(8,128)S(1)} %slice.847, f32[528,1920]{1,0:T(8,128)} %copy-done.16, ...), kind=kLoop, calls=%fused_computation.48 | loop fusion | flops 20176128 | bytes 18443264 | tf_op jit(solution)/shard_map/reduce_sum | solution.py:464
  357.0 6.3 %collective-permute-start.49 = (f32[8,128]{1,0:T(8,128)S(1)}, f32[8,128]{1,0:T(8,128)S(1)}, u32[]{:S(2)}, u32[]{:S(2)}) collective-permute-start(f32[8,128]{1,0:T(8,128)S(1)} %select_maximum_fusion), channel_id=1, source_target_pairs={{0,32},{1,97},{32,0},{33,65},{64,96},{65,33},{96,64},{97,1},{2,34}... | collective-permute-start | bytes 12296 | tf_op jit(solution)/shard_map/ppermute | solution.py:119
  370.9 8.7 %select_convert_fusion = bf16[1536,3328]{1,0:T(8,128)(2,1)} fusion(s32[1536]{0:T(1024)S(1)} %copy-done.114, s32[3328]{0:T(1024)S(1)} %copy-done.105, s32[3328]{0:T(1024)S(1)} %copy-done.106, pred[3328]{0:T(1024)(128)(4,1)S(1)} %copy-done.130, s32[1536]{0:T(1024)S(1)} %copy-done.115, f32[8,256]{1,0:T(8,128)S(1)} %slice-done.7, f32[8,3072]{1,0:T(8,128)S(1)} %pad_select_fusion), kind=kOutput, calls=%fused_computation | convolution fusion | flops 265852928 | bytes 10372352 | tf_op jit(solution)/shard_map/dot_general | solution.py:53
  382.4 7.1 %fusion.64 = f32[1536,128]{1,0:T(8,128)S(1)} fusion(bf16[1536,3328]{1,0:T(8,128)(2,1)} %select_convert_fusion, s32[3328]{0:T(1024)S(1)} %copy-done.103, s32[3328]{0:T(1024)S(1)} %copy-done.104, pred[3328]{0:T(1024)(128)(4,1)S(1)} %copy-done.129), kind=kOutput, calls=%fused_computation.118 | convolution fusion | flops 1309900800 | bytes 11040000 | tf_op jit(solution)/shard_map/dot_general | solution.py:47
  405.3 5.2 collective-permute-start.17
  431.4 27.9 %collective-permute-done.39 = bf16[768,1536]{1,0:T(8,128)(2,1)} collective-permute-done((bf16[768,1536]{1,0:T(8,128)(2,1)}, bf16[768,1536]{1,0:T(8,128)(2,1)}, u32[]{:S(2)}, u32[]{:S(2)}) %collective-permute-start.39) | collective-permute-done | bytes 2359328 | tf_op jit(solution)/shard_map/ppermute | solution.py:119
  469.4 4.9 collective-permute-done.28
  474.3 3.9 collective-permute-start.22
  478.3 5.8 %collective-permute-done.19 = f32[128,1536]{1,0:T(8,128)S(1)} collective-permute-done((f32[128,1536]{1,0:T(8,128)S(1)}, f32[128,1536]{1,0:T(8,128)S(1)}, u32[]{:S(2)}, u32[]{:S(2)}) %collective-permute-start.19) | collective-permute-done | bytes 786464 | tf_op jit(solution)/shard_map/ppermute | solution.py:93
  485.5 4.6 collective-permute-done.29
  492.0 9.6 %collective-permute-done.22 = bf16[192,1024]{1,0:T(8,128)(2,1)S(1)} collective-permute-done((bf16[192,1024]{1,0:T(8,128)(2,1)S(1)}, bf16[192,1024]{1,0:T(8,128)(2,1)S(1)}, u32[]{:S(2)}, u32[]{:S(2)}) %collective-permute-start.22) | collective-permute-done | bytes 393248 | tf_op jit(solution)/shard_map/ppermute | solution.py:119
  515.1 7.1 %collective-permute-done.41 = bf16[192,1536]{1,0:T(8,128)(2,1)S(1)} collective-permute-done((bf16[192,1536]{1,0:T(8,128)(2,1)S(1)}, bf16[192,1536]{1,0:T(8,128)(2,1)S(1)}, u32[]{:S(2)}, u32[]{:S(2)}) %collective-permute-start.41) | collective-permute-done | bytes 589856 | tf_op jit(solution)/shard_map/ppermute | solution.py:119
  537.1 7.8 %collective-permute-start.45 = (f32[24,1536]{1,0:T(8,128)S(1)}, f32[24,1536]{1,0:T(8,128)S(1)}, u32[]{:S(2)}, u32[]{:S(2)}) collective-permute-start(f32[24,1536]{1,0:T(8,128)S(1)} %slice_add_fusion.17), channel_id=1, source_target_pairs={{0,0},{1,64},{32,32},{33,96},{64,1},{65,65},{96,33},{97,97},{2,2},... | collective-permute-start | bytes 442376 | tf_op jit(solution)/shard_map/ppermute | solution.py:102
  (698 shorter events, 281.6 us)
Async XLA Ops:
  7.2 118.6 %all-gather.2.cloned.1.call-start = ((), (), s32[]{:S(2)}) async-start(), calls=%async_computation | async-start | bytes 15575040 | tf_op jit(solution)/shard_map/all_gather | solution.py:291
  21.2 64.0 %collective-permute-start = (bf16[2,128,1536]{2,1,0:T(8,128)(2,1)S(1)}, bf16[2,128,1536]{2,1,0:T(8,128)(2,1)S(1)}, u32[]{:S(2)}, u32[]{:S(2)}) collective-permute-start(bf16[2,128,1536]{2,1,0:T(8,128)(2,1)S(1)} %get-tuple-element.101), channel_id=1, source_target_pairs={{0,0},{1,16},{8,8},{9,24},{16,1},{17,17},{24,9},{25,25},{2,2},{3,1... | collective-permute-start | bytes 2359304 | tf_op jit(solution)/shard_map/ppermute | solution.py:93
  21.9 63.2 %collective-permute-start.1 = (bf16[2,128,1536]{2,1,0:T(8,128)(2,1)S(1)}, bf16[2,128,1536]{2,1,0:T(8,128)(2,1)}, u32[]{:S(2)}, u32[]{:S(2)}) collective-permute-start(bf16[2,128,1536]{2,1,0:T(8,128)(2,1)S(1)} %get-tuple-element.102), channel_id=1, source_target_pairs={{0,8},{1,24},{8,0},{9,16},{16,9},{17,25},{24,1},{25,17},{2,10},{3,... | collective-permute-start | bytes 2359304 | tf_op jit(solution)/shard_map/ppermute | solution.py:93
  153.2 71.9 %collective-permute-start.7 = (f32[1544,128]{1,0:T(8,128)}, f32[1544,128]{1,0:T(8,128)}, u32[]{:S(2)}, u32[]{:S(2)}) collective-permute-start(f32[1544,128]{1,0:T(8,128)} %pad_maximum_fusion.12), channel_id=1, source_target_pairs={{0,64},{32,96},{1,65},{33,97},{2,66},{34,98},{3,67},{35,99},{4,68}... | collective-permute-start | bytes 2371592 | tf_op jit(solution)/shard_map/ppermute | solution.py:106
  158.7 69.1 %collective-permute-start.6 = (f32[1544,128]{1,0:T(8,128)}, f32[1544,128]{1,0:T(8,128)}, u32[]{:S(2)}, u32[]{:S(2)}) collective-permute-start(f32[1544,128]{1,0:T(8,128)} %pad_maximum_fusion.12), channel_id=1, source_target_pairs={{0,32},{32,64},{64,96},{1,33},{33,65},{65,97},{2,34},{34,66},{66,9... | collective-permute-start | bytes 2371592 | tf_op jit(solution)/shard_map/ppermute | solution.py:106
  192.2 38.3 %collective-permute-start.8 = (f32[1544,128]{1,0:T(8,128)}, f32[1544,128]{1,0:T(8,128)}, u32[]{:S(2)}, u32[]{:S(2)}) collective-permute-start(f32[1544,128]{1,0:T(8,128)} %pad_maximum_fusion.12), channel_id=1, source_target_pairs={{0,96},{1,97},{2,98},{3,99},{4,100},{5,101},{6,102},{7,103},{8,104... | collective-permute-start | bytes 2371592 | tf_op jit(solution)/shard_map/ppermute | solution.py:106
  274.9 42.2 %collective-permute-start.15 = (bf16[1552,128]{1,0:T(8,128)(2,1)}, bf16[1552,128]{1,0:T(8,128)(2,1)}, u32[]{:S(2)}, u32[]{:S(2)}) collective-permute-start(bf16[1552,128]{1,0:T(8,128)(2,1)} %pad_maximum_fusion.15), channel_id=1, source_target_pairs={{96,0},{97,1},{98,2},{99,3},{100,4},{101,5},{102,6},{103,7},{104,8... | collective-permute-start | bytes 1191944 | tf_op jit(solution)/shard_map/ppermute | solution.py:106
  276.1 35.4 %collective-permute-start.14 = (bf16[1552,128]{1,0:T(8,128)(2,1)}, bf16[1552,128]{1,0:T(8,128)(2,1)}, u32[]{:S(2)}, u32[]{:S(2)}) collective-permute-start(bf16[1552,128]{1,0:T(8,128)(2,1)} %pad_maximum_fusion.15), channel_id=1, source_target_pairs={{64,0},{96,32},{65,1},{97,33},{66,2},{98,34},{67,3},{99,35},{68,4}... | collective-permute-start | bytes 1191944 | tf_op jit(solution)/shard_map/ppermute | solution.py:106
  277.4 36.8 %collective-permute-start.13 = (bf16[1552,128]{1,0:T(8,128)(2,1)}, bf16[1552,128]{1,0:T(8,128)(2,1)}, u32[]{:S(2)}, u32[]{:S(2)}) collective-permute-start(bf16[1552,128]{1,0:T(8,128)(2,1)} %pad_maximum_fusion.15), channel_id=1, source_target_pairs={{32,0},{64,32},{96,64},{33,1},{65,33},{97,65},{34,2},{66,34},{98,6... | collective-permute-start | bytes 1191944 | tf_op jit(solution)/shard_map/ppermute | solution.py:106
  357.0 32.5 %collective-permute-start.49 = (f32[8,128]{1,0:T(8,128)S(1)}, f32[8,128]{1,0:T(8,128)S(1)}, u32[]{:S(2)}, u32[]{:S(2)}) collective-permute-start(f32[8,128]{1,0:T(8,128)S(1)} %select_maximum_fusion), channel_id=1, source_target_pairs={{0,32},{1,97},{32,0},{33,65},{64,96},{65,33},{96,64},{97,1},{2,34}... | collective-permute-start | bytes 12296 | tf_op jit(solution)/shard_map/ppermute | solution.py:119
  365.9 58.7 %collective-permute-start.20 = (bf16[768,1024]{1,0:T(8,128)(2,1)}, bf16[768,1024]{1,0:T(8,128)(2,1)}, u32[]{:S(2)}, u32[]{:S(2)}) collective-permute-start(bf16[768,1024]{1,0:T(8,128)(2,1)} %convolution_convert_fusion.2), channel_id=1, source_target_pairs={{0,32},{1,97},{32,0},{33,65},{64,96},{65,33},{96,64},{97,1},{2,34}... | collective-permute-start | bytes 4718600 | tf_op jit(solution)/shard_map/ppermute | solution.py:119
  369.5 35.4 %collective-permute-start.16 = (f32[16,1536]{1,0:T(8,128)S(1)}, f32[16,1536]{1,0:T(8,128)S(1)}, u32[]{:S(2)}, u32[]{:S(2)}) collective-permute-start(f32[16,1536]{1,0:T(8,128)S(1)} %slice.895), channel_id=1, source_target_pairs={{32,0},{64,32},{96,64},{33,1},{65,33},{97,65},{34,2},{66,34},{98,6... | collective-permute-start | bytes 294920 | tf_op jit(solution)/shard_map/ppermute | solution.py:106
  403.8 18.5 %collective-permute-start.26 = (bf16[768,896]{1,0:T(8,128)(2,1)S(1)}, bf16[768,896]{1,0:T(8,128)(2,1)S(1)}, u32[]{:S(2)}, u32[]{:S(2)}) collective-permute-start(bf16[768,896]{1,0:T(8,128)(2,1)S(1)} %add_convert_fusion.1), channel_id=1, source_target_pairs={{0,8},{1,25},{8,0},{9,17},{16,24},{17,9},{24,16},{25,1},{2,10},{3,... | collective-permute-start | bytes 4128776 | tf_op jit(solution)/shard_map/ppermute | solution.py:119
  405.3 22.5 %collective-permute-start.17 = (f32[256,1536]{1,0:T(8,128)S(1)}, f32[256,1536]{1,0:T(8,128)S(1)}, u32[]{:S(2)}, u32[]{:S(2)}) collective-permute-start(f32[256,1536]{1,0:T(8,128)S(1)} %slice_select_fusion), channel_id=1, source_target_pairs={{0,1},{1,0},{2,3},{3,2},{4,5},{5,4},{6,7},{7,6},{8,9},{9,8},{10,11... | collective-permute-start | bytes 4718600 | tf_op jit(solution)/shard_map/ppermute | solution.py:86
  413.3 16.1 %collective-permute-start.10 = (f32[256,1536]{1,0:T(8,128)S(1)}, f32[256,1536]{1,0:T(8,128)S(1)}, u32[]{:S(2)}, u32[]{:S(2)}) collective-permute-start(f32[256,1536]{1,0:T(8,128)S(1)} %copy-done.49), channel_id=1, source_target_pairs={{0,1},{1,0},{2,3},{3,2},{4,5},{5,4},{6,7},{7,6},{8,9},{9,8},{10,11... | collective-permute-start | bytes 4718600 | tf_op jit(solution)/shard_map/ppermute | solution.py:86
  416.7 42.5 %collective-permute-start.39 = (bf16[768,1536]{1,0:T(8,128)(2,1)}, bf16[768,1536]{1,0:T(8,128)(2,1)}, u32[]{:S(2)}, u32[]{:S(2)}) collective-permute-start(bf16[768,1536]{1,0:T(8,128)(2,1)} %convolution_convert_fusion), channel_id=1, source_target_pairs={{0,8},{1,25},{8,0},{9,17},{16,24},{17,9},{24,16},{25,1},{2,10},{3,... | collective-permute-start | bytes 7077896 | tf_op jit(solution)/shard_map/ppermute | solution.py:119
  422.3 40.1 %collective-permute-start.32 = (bf16[768,1536]{1,0:T(8,128)(2,1)}, bf16[768,1536]{1,0:T(8,128)(2,1)S(1)}, u32[]{:S(2)}, u32[]{:S(2)}) collective-permute-start(bf16[768,1536]{1,0:T(8,128)(2,1)} %convolution_convert_fusion.1), channel_id=1, source_target_pairs={{0,32},{1,97},{32,0},{33,65},{64,96},{65,33},{96,64},{97,1},{2,34}... | collective-permute-start | bytes 7077896 | tf_op jit(solution)/shard_map/ppermute | solution.py:119
  424.6 40.2 %collective-permute-start.27 = (bf16[384,896]{1,0:T(8,128)(2,1)S(1)}, bf16[384,896]{1,0:T(8,128)(2,1)S(1)}, u32[]{:S(2)}, u32[]{:S(2)}) collective-permute-start(bf16[384,896]{1,0:T(8,128)(2,1)S(1)} %slice.1293), channel_id=1, source_target_pairs={{0,24},{1,9},{8,16},{9,1},{16,8},{17,25},{24,0},{25,17},{2,26},{3,... | collective-permute-start | bytes 2064392 | tf_op jit(solution)/shard_map/ppermute | solution.py:119
  427.8 41.4 %collective-permute-start.21 = (bf16[384,1024]{1,0:T(8,128)(2,1)S(1)}, bf16[384,1024]{1,0:T(8,128)(2,1)S(1)}, u32[]{:S(2)}, u32[]{:S(2)}) collective-permute-start(bf16[384,1024]{1,0:T(8,128)(2,1)S(1)} %slice.1292), channel_id=1, source_target_pairs={{0,96},{1,33},{32,64},{33,1},{64,32},{65,97},{96,0},{97,65},{2,98}... | collective-permute-start | bytes 2359304 | tf_op jit(solution)/shard_map/ppermute | solution.py:119
  430.4 36.1 %collective-permute-start.11 = (bf16[128,1536]{1,0:T(8,128)(2,1)S(1)}, bf16[128,1536]{1,0:T(8,128)(2,1)S(1)}, u32[]{:S(2)}, u32[]{:S(2)}) collective-permute-start(bf16[128,1536]{1,0:T(8,128)(2,1)S(1)} %get-tuple-element.107), channel_id=1, source_target_pairs={{0,0},{1,16},{8,8},{9,24},{16,1},{17,17},{24,9},{25,25},{2,2},{3,1... | collective-permute-start | bytes 1179656 | tf_op jit(solution)/shard_map/ppermute | solution.py:93
  462.3 15.9 %collective-permute-start.18 = (f32[128,1536]{1,0:T(8,128)S(1)}, f32[128,1536]{1,0:T(8,128)S(1)}, u32[]{:S(2)}, u32[]{:S(2)}) collective-permute-start(f32[128,1536]{1,0:T(8,128)S(1)} %get-tuple-element.97), channel_id=1, source_target_pairs={{0,0},{1,16},{8,8},{9,24},{16,1},{17,17},{24,9},{25,25},{2,2},{3,1... | collective-permute-start | bytes 2359304 | tf_op jit(solution)/shard_map/ppermute | solution.py:93
  464.8 19.4 %collective-permute-start.19 = (f32[128,1536]{1,0:T(8,128)S(1)}, f32[128,1536]{1,0:T(8,128)S(1)}, u32[]{:S(2)}, u32[]{:S(2)}) collective-permute-start(f32[128,1536]{1,0:T(8,128)S(1)} %get-tuple-element.98), channel_id=1, source_target_pairs={{0,8},{1,24},{8,0},{9,16},{16,9},{17,25},{24,1},{25,17},{2,10},{3,... | collective-permute-start | bytes 2359304 | tf_op jit(solution)/shard_map/ppermute | solution.py:93
  466.5 45.3 %collective-permute-start.40 = (bf16[384,1536]{1,0:T(8,128)(2,1)S(1)}, bf16[384,1536]{1,0:T(8,128)(2,1)S(1)}, u32[]{:S(2)}, u32[]{:S(2)}) collective-permute-start(bf16[384,1536]{1,0:T(8,128)(2,1)S(1)} %slice.1290), channel_id=1, source_target_pairs={{0,24},{1,9},{8,16},{9,1},{16,8},{17,25},{24,0},{25,17},{2,26},{3,... | collective-permute-start | bytes 3538952 | tf_op jit(solution)/shard_map/ppermute | solution.py:119
  469.1 45.4 %collective-permute-start.33 = (bf16[384,1536]{1,0:T(8,128)(2,1)S(1)}, bf16[384,1536]{1,0:T(8,128)(2,1)S(1)}, u32[]{:S(2)}, u32[]{:S(2)}) collective-permute-start(bf16[384,1536]{1,0:T(8,128)(2,1)S(1)} %slice.1291), channel_id=1, source_target_pairs={{0,96},{1,33},{32,64},{33,1},{64,32},{65,97},{96,0},{97,65},{2,98}... | collective-permute-start | bytes 3538952 | tf_op jit(solution)/shard_map/ppermute | solution.py:119
  474.3 27.3 %collective-permute-start.22 = (bf16[192,1024]{1,0:T(8,128)(2,1)S(1)}, bf16[192,1024]{1,0:T(8,128)(2,1)S(1)}, u32[]{:S(2)}, u32[]{:S(2)}) collective-permute-start(bf16[192,1024]{1,0:T(8,128)(2,1)S(1)} %slice.1296), channel_id=1, source_target_pairs={{0,8},{1,25},{8,0},{9,17},{16,24},{17,9},{24,16},{25,1},{2,10},{3,... | collective-permute-start | bytes 1179656 | tf_op jit(solution)/shard_map/ppermute | solution.py:119
  478.3 11.8 %collective-permute-start.29 = (bf16[96,896]{1,0:T(8,128)(2,1)S(1)}, bf16[96,896]{1,0:T(8,128)(2,1)S(1)}, u32[]{:S(2)}, u32[]{:S(2)}) collective-permute-start(bf16[96,896]{1,0:T(8,128)(2,1)S(1)} %slice.1301), channel_id=1, source_target_pairs={{0,96},{1,33},{32,64},{33,1},{64,32},{65,97},{96,0},{97,65},{2,98}... | collective-permute-start | bytes 516104 | tf_op jit(solution)/shard_map/ppermute | solution.py:119
  490.1 13.2 %collective-permute-start.30 = (bf16[48,896]{1,0:T(8,128)(2,1)S(1)}, bf16[48,896]{1,0:T(8,128)(2,1)S(1)}, u32[]{:S(2)}, u32[]{:S(2)}) collective-permute-start(bf16[48,896]{1,0:T(8,128)(2,1)S(1)} %slice.1305), channel_id=1, source_target_pairs={{0,2},{1,7},{2,0},{3,5},{4,6},{5,3},{6,4},{7,1},{8,10},{9,15},{10,... | collective-permute-start | bytes 258056 | tf_op jit(solution)/shard_map/ppermute | solution.py:119
  512.2 10.0 %collective-permute-start.41 = (bf16[192,1536]{1,0:T(8,128)(2,1)S(1)}, bf16[192,1536]{1,0:T(8,128)(2,1)S(1)}, u32[]{:S(2)}, u32[]{:S(2)}) collective-permute-start(bf16[192,1536]{1,0:T(8,128)(2,1)S(1)} %slice.1294), channel_id=1, source_target_pairs={{0,32},{1,97},{32,0},{33,65},{64,96},{65,33},{96,64},{97,1},{2,34}... | collective-permute-start | bytes 1769480 | tf_op jit(solution)/shard_map/ppermute | solution.py:119
  515.0 10.0 %collective-permute-start.34 = (bf16[192,1536]{1,0:T(8,128)(2,1)S(1)}, bf16[192,1536]{1,0:T(8,128)(2,1)S(1)}, u32[]{:S(2)}, u32[]{:S(2)}) collective-permute-start(bf16[192,1536]{1,0:T(8,128)(2,1)S(1)} %slice.1295), channel_id=1, source_target_pairs={{0,8},{1,25},{8,0},{9,17},{16,24},{17,9},{24,16},{25,1},{2,10},{3,... | collective-permute-start | bytes 1769480 | tf_op jit(solution)/shard_map/ppermute | solution.py:119
  537.1 10.7 %collective-permute-start.45 = (f32[24,1536]{1,0:T(8,128)S(1)}, f32[24,1536]{1,0:T(8,128)S(1)}, u32[]{:S(2)}, u32[]{:S(2)}) collective-permute-start(f32[24,1536]{1,0:T(8,128)S(1)} %slice_add_fusion.17), channel_id=1, source_target_pairs={{0,0},{1,64},{32,32},{33,96},{64,1},{65,65},{96,33},{97,97},{2,2},... | collective-permute-start | bytes 442376 | tf_op jit(solution)/shard_map/ppermute | solution.py:102
  550.4 10.6 %collective-permute-start.48 = (f32[12]{0:T(128)S(1)}, f32[12]{0:T(128)S(1)}, u32[]{:S(2)}, u32[]{:S(2)}) collective-permute-start(f32[12]{0:T(128)S(1)} %dynamic-slice_divide_fusion), channel_id=1, source_target_pairs={{2,0},{5,1},{8,2},{11,3},{14,4},{17,5},{20,6},{23,7},{26,8},{29,9}... | collective-permute-start | bytes 152 | tf_op jit(solution)/shard_map/ppermute | solution.py:545
  551.7 11.2 %collective-permute-start.47 = (f32[12]{0:T(128)S(1)}, f32[12]{0:T(128)S(1)}, u32[]{:S(2)}, u32[]{:S(2)}) collective-permute-start(f32[12]{0:T(128)S(1)} %dynamic-slice_divide_fusion), channel_id=1, source_target_pairs={{1,0},{4,1},{7,2},{10,3},{13,4},{16,5},{19,6},{22,7},{25,8},{28,9}... | collective-permute-start | bytes 152 | tf_op jit(solution)/shard_map/ppermute | solution.py:545
  (194 other events, 1730.7 us)
Sparse Core Ops, SparseCore 0:
  20.7 104.9 all-gather.1

commit v2 on v1

--- a/solution.py
+++ b/solution.py
@@ -61,6 +61,10 @@
     return lax.reduce_precision(v, 8, 7)
 
 
+def hold(*values):
+    return lax.optimization_barrier(values)
+
+
 def iota(shape, dim):
     return lax.broadcasted_iota(jnp.int32, shape, dim)
 
@@ -149,17 +153,37 @@
     return (rows[:, None] == iota((1536, 1536), 1)).astype(BF16)
 
 
-def reduce_scatter(sends, keeps, orders):
-    for step in range(6):
-        arrived = []
-        for send, order in zip(sends, orders):
-            arrived.append(exchange(send.astype(BF16), order[step // 2], step % 2))
-        totals = [keep.astype(F32) + got.astype(F32) for keep, got in zip(keeps, arrived)]
+class Halving:
+    def __init__(self, sends, keeps, orders):
+        self.sends = [v.astype(BF16) for v in sends]
+        self.keeps, self.orders, self.step = keeps, orders, 0
+        self.start()
+
+    def start(self):
+        self.arrived = [
+            exchange(v, order[self.step // 2], self.step % 2)
+            for v, order in zip(self.sends, self.orders)
+        ]
+
+    def add(self):
+        totals = [keep + got.astype(F32) for keep, got in zip(self.keeps, self.arrived)]
+        self.step += 1
+        if self.step == 6:
+            self.totals = totals
+            return
         half = totals[0].shape[0] // 2
-        if step < 5:
-            sends = [t[half:] for t in totals]
-            keeps = [t[:half] for t in totals]
-    return totals
+        self.sends = [t[half:].astype(BF16) for t in totals]
+        self.keeps = [t[:half] for t in totals]
+        self.start()
+
+
+def wait(halvings, *values):
+    held = [h.arrived for h in halvings], [h.keeps for h in halvings], values
+    arrived, keeps, values = lax.optimization_barrier(held)
+    for h, a, k in zip(halvings, arrived, keeps):
+        h.arrived, h.keeps = a, k
+        h.add()
+    return values
 
 
 PAIRS = HALF_HEADS // 2
@@ -267,13 +291,21 @@
             flag, jnp.concatenate([mine, other], axis=axis), jnp.concatenate([other, mine], axis=axis)
         )
 
+    riders_out = jnp.concatenate(
+        [
+            jnp.pad(conv_master, ((0, 0), (0, LANES - HALF_HEADS - 26))),
+            jnp.pad(gain_master[None], ((0, 6), (0, LANES - HALF_HEADS - 36))),
+        ],
+        axis=0,
+    )
+
     def half_columns(c):
         return jnp.concatenate(
             [
                 in_master[:, INNER + c * HALF : INNER + (c + 1) * HALF],
                 in_master[:, 2 * INNER : INNER + CONV],
                 in_master[:, INNER + CONV + c * HALF_HEADS : INNER + CONV + (c + 1) * HALF_HEADS],
-                jnp.zeros((12, LANES - HALF_HEADS), F32),
+                riders_out,
                 in_master[:, c * HALF : (c + 1) * HALF],
             ],
             axis=1,
@@ -284,28 +316,30 @@
     theirs = jnp.where(first_core, halves[1], halves[0])
     in_rows_low = ordered(first_core, mine, swap_cores(theirs)).astype(BF16)
     out_rows_low = cross_halves(out_master).astype(BF16)
-    small = jnp.zeros((8, LANES), F32)
-    small = small.at[:5, :26].set(rounded(conv_master))
-    small = small.at[5, :36].set(rounded(gain_master))
-    small_all = lax.all_gather(small, ALL, axis=0, tiled=False)
-    gathered = lax.all_gather(
-        jnp.concatenate([in_rows_low, out_rows_low], axis=1), CHIPS, axis=0, tiled=True
-    )
-    w_crit = gathered[:, :CRIT]
-    w_gate = gathered[:, CRIT : CRIT + HALF]
+    w_crit = lax.all_gather(in_rows_low[:, :CRIT], CHIPS, axis=0, tiled=True)
+    rest_low = jnp.concatenate([in_rows_low[:, CRIT:], out_rows_low], axis=1)
+    rest_low, w_crit = hold(rest_low, w_crit)
+    w_rest = lax.all_gather(rest_low, CHIPS, axis=0, tiled=True)
+    w_gate = w_rest[:, :HALF]
     w_out = (
-        gathered[:, CRIT + HALF :]
+        w_rest[:, HALF:]
         .reshape(2, 2, 16, ROWS, WIDTH)
         .transpose(1, 2, 0, 3, 4)
         .reshape(HALF, WIDTH)
     )
-    conv_all = small_all[:, :5, :26].transpose(1, 0, 2).reshape(5, CONV)
-    gain_all = small_all[:, 5, :36].reshape(-1)
-    norm_gain = gain_all[:WIDTH]
-    gate_gain = lax.dynamic_slice(gain_all, (WIDTH + core * HALF,), (HALF,))
-    conv_weights = jnp.concatenate(
-        [lax.dynamic_slice(conv_all, (0, core * HALF), (5, HALF)), conv_all[:, INNER:]], axis=1
-    )
+    smalls = w_crit[:, ACT:]
+    device_at, slot_at = iota((1536, 1), 0) // 12, iota((1536, 1), 0) % 12
+
+    def gather_small(columns, width, slots):
+        unfold = (HALF_HEADS + columns % width == iota((LANES, columns.shape[1]), 0)).astype(BF16)
+        wide = jnp.where(device_at == columns // width, mm(smalls, unfold), 0.0)
+        return mm((slot_at == slots).astype(BF16), wide, TN)
+
+    norm_gain = gather_small(iota((1, WIDTH), 1), 36, 5 + iota((1, 8), 1))[0]
+    gate_gain = gather_small(WIDTH + core * HALF + iota((1, HALF), 1), 36, 5 + iota((1, 8), 1))[0]
+    conv_at = iota((1, ACT), 1)
+    conv_at = jnp.where(conv_at < HALF, core * HALF + conv_at, INNER - HALF + conv_at)
+    conv_weights = gather_small(conv_at, 26, iota((1, 8), 1))
     head_half = jnp.pad(
         lax.dynamic_slice(head_master, (0, core * HALF_HEADS), (3, HALF_HEADS)),
         ((0, 0), (0, LANES - HALF_HEADS)),
@@ -398,15 +432,6 @@
         back[k] = sum((between(k + 1, i) * chunk_backs[i] for i in range(k + 1, CHUNKS)), jnp.zeros_like(own[0]))
     to_before = sum(between(0, i) * chunk_backs[i] for i in range(CHUNKS))
     leaving = combine(pack_state(to_before, piece_decay), -1, unpack_state)
-    dy_pairs = by_pair(dy_low.astype(BF16))
-    du_chunk = from_pairs(product("kpjts,kpjtc->kpsc", mixes, one_head(dy_pairs)))
-    both = product("kptc,kpjsc->kpjts", dy_pairs, u_pairs)
-    d_scores = jnp.sum(decay * both, axis=(1, 2)).astype(BF16)
-    db_chunk = product("kts,ktn->ksn", d_scores, c_low)
-    dc_chunk = product("kts,ksn->ktn", d_scores, b_low)
-
-    part_out = mm(gated_low, w_out)
-
     def own_rows(value):
         return jnp.where(first_core, value[:OWN], value[OWN:]), jnp.where(
             first_core, value[OWN:], value[:OWN]
@@ -417,10 +442,6 @@
         sent = [jnp.where(even_x, low, high), jnp.where(even_x, high, low)]
         back0, back1 = regroup(sent[0], 0), regroup(sent[1], 1)
         return jnp.where(even_x, jnp.stack([back0, back1]), jnp.stack([back1, back0]))
-
-    kept, other = own_rows(part_out)
-    own_out = own_in.astype(F32) + (kept + swap_cores(other))
-    block_out = to_owner(own_out.astype(BF16))
 
     order_a, order_b = ("y", "x", "z"), ("x", "y", "z")
     pick_in_a, pick_in_b = pick(in_rows(order_a)), pick(in_rows(order_b))
@@ -429,16 +450,31 @@
     normed_b = mm(pick_in_b, normed, NT).astype(BF16)
     gated_b = mm(pick_out_b, gated_low, NT).astype(BF16)
     middle = WIDTH // 2
-    gate_rows, out_rows_grad = reduce_scatter(
+    first = Halving(
         [mm(normed_a[middle:, :TOKENS], d_gate), mm(gated_b[middle:], cot)],
         [mm(normed_a[:middle, :TOKENS], d_gate), mm(gated_b[:middle], cot)],
         [order_a, order_b],
     )
+
+    dy_pairs = by_pair(dy_low.astype(BF16))
+    du_chunk = from_pairs(product("kpjts,kpjtc->kpsc", mixes, one_head(dy_pairs)))
+    both = product("kptc,kpjsc->kpjts", dy_pairs, u_pairs)
+    d_scores = jnp.sum(decay * both, axis=(1, 2)).astype(BF16)
+    db_chunk = product("kts,ktn->ksn", d_scores, c_low)
+    dc_chunk = product("kts,ksn->ktn", d_scores, b_low)
+
+    part_out = mm(gated_low, w_out)
+    kept, other = own_rows(part_out)
+    own_out = own_in.astype(F32) + (kept + swap_cores(other))
+    block_out = to_owner(own_out.astype(BF16))
+
+    leaving, du_chunk, db_chunk, dc_chunk = wait([first], leaving, du_chunk, db_chunk, dc_chunk)
 
     ends = jnp.stack([between(k + 1, CHUNKS) * leaving + back[k] for k in range(CHUNKS)])
     du = du_chunk + flat(jnp.einsum("ktn,krn->ktr", b_proj, ends, precision=PRECISE)) * to_end_wide
     d_b = flat(db_chunk + jnp.einsum("ktr,krn->ktn", chunked(u_wide), ends, precision=PRECISE))
     d_c = flat(dc_chunk + jnp.einsum("ktr,krn->ktn", dy_start, starts, precision=PRECISE))
+    du, d_b, d_c = wait([first], du, d_b, d_c)
     d_bc = jnp.concatenate([d_b, d_c], axis=1)
     nexts = jnp.concatenate([starts[1:], state_end[None]], axis=0)
     carries = exact(jnp.sum(ends * nexts, axis=2), spread, NT)
@@ -456,6 +492,7 @@
     d_x = exact(dt, spread) * du + skip_wide * dy
     d_act = jnp.concatenate([d_x, d_bc], axis=1)
     d_pre = d_act * (gate_of_act * (1.0 + preact * (1.0 - gate_of_act)))
+    (d_pre,) = wait([first], d_pre)
     d_ext = sum(
         conv_weights[k] * jnp.pad(d_pre, ((5 + k, 3 - k), (0, 0))) for k in range(KERNEL)
     )
@@ -467,6 +504,7 @@
     d_crit = jnp.concatenate(
         [d_ext, jnp.pad(d_dt_raw, ((0, HALO), (0, 0)))], axis=1
     ).astype(BF16)
+    (d_crit,) = wait([first], d_crit)
 
     y_of, x_of, z_of = block_order(order_b)
     row_at = rows_of((y_of * 4 + x_of) * 4 + z_of)[:, None]
@@ -492,7 +530,7 @@
         with_riders = jnp.pad(riders[rows], ((0, 0), (CRIT - PART - LANES, 0)))
         return mm(normed_b[rows], crit_b) + with_riders
 
-    rows_a, rows_b = reduce_scatter(
+    second = Halving(
         [mm(normed_a[middle:], d_crit[:, :PART]), part_b(slice(middle, None))],
         [mm(normed_a[:middle], d_crit[:, :PART]), part_b(slice(0, middle))],
         [order_a, order_b],
@@ -515,6 +553,13 @@
         own * d_own, axis=1, keepdims=True
     )
     input_grad = to_owner(own_cot.astype(F32) + d_tokens)
+
+    wait([second, first])
+    wait([second, first])
+    for _ in range(4):
+        wait([second])
+    rows_a, rows_b = second.totals
+    gate_rows, out_rows_grad = first.totals
 
     rows = jnp.concatenate([rows_a, rows_b, gate_rows], axis=1)
     mine = jnp.where(first_core, rows[:12], rows[12:])

time: 580 us -> 604 us (1.041); the launches traced: 572 us -> 604 us
  blocking collectives: 54.4 us -> 0 us
  starting transfers between devices: 82.8 us -> 137 us
  matrix products: 134 us -> 145 us
  local copies, waits for them, and re-layouts: 85.8 us -> 95.1 us
  waiting for transfers between devices: 118 us -> 127 us
    all_gather x1 -> x0, blocking collectives: 54.4 us -> none  [on_device(): small_all = lax.all_gather(small, ALL, axis=0, tiled=False)]
    all_gather x1 -> x2, waiting for transfers between devices: 17.5 us -> 64.1 us  [the longest x1 64.1 us: on_device(): w_crit = lax.all_gather(in_rows_low[:, :CRIT], CHIPS, axis=0, tiled=True)]
    ppermute x30, waiting for transfers between devices: 79.4 us -> 42.6 us  [exchange(): return lax.ppermute(value, axes, pairs)]
    ppermute x7, starting transfers between devices: 8.4 us -> 35.4 us  [swap_cores(): return lax.ppermute(value, 'c', [(0, 1), (1, 0)])]
    ppermute x30, starting transfers between devices: 32.9 us -> 54.2 us  [exchange(): return lax.ppermute(value, axes, pairs)]
    add x21 -> x31, other arithmetic: 2.34 us -> 16.3 us  [the longest x24 10.2 us: add(): keep + got.astype(F32)]
    add x1, other arithmetic: 10.2 us -> 1.04 us  [on_device(): d_x = exact(dt, spread) * du + skip_wide * dy]
    unnamed x333 -> x358, local copies, waits for them, and re-layouts: 9.43 us -> 18.5 us
  transfers between devices with their start and end apart: 57 -> 58, of which waited for: 25 -> 22; matrix products, arithmetic and copies ran while one was open for 32% -> 39% of each run, Pallas kernels for 0% -> 0%
where the time goes in v2:
time: 604 us
  matrix products  145 us (24%)
  starting transfers between devices  137 us (23%)
  waiting for transfers between devices  127 us (21%)
  local copies, waits for them, and re-layouts  95.1 us (16%)
  other arithmetic  83.5 us (14%)
  between operations  17.3 us (3%)
    dot_general x22, matrix products, mm(): lax.dot_general(a.astype(BF16), b.astype(BF16), (dims, ((), ())), preferr...  86 us
    all_gather x1, waiting for transfers between devices, on_device(): w_crit = lax.all_gather(in_rows_low[:, :CRIT], CHIPS, axis=0, tiled=True)  64.1 us
    ppermute x30, starting transfers between devices, exchange(): return lax.ppermute(value, axes, pairs)  54.2 us
    ppermute x30, waiting for transfers between devices, exchange(): return lax.ppermute(value, axes, pairs)  42.6 us
    ppermute x7, starting transfers between devices, swap_cores(): return lax.ppermute(value, 'c', [(0, 1), (1, 0)])  35.4 us
    dot_general x9, matrix products, exact(): lax.dot_general(a, b, (dims, ((), ())), precision=PRECISE, preferred_elem...  20.9 us
    ppermute x8, starting transfers between devices, along_y(): lax.ppermute(value, 'y', [(y, y + steps) for y in range(4) if 0 <= y + st...  19.3 us
    unnamed x358, local copies, waits for them, and re-layouts  18.5 us
  transfers between devices with their start and end apart: 58, of which 22 were waited for; matrix products, arithmetic and copies ran while one was open for 39% of the time, Pallas kernels for 0%

profile of v2, /device:TPU:7, one launch (start us, length us, event | category | flops | bytes accessed | tf_op | source)
XLA Modules:
  0.0 604.1 jit_solution(11351761221940262640)
XLA Ops:
  15.1 5.1 collective-permute-start.3
  22.9 64.1 %all-gather.3.cloned.1.call-done = bf16[1536,1920]{1,0:T(8,128)(2,1)} async-done(((bf16[24,1920]{1,0:T(8,128)(2,1)}), bf16[1536,1920]{1,0:T(8,128)(2,1)}) %all-gather.3.cloned.1.call-update) | async-done | bytes 5898256 | tf_op jit(solution)/shard_map/all_gather | solution.py:319
  97.8 9.5 %collective-permute-done.1 = bf16[2,128,1536]{2,1,0:T(8,128)(2,1)S(1)} collective-permute-done((bf16[2,128,1536]{2,1,0:T(8,128)(2,1)S(1)}, bf16[2,128,1536]{2,1,0:T(8,128)(2,1)S(1)}, u32[]{:S(2)}, u32[]{:S(2)}) %collective-permute-start.1) | collective-permute-done | bytes 786464 | tf_op jit(solution)/shard_map/ppermute | solution.py:97
  107.9 6.0 collective-permute-start.4
  127.4 6.4 %fusion.287 = f32[528,1920]{1,0:T(8,128)S(1)} fusion(bf16[528,1536]{1,0:T(8,128)(2,1)S(1)} %fusion.27, bf16[1536,1920]{1,0:T(8,128)(2,1)} %all-gather.3.cloned.1.call-done), kind=kOutput, calls=%fused_computation.555 | convolution fusion | flops 3114270720 | bytes 11575296 | tf_op jit(solution)/shard_map/dot_general | solution.py:47
  143.8 8.6 %fusion.24 = (f32[512,1792]{1,0:T(8,128)S(1)}, f32[512,1792]{1,0:T(8,128)}) fusion(f32[512,1792]{1,0:T(8,128)} %slice.812, f32[1792]{0:T(1024)S(1)} %get-tuple-element.145, f32[8,1792]{1,0:T(8,128)S(1)} %slice.811, f32[1792]{0:T(1024)S(1)} %get-tuple-element.146, f32[1792]{0:T(1024)S(1)} %get-tuple-element.147, f32[1792]{0:T(1024)S(1)} %get-tuple-element.148, ...), kind=kLoop, calls=%fused_computation.52 | loop fusion | flops 13762560 | bytes 11103232 | tf_op jit(solution)/shard_map/mul | solution.py:367
  154.3 5.0 reduce-precision_convert_fusion.1
  164.1 5.7 collective-permute-start.8
  197.3 5.3 fusion.56
  215.1 5.7 copy.92
  230.1 4.4 add_bitcast_fusion
  253.8 10.7 %multiply_reduce_fusion.7 = (f32[512]{0:T(512)S(1)}, f32[512]{0:T(512)S(1)}, f32[512,1536]{1,0:T(8,128)}, f32[512,1536]{1,0:T(8,128)}, f32[512,1536]{1,0:T(8,128)}) fusion(f32[1536]{0:T(1024)S(1)} %copy-done.112, f32[512,1536]{1,0:T(8,128)} %fusion.19, f32[512,1792]{1,0:T(8,128)S(1)} %copy-done.1, f32[1536]{0:T(1024)S(1)} %copy-done.99, ...), kind=kOutput, calls=%fused_computation.86 | convolution fusion | flops 2426928128 | bytes 31477760 | tf_op jit(solution)/shard_map/dot_general | solution.py:47
  267.5 7.8 %multiply_reduce_fusion.4 = (f32[1536]{0:T(1024)}, f32[512,1536]{1,0:T(8,128)S(1)}, bf16[512,1536]{1,0:T(8,128)(2,1)}, bf16[1536]{0:T(1024)(128)(2,1)}) fusion(f32[512,1792]{1,0:T(8,128)S(1)} %copy-done.1, f32[512,1536]{1,0:T(8,128)} %fusion.19, f32[512]{0:T(512)S(1)} %bitcast.376, f32[512,1536]{1,0:T(8,128)} %get-tuple-element.171, f32[512]{0:T(512)S(1)} %bitcast.375, ...), kind=kLoop, calls=%fused_computation.70 | loop fusion | flops 18871296 | bytes 20474880 | tf_op jit(solution)/shard_map/reduce_sum | solution.py:489
  280.1 4.3 fusion.290
  316.5 5.4 fusion.53
  327.1 6.3 %collective-permute-start.13 = (bf16[768,1536]{1,0:T(8,128)(2,1)}, bf16[768,1536]{1,0:T(8,128)(2,1)}, u32[]{:S(2)}, u32[]{:S(2)}) collective-permute-start(bf16[768,1536]{1,0:T(8,128)(2,1)} %convolution_convert_fusion.1), channel_id=1, source_target_pairs={{0,32},{1,97},{32,0},{33,65},{64,96},{65,33},{96,64},{97,1},{2,34}... | collective-permute-start | bytes 7077896 | tf_op jit(solution)/shard_map/ppermute | solution.py:123
  334.2 4.9 copy.79
  343.1 4.7 fusion.112
  352.4 7.5 %collective-permute-done.13 = bf16[768,1536]{1,0:T(8,128)(2,1)} collective-permute-done((bf16[768,1536]{1,0:T(8,128)(2,1)}, bf16[768,1536]{1,0:T(8,128)(2,1)}, u32[]{:S(2)}, u32[]{:S(2)}) %collective-permute-start.13) | collective-permute-done | bytes 2359328 | tf_op jit(solution)/shard_map/ppermute | solution.py:123
  382.1 11.6 %collective-permute-start.19 = (bf16[384,1536]{1,0:T(8,128)(2,1)}, bf16[384,1536]{1,0:T(8,128)(2,1)S(1)}, u32[]{:S(2)}, u32[]{:S(2)}) collective-permute-start(bf16[384,1536]{1,0:T(8,128)(2,1)} %slice.1216), channel_id=1, source_target_pairs={{0,24},{1,9},{8,16},{9,1},{16,8},{17,25},{24,0},{25,17},{2,26},{3,... | collective-permute-start | bytes 3538952 | tf_op jit(solution)/shard_map/ppermute | solution.py:123
  400.6 8.6 %collective-permute-done.19 = bf16[384,1536]{1,0:T(8,128)(2,1)S(1)} collective-permute-done((bf16[384,1536]{1,0:T(8,128)(2,1)}, bf16[384,1536]{1,0:T(8,128)(2,1)S(1)}, u32[]{:S(2)}, u32[]{:S(2)}) %collective-permute-start.19) | collective-permute-done | bytes 1179680 | tf_op jit(solution)/shard_map/ppermute | solution.py:123
  437.6 5.0 collective-permute-start.55
  452.9 6.9 %select_convert_fusion = bf16[1536,3328]{1,0:T(8,128)(2,1)S(1)} fusion(s32[1536]{0:T(1024)S(1)} %copy-done.115, s32[3328]{0:T(1024)S(1)} %copy-done.104, s32[3328]{0:T(1024)S(1)} %copy-done.105, pred[3328]{0:T(1024)(128)(4,1)S(1)} %copy-done.137, s32[1536]{0:T(1024)S(1)} %copy-done.116, f32[8,256]{1,0:T(8,128)S(1)} %slice-done.20, ...), kind=kOutput, calls=%fused_computation | convolution fusion | flops 265852928 | bytes 10372352 | tf_op jit(solution)/shard_map/dot_general | solution.py:53
  466.8 8.1 %fusion.291 = f32[528,1536]{1,0:T(8,128)} fusion(bf16[528,1920]{1,0:T(8,128)(2,1)S(1)} %fusion.50, bf16[1536,1920]{1,0:T(8,128)(2,1)} %all-gather.3.cloned.1.call-done), kind=kOutput, calls=%fused_computation.559 | convolution fusion | flops 3114270720 | bytes 11169792 | tf_op jit(solution)/shard_map/dot_general | solution.py:47
  488.9 4.5 slice_add_fusion
  513.3 5.9 collective-permute-done.33
  520.0 5.1 collective-permute-start.36
  533.0 8.3 %collective-permute-done.36 = bf16[192,1024]{1,0:T(8,128)(2,1)S(1)} collective-permute-done((bf16[192,1024]{1,0:T(8,128)(2,1)S(1)}, bf16[192,1024]{1,0:T(8,128)(2,1)S(1)}, u32[]{:S(2)}, u32[]{:S(2)}) %collective-permute-start.36) | collective-permute-done | bytes 393248 | tf_op jit(solution)/shard_map/ppermute | solution.py:123
  541.8 9.6 %collective-permute-start.45 = (f32[24,1536]{1,0:T(8,128)S(1)}, f32[24,1536]{1,0:T(8,128)S(1)}, u32[]{:S(2)}, u32[]{:S(2)}) collective-permute-start(f32[24,1536]{1,0:T(8,128)S(1)} %convert_add_fusion.21), channel_id=1, source_target_pairs={{0,0},{1,64},{32,32},{33,96},{64,1},{65,65},{96,33},{97,97},{2,2},... | collective-permute-start | bytes 442376 | tf_op jit(solution)/shard_map/ppermute | solution.py:106
  561.5 14.5 %collective-permute-start.44 = (f32[12,3456]{1,0:T(8,128)S(1)}, f32[12,3456]{1,0:T(8,128)S(1)}, u32[]{:S(2)}, u32[]{:S(2)}) collective-permute-start(f32[12,3456]{1,0:T(8,128)S(1)} %slice_select_fusion.4), channel_id=1, source_target_pairs={{0,1},{1,0},{2,3},{3,2},{4,5},{5,4},{6,7},{7,6},{8,9},{9,8},{10,11... | collective-permute-start | bytes 497672 | tf_op jit(solution)/shard_map/ppermute | solution.py:90
  580.7 6.5 %collective-permute-start.47 = (f32[12]{0:T(128)S(1)}, f32[12]{0:T(128)S(1)}, u32[]{:S(2)}, u32[]{:S(2)}) collective-permute-start(f32[12]{0:T(128)S(1)} %bitcast_divide_fusion), channel_id=1, source_target_pairs={{1,0},{4,1},{7,2},{10,3},{13,4},{16,5},{19,6},{22,7},{25,8},{28,9}... | collective-permute-start | bytes 152 | tf_op jit(solution)/shard_map/ppermute | solution.py:590
  591.9 4.5 collective-permute-done.46
  (764 shorter events, 310.1 us)
Async XLA Ops:
  7.2 79.8 %all-gather.3.cloned.1.call-start = ((), (), s32[]{:S(2)}) async-start(), calls=%async_computation | async-start | bytes 5990400 | tf_op jit(solution)/shard_map/all_gather | solution.py:319
  14.1 227.3 %all-gather.5.cloned.1.call-start = ((), (), s32[]{:S(2)}) async-start(), calls=%async_computation.1 | async-start | bytes 9584640 | tf_op jit(solution)/shard_map/all_gather | solution.py:322
  88.1 19.2 %collective-permute-start.1 = (bf16[2,128,1536]{2,1,0:T(8,128)(2,1)S(1)}, bf16[2,128,1536]{2,1,0:T(8,128)(2,1)S(1)}, u32[]{:S(2)}, u32[]{:S(2)}) collective-permute-start(bf16[2,128,1536]{2,1,0:T(8,128)(2,1)S(1)} %get-tuple-element.194), channel_id=1, source_target_pairs={{0,8},{1,24},{8,0},{9,16},{16,9},{17,25},{24,1},{25,17},{2,10},{3,... | collective-permute-start | bytes 2359304 | tf_op jit(solution)/shard_map/ppermute | solution.py:97
  164.1 66.0 %collective-permute-start.8 = (f32[1544,128]{1,0:T(8,128)}, f32[1544,128]{1,0:T(8,128)}, u32[]{:S(2)}, u32[]{:S(2)}) collective-permute-start(f32[1544,128]{1,0:T(8,128)} %pad_maximum_fusion.8), channel_id=1, source_target_pairs={{0,96},{1,97},{2,98},{3,99},{4,100},{5,101},{6,102},{7,103},{8,104... | collective-permute-start | bytes 2371592 | tf_op jit(solution)/shard_map/ppermute | solution.py:110
  169.8 54.8 %collective-permute-start.7 = (f32[1544,128]{1,0:T(8,128)}, f32[1544,128]{1,0:T(8,128)}, u32[]{:S(2)}, u32[]{:S(2)}) collective-permute-start(f32[1544,128]{1,0:T(8,128)} %pad_maximum_fusion.8), channel_id=1, source_target_pairs={{0,64},{32,96},{1,65},{33,97},{2,66},{34,98},{3,67},{35,99},{4,68}... | collective-permute-start | bytes 2371592 | tf_op jit(solution)/shard_map/ppermute | solution.py:110
  171.9 55.4 %collective-permute-start.6 = (f32[1544,128]{1,0:T(8,128)}, f32[1544,128]{1,0:T(8,128)}, u32[]{:S(2)}, u32[]{:S(2)}) collective-permute-start(f32[1544,128]{1,0:T(8,128)} %pad_maximum_fusion.8), channel_id=1, source_target_pairs={{0,32},{32,64},{64,96},{1,33},{33,65},{65,97},{2,34},{34,66},{66,9... | collective-permute-start | bytes 2371592 | tf_op jit(solution)/shard_map/ppermute | solution.py:110
  298.3 52.3 %collective-permute-start.17 = (bf16[1552,128]{1,0:T(8,128)(2,1)}, bf16[1552,128]{1,0:T(8,128)(2,1)}, u32[]{:S(2)}, u32[]{:S(2)}) collective-permute-start(bf16[1552,128]{1,0:T(8,128)(2,1)} %pad_maximum_fusion.11), channel_id=1, source_target_pairs={{96,0},{97,1},{98,2},{99,3},{100,4},{101,5},{102,6},{103,7},{104,8... | collective-permute-start | bytes 1191944 | tf_op jit(solution)/shard_map/ppermute | solution.py:110
  299.9 47.9 %collective-permute-start.16 = (bf16[1552,128]{1,0:T(8,128)(2,1)}, bf16[1552,128]{1,0:T(8,128)(2,1)}, u32[]{:S(2)}, u32[]{:S(2)}) collective-permute-start(bf16[1552,128]{1,0:T(8,128)(2,1)} %pad_maximum_fusion.11), channel_id=1, source_target_pairs={{64,0},{96,32},{65,1},{97,33},{66,2},{98,34},{67,3},{99,35},{68,4}... | collective-permute-start | bytes 1191944 | tf_op jit(solution)/shard_map/ppermute | solution.py:110
  301.2 48.1 %collective-permute-start.15 = (bf16[1552,128]{1,0:T(8,128)(2,1)}, bf16[1552,128]{1,0:T(8,128)(2,1)}, u32[]{:S(2)}, u32[]{:S(2)}) collective-permute-start(bf16[1552,128]{1,0:T(8,128)(2,1)} %pad_maximum_fusion.11), channel_id=1, source_target_pairs={{32,0},{64,32},{96,64},{33,1},{65,33},{97,65},{34,2},{66,34},{98,6... | collective-permute-start | bytes 1191944 | tf_op jit(solution)/shard_map/ppermute | solution.py:110
  321.9 30.6 %collective-permute-start.14 = (bf16[768,1536]{1,0:T(8,128)(2,1)}, bf16[768,1536]{1,0:T(8,128)(2,1)}, u32[]{:S(2)}, u32[]{:S(2)}) collective-permute-start(bf16[768,1536]{1,0:T(8,128)(2,1)} %convolution_convert_fusion), channel_id=1, source_target_pairs={{0,8},{1,25},{8,0},{9,17},{16,24},{17,9},{24,16},{25,1},{2,10},{3,... | collective-permute-start | bytes 7077896 | tf_op jit(solution)/shard_map/ppermute | solution.py:123
  327.1 32.9 %collective-permute-start.13 = (bf16[768,1536]{1,0:T(8,128)(2,1)}, bf16[768,1536]{1,0:T(8,128)(2,1)}, u32[]{:S(2)}, u32[]{:S(2)}) collective-permute-start(bf16[768,1536]{1,0:T(8,128)(2,1)} %convolution_convert_fusion.1), channel_id=1, source_target_pairs={{0,32},{1,97},{32,0},{33,65},{64,96},{65,33},{96,64},{97,1},{2,34}... | collective-permute-start | bytes 7077896 | tf_op jit(solution)/shard_map/ppermute | solution.py:123
  378.5 22.1 %collective-permute-start.18 = (bf16[384,1536]{1,0:T(8,128)(2,1)}, bf16[384,1536]{1,0:T(8,128)(2,1)}, u32[]{:S(2)}, u32[]{:S(2)}) collective-permute-start(bf16[384,1536]{1,0:T(8,128)(2,1)} %slice.1217), channel_id=1, source_target_pairs={{0,96},{1,33},{32,64},{33,1},{64,32},{65,97},{96,0},{97,65},{2,98}... | collective-permute-start | bytes 3538952 | tf_op jit(solution)/shard_map/ppermute | solution.py:123
  382.1 27.1 %collective-permute-start.19 = (bf16[384,1536]{1,0:T(8,128)(2,1)}, bf16[384,1536]{1,0:T(8,128)(2,1)S(1)}, u32[]{:S(2)}, u32[]{:S(2)}) collective-permute-start(bf16[384,1536]{1,0:T(8,128)(2,1)} %slice.1216), channel_id=1, source_target_pairs={{0,24},{1,9},{8,16},{9,1},{16,8},{17,25},{24,0},{25,17},{2,26},{3,... | collective-permute-start | bytes 3538952 | tf_op jit(solution)/shard_map/ppermute | solution.py:123
  424.0 86.9 %collective-permute-start.10 = (f32[256,1536]{1,0:T(8,128)S(1)}, f32[256,1536]{1,0:T(8,128)S(1)}, u32[]{:S(2)}, u32[]{:S(2)}) collective-permute-start(f32[256,1536]{1,0:T(8,128)S(1)} %slice_select_fusion.1), channel_id=1, source_target_pairs={{0,1},{1,0},{2,3},{3,2},{4,5},{5,4},{6,7},{7,6},{8,9},{9,8},{10,11... | collective-permute-start | bytes 4718600 | tf_op jit(solution)/shard_map/ppermute | solution.py:90
  432.7 12.8 %collective-permute-start.20 = (bf16[192,1536]{1,0:T(8,128)(2,1)S(1)}, bf16[192,1536]{1,0:T(8,128)(2,1)S(1)}, u32[]{:S(2)}, u32[]{:S(2)}) collective-permute-start(bf16[192,1536]{1,0:T(8,128)(2,1)S(1)} %slice.1221), channel_id=1, source_target_pairs={{0,8},{1,25},{8,0},{9,17},{16,24},{17,9},{24,16},{25,1},{2,10},{3,... | collective-permute-start | bytes 1769480 | tf_op jit(solution)/shard_map/ppermute | solution.py:123
  450.7 15.0 %collective-permute-start.22 = (bf16[96,1536]{1,0:T(8,128)(2,1)S(1)}, bf16[96,1536]{1,0:T(8,128)(2,1)S(1)}, u32[]{:S(2)}, u32[]{:S(2)}) collective-permute-start(bf16[96,1536]{1,0:T(8,128)(2,1)S(1)} %slice.1225), channel_id=1, source_target_pairs={{0,24},{1,9},{8,16},{9,1},{16,8},{17,25},{24,0},{25,17},{2,26},{3,... | collective-permute-start | bytes 884744 | tf_op jit(solution)/shard_map/ppermute | solution.py:123
  452.0 13.7 %collective-permute-start.23 = (bf16[96,1536]{1,0:T(8,128)(2,1)S(1)}, bf16[96,1536]{1,0:T(8,128)(2,1)S(1)}, u32[]{:S(2)}, u32[]{:S(2)}) collective-permute-start(bf16[96,1536]{1,0:T(8,128)(2,1)S(1)} %slice.1224), channel_id=1, source_target_pairs={{0,96},{1,33},{32,64},{33,1},{64,32},{65,97},{96,0},{97,65},{2,98}... | collective-permute-start | bytes 884744 | tf_op jit(solution)/shard_map/ppermute | solution.py:123
  479.2 17.0 %collective-permute-start.24 = (f32[16,1536]{1,0:T(8,128)S(1)}, f32[16,1536]{1,0:T(8,128)S(1)}, u32[]{:S(2)}, u32[]{:S(2)}) collective-permute-start(f32[16,1536]{1,0:T(8,128)S(1)} %slice.878), channel_id=1, source_target_pairs={{32,0},{64,32},{96,64},{33,1},{65,33},{97,65},{34,2},{66,34},{98,6... | collective-permute-start | bytes 294920 | tf_op jit(solution)/shard_map/ppermute | solution.py:110
  480.7 17.0 %collective-permute-start.30 = (bf16[48,1536]{1,0:T(8,128)(2,1)S(1)}, bf16[48,1536]{1,0:T(8,128)(2,1)S(1)}, u32[]{:S(2)}, u32[]{:S(2)}) collective-permute-start(bf16[48,1536]{1,0:T(8,128)(2,1)S(1)} %slice.1229), channel_id=1, source_target_pairs={{0,2},{1,7},{2,0},{3,5},{4,6},{5,3},{6,4},{7,1},{8,10},{9,15},{10,... | collective-permute-start | bytes 442376 | tf_op jit(solution)/shard_map/ppermute | solution.py:123
  482.1 22.5 %collective-permute-start.28 = (bf16[768,1024]{1,0:T(8,128)(2,1)S(1)}, bf16[768,1024]{1,0:T(8,128)(2,1)S(1)}, u32[]{:S(2)}, u32[]{:S(2)}) collective-permute-start(bf16[768,1024]{1,0:T(8,128)(2,1)S(1)} %convolution_convert_fusion.2), channel_id=1, source_target_pairs={{0,32},{1,97},{32,0},{33,65},{64,96},{65,33},{96,64},{97,1},{2,34}... | collective-permute-start | bytes 4718600 | tf_op jit(solution)/shard_map/ppermute | solution.py:123
  486.1 18.5 %collective-permute-start.29 = (bf16[768,896]{1,0:T(8,128)(2,1)S(1)}, bf16[768,896]{1,0:T(8,128)(2,1)S(1)}, u32[]{:S(2)}, u32[]{:S(2)}) collective-permute-start(bf16[768,896]{1,0:T(8,128)(2,1)S(1)} %add_convert_fusion.1), channel_id=1, source_target_pairs={{0,8},{1,25},{8,0},{9,17},{16,24},{17,9},{24,16},{25,1},{2,10},{3,... | collective-permute-start | bytes 4128776 | tf_op jit(solution)/shard_map/ppermute | solution.py:123
  497.7 11.7 %collective-permute-start.25 = (f32[256,1536]{1,0:T(8,128)S(1)}, f32[256,1536]{1,0:T(8,128)S(1)}, u32[]{:S(2)}, u32[]{:S(2)}) collective-permute-start(f32[256,1536]{1,0:T(8,128)S(1)} %slice_select_fusion), channel_id=1, source_target_pairs={{0,1},{1,0},{2,3},{3,2},{4,5},{5,4},{6,7},{7,6},{8,9},{9,8},{10,11... | collective-permute-start | bytes 4718600 | tf_op jit(solution)/shard_map/ppermute | solution.py:90
  508.8 10.8 %collective-permute-start.32 = (bf16[384,1024]{1,0:T(8,128)(2,1)S(1)}, bf16[384,1024]{1,0:T(8,128)(2,1)S(1)}, u32[]{:S(2)}, u32[]{:S(2)}) collective-permute-start(bf16[384,1024]{1,0:T(8,128)(2,1)S(1)} %slice.1218), channel_id=1, source_target_pairs={{0,96},{1,33},{32,64},{33,1},{64,32},{65,97},{96,0},{97,65},{2,98}... | collective-permute-start | bytes 2359304 | tf_op jit(solution)/shard_map/ppermute | solution.py:123
  511.7 16.3 %collective-permute-start.11 = (bf16[128,1536]{1,0:T(8,128)(2,1)S(1)}, bf16[128,1536]{1,0:T(8,128)(2,1)S(1)}, u32[]{:S(2)}, u32[]{:S(2)}) collective-permute-start(bf16[128,1536]{1,0:T(8,128)(2,1)S(1)} %get-tuple-element.198), channel_id=1, source_target_pairs={{0,0},{1,16},{8,8},{9,24},{16,1},{17,17},{24,9},{25,25},{2,2},{3,1... | collective-permute-start | bytes 1179656 | tf_op jit(solution)/shard_map/ppermute | solution.py:97
  512.5 15.8 %collective-permute-start.12 = (bf16[128,1536]{1,0:T(8,128)(2,1)S(1)}, bf16[128,1536]{1,0:T(8,128)(2,1)S(1)}, u32[]{:S(2)}, u32[]{:S(2)}) collective-permute-start(bf16[128,1536]{1,0:T(8,128)(2,1)S(1)} %get-tuple-element.199), channel_id=1, source_target_pairs={{0,8},{1,24},{8,0},{9,16},{16,9},{17,25},{24,1},{25,17},{2,10},{3,... | collective-permute-start | bytes 1179656 | tf_op jit(solution)/shard_map/ppermute | solution.py:97
  520.0 21.3 %collective-permute-start.36 = (bf16[192,1024]{1,0:T(8,128)(2,1)S(1)}, bf16[192,1024]{1,0:T(8,128)(2,1)S(1)}, u32[]{:S(2)}, u32[]{:S(2)}) collective-permute-start(bf16[192,1024]{1,0:T(8,128)(2,1)S(1)} %slice.1222), channel_id=1, source_target_pairs={{0,8},{1,25},{8,0},{9,17},{16,24},{17,9},{24,16},{25,1},{2,10},{3,... | collective-permute-start | bytes 1179656 | tf_op jit(solution)/shard_map/ppermute | solution.py:123
  527.3 32.0 %collective-permute-start.26 = (f32[128,1536]{1,0:T(8,128)S(1)}, f32[128,1536]{1,0:T(8,128)S(1)}, u32[]{:S(2)}, u32[]{:S(2)}) collective-permute-start(f32[128,1536]{1,0:T(8,128)S(1)} %get-tuple-element.189), channel_id=1, source_target_pairs={{0,0},{1,16},{8,8},{9,24},{16,1},{17,17},{24,9},{25,25},{2,2},{3,1... | collective-permute-start | bytes 2359304 | tf_op jit(solution)/shard_map/ppermute | solution.py:97
  528.0 31.2 %collective-permute-start.27 = (f32[128,1536]{1,0:T(8,128)S(1)}, f32[128,1536]{1,0:T(8,128)S(1)}, u32[]{:S(2)}, u32[]{:S(2)}) collective-permute-start(f32[128,1536]{1,0:T(8,128)S(1)} %get-tuple-element.190), channel_id=1, source_target_pairs={{0,8},{1,24},{8,0},{9,16},{16,9},{17,25},{24,1},{25,17},{2,10},{3,... | collective-permute-start | bytes 2359304 | tf_op jit(solution)/shard_map/ppermute | solution.py:97
  541.8 34.2 %collective-permute-start.45 = (f32[24,1536]{1,0:T(8,128)S(1)}, f32[24,1536]{1,0:T(8,128)S(1)}, u32[]{:S(2)}, u32[]{:S(2)}) collective-permute-start(f32[24,1536]{1,0:T(8,128)S(1)} %convert_add_fusion.21), channel_id=1, source_target_pairs={{0,0},{1,64},{32,32},{33,96},{64,1},{65,65},{96,33},{97,97},{2,2},... | collective-permute-start | bytes 442376 | tf_op jit(solution)/shard_map/ppermute | solution.py:106
  561.5 15.6 %collective-permute-start.44 = (f32[12,3456]{1,0:T(8,128)S(1)}, f32[12,3456]{1,0:T(8,128)S(1)}, u32[]{:S(2)}, u32[]{:S(2)}) collective-permute-start(f32[12,3456]{1,0:T(8,128)S(1)} %slice_select_fusion.4), channel_id=1, source_target_pairs={{0,1},{1,0},{2,3},{3,2},{4,5},{5,4},{6,7},{7,6},{8,9},{9,8},{10,11... | collective-permute-start | bytes 497672 | tf_op jit(solution)/shard_map/ppermute | solution.py:90
  579.5 10.6 %collective-permute-start.48 = (f32[12]{0:T(128)S(1)}, f32[12]{0:T(128)S(1)}, u32[]{:S(2)}, u32[]{:S(2)}) collective-permute-start(f32[12]{0:T(128)S(1)} %bitcast_divide_fusion), channel_id=1, source_target_pairs={{2,0},{5,1},{8,2},{11,3},{14,4},{17,5},{20,6},{23,7},{26,8},{29,9}... | collective-permute-start | bytes 152 | tf_op jit(solution)/shard_map/ppermute | solution.py:590
  580.7 11.2 %collective-permute-start.47 = (f32[12]{0:T(128)S(1)}, f32[12]{0:T(128)S(1)}, u32[]{:S(2)}, u32[]{:S(2)}) collective-permute-start(f32[12]{0:T(128)S(1)} %bitcast_divide_fusion), channel_id=1, source_target_pairs={{1,0},{4,1},{7,2},{10,3},{13,4},{16,5},{19,6},{22,7},{25,8},{28,9}... | collective-permute-start | bytes 152 | tf_op jit(solution)/shard_map/ppermute | solution.py:590
  (218 other events, 1674.4 us)
Sparse Core Ops, SparseCore 0:
  14.2 72.7 all-gather.2
  90.4 82.9 all-gather.4

commit v3 on v2

--- a/solution.py
+++ b/solution.py
@@ -61,10 +61,6 @@
     return lax.reduce_precision(v, 8, 7)
 
 
-def hold(*values):
-    return lax.optimization_barrier(values)
-
-
 def iota(shape, dim):
     return lax.broadcasted_iota(jnp.int32, shape, dim)
 
@@ -253,13 +249,6 @@
 
 def flat(value):
     return value.reshape(TOKENS, value.shape[-1])
-
-
-def sum_all_chips(value):
-    for axis in CHIPS:
-        for turn in range(2):
-            value = value + exchange(value, axis, turn)
-    return value
 
 
 def on_device(
@@ -318,7 +307,6 @@
     out_rows_low = cross_halves(out_master).astype(BF16)
     w_crit = lax.all_gather(in_rows_low[:, :CRIT], CHIPS, axis=0, tiled=True)
     rest_low = jnp.concatenate([in_rows_low[:, CRIT:], out_rows_low], axis=1)
-    rest_low, w_crit = hold(rest_low, w_crit)
     w_rest = lax.all_gather(rest_low, CHIPS, axis=0, tiled=True)
     w_gate = w_rest[:, :HALF]
     w_out = (
@@ -443,17 +431,17 @@
         back0, back1 = regroup(sent[0], 0), regroup(sent[1], 1)
         return jnp.where(even_x, jnp.stack([back0, back1]), jnp.stack([back1, back0]))
 
-    order_a, order_b = ("y", "x", "z"), ("x", "y", "z")
-    pick_in_a, pick_in_b = pick(in_rows(order_a)), pick(in_rows(order_b))
-    pick_out_b = pick(out_rows(order_b))
-    normed_a = mm(pick_in_a, normed, NT).astype(BF16)
-    normed_b = mm(pick_in_b, normed, NT).astype(BF16)
-    gated_b = mm(pick_out_b, gated_low, NT).astype(BF16)
+    order_gate, order_out = ("x", "z", "y"), ("z", "x", "y")
+    order_a, order_b = ("y", "z", "x"), ("z", "y", "x")
+    normed_gate = mm(pick(in_rows(order_gate)), normed, NT).astype(BF16)
+    normed_a = mm(pick(in_rows(order_a)), normed, NT).astype(BF16)
+    normed_b = mm(pick(in_rows(order_b)), normed, NT).astype(BF16)
+    gated_b = mm(pick(out_rows(order_out)), gated_low, NT).astype(BF16)
     middle = WIDTH // 2
     first = Halving(
-        [mm(normed_a[middle:, :TOKENS], d_gate), mm(gated_b[middle:], cot)],
-        [mm(normed_a[:middle, :TOKENS], d_gate), mm(gated_b[:middle], cot)],
-        [order_a, order_b],
+        [mm(normed_gate[middle:, :TOKENS], d_gate), mm(gated_b[middle:], cot)],
+        [mm(normed_gate[:middle, :TOKENS], d_gate), mm(gated_b[:middle], cot)],
+        [order_gate, order_out],
     )
 
     dy_pairs = by_pair(dy_low.astype(BF16))
@@ -535,8 +523,6 @@
         [mm(normed_a[:middle], d_crit[:, :PART]), part_b(slice(0, middle))],
         [order_a, order_b],
     )
-    head_own = sum_all_chips(jnp.pad(d_head, ((0, 5), (0, 0))))
-    head_other = swap_cores(head_own)
 
     d_normed = mm(d_crit, w_crit, NT)
     d_halo = along_y(d_normed[TOKENS:], -1)
@@ -552,12 +538,14 @@
     d_tokens = own_inv * d_own - (own_inv * own_inv * own_inv) * own * jnp.mean(
         own * d_own, axis=1, keepdims=True
     )
-    input_grad = to_owner(own_cot.astype(F32) + d_tokens)
-
-    wait([second, first])
-    wait([second, first])
-    for _ in range(4):
-        wait([second])
+    input_grad = to_owner((own_cot.astype(F32) + d_tokens).astype(BF16)).astype(F32)
+
+    head_own = jnp.pad(d_head, ((0, 5), (0, 0)))
+    for step in range(6):
+        head_got = exchange(head_own, CHIPS[step // 2], step % 2)
+        head_own, head_got = wait([second, first] if step < 2 else [second], head_own, head_got)
+        head_own = head_own + head_got
+    head_other = swap_cores(head_own)
     rows_a, rows_b = second.totals
     gate_rows, out_rows_grad = first.totals
 

time: 604 us -> 552 us (0.914); the launches traced: 604 us -> 546 us
  starting transfers between devices: 137 us -> 106 us
  waiting for transfers between devices: 127 us -> 99.2 us
    all_gather x1, waiting for transfers between devices: 64.1 us -> 32.8 us  [on_device(): w_crit = lax.all_gather(in_rows_low[:, :CRIT], CHIPS, axis=0, tiled=True)]
    ppermute x7, starting transfers between devices: 35.4 us -> 18.3 us  [swap_cores(): return lax.ppermute(value, 'c', [(0, 1), (1, 0)])]
    ppermute x30, starting transfers between devices: 54.2 us -> 47.1 us  [exchange(): return lax.ppermute(value, axes, pairs)]
    dot_general x22 -> x23, matrix products: 86 us -> 91.1 us  [mm(): lax.dot_general(a.astype(BF16), b.astype(BF16), (dims, ((), ())), preferr...]
    unnamed x358 -> x352, local copies, waits for them, and re-layouts: 18.5 us -> 21.5 us
  transfers between devices with their start and end apart: 58 -> 58, of which waited for: 22 -> 22; matrix products, arithmetic and copies ran while one was open for 39% -> 40% of each run, Pallas kernels for 0% -> 0%
where the time goes in v3:
time: 552 us; the launch traced here: 546 us
  matrix products  149 us (27%)
  starting transfers between devices  106 us (19%)
  waiting for transfers between devices  99.2 us (18%)
  local copies, waits for them, and re-layouts  93.1 us (17%)
  other arithmetic  81.4 us (15%)
  between operations  17.4 us (3%)
    dot_general x23, matrix products, mm(): lax.dot_general(a.astype(BF16), b.astype(BF16), (dims, ((), ())), preferr...  91.1 us
    ppermute x30, starting transfers between devices, exchange(): return lax.ppermute(value, axes, pairs)  47.1 us
    ppermute x30, waiting for transfers between devices, exchange(): return lax.ppermute(value, axes, pairs)  46.2 us
    all_gather x1, waiting for transfers between devices, on_device(): w_crit = lax.all_gather(in_rows_low[:, :CRIT], CHIPS, axis=0, tiled=True)  32.8 us
    unnamed x352, local copies, waits for them, and re-layouts  21.5 us
    dot_general x9, matrix products, exact(): lax.dot_general(a, b, (dims, ((), ())), precision=PRECISE, preferred_elem...  20.4 us
    ppermute x7, starting transfers between devices, swap_cores(): return lax.ppermute(value, 'c', [(0, 1), (1, 0)])  18.3 us
    ppermute x8, starting transfers between devices, along_y(): lax.ppermute(value, 'y', [(y, y + steps) for y in range(4) if 0 <= y + st...  18.3 us
  transfers between devices with their start and end apart: 58, of which 22 were waited for; matrix products, arithmetic and copies ran while one was open for 40% of the time, Pallas kernels for 0%

profile of v3, /device:TPU:7, one launch (start us, length us, event | category | flops | bytes accessed | tf_op | source)
XLA Modules:
  0.0 546.0 jit_solution(9930245548969229707)
XLA Ops:
  15.1 5.1 collective-permute-start.8
  33.8 8.6 %collective-permute-done.1 = bf16[2,128,1536]{2,1,0:T(8,128)(2,1)S(1)} collective-permute-done((bf16[2,128,1536]{2,1,0:T(8,128)(2,1)S(1)}, bf16[2,128,1536]{2,1,0:T(8,128)(2,1)S(1)}, u32[]{:S(2)}, u32[]{:S(2)}) %collective-permute-start.1) | collective-permute-done | bytes 786464 | tf_op jit(solution)/shard_map/ppermute | solution.py:93
  56.3 32.8 %all-gather.3.cloned.1.call-done = bf16[1536,1920]{1,0:T(8,128)(2,1)} async-done(((bf16[24,1920]{1,0:T(8,128)(2,1)}), bf16[1536,1920]{1,0:T(8,128)(2,1)}) %all-gather.3.cloned.1.call-update) | async-done | bytes 5898256 | tf_op jit(solution)/shard_map/all_gather | solution.py:308
  93.3 6.4 %fusion.291 = f32[528,1920]{1,0:T(8,128)S(1)} fusion(bf16[528,1536]{1,0:T(8,128)(2,1)S(1)} %fusion.29, bf16[1536,1920]{1,0:T(8,128)(2,1)} %all-gather.3.cloned.1.call-done), kind=kOutput, calls=%fused_computation.565 | convolution fusion | flops 3114270720 | bytes 11575296 | tf_op jit(solution)/shard_map/dot_general | solution.py:47
  109.8 8.6 %fusion.26 = (f32[512,1792]{1,0:T(8,128)S(1)}, f32[512,1792]{1,0:T(8,128)}) fusion(f32[512,1792]{1,0:T(8,128)} %slice.812, f32[1792]{0:T(1024)S(1)} %get-tuple-element.165, f32[8,1792]{1,0:T(8,128)S(1)} %slice.811, f32[1792]{0:T(1024)S(1)} %get-tuple-element.166, f32[1792]{0:T(1024)S(1)} %get-tuple-element.167, f32[1792]{0:T(1024)S(1)} %get-tuple-element.168, ...), kind=kLoop, calls=%fused_computation.55 | loop fusion | flops 13762560 | bytes 11103232 | tf_op jit(solution)/shard_map/mul | solution.py:355
  120.3 5.0 reduce-precision_convert_fusion.1
  130.0 5.2 collective-permute-start.7
  157.0 4.3 fusion.44
  165.6 4.3 fusion.46
  169.9 5.4 fusion.59
  182.7 5.8 %copy.92 = f32[4,128,12,128]{3,2,1,0:T(8,128)} copy(f32[4,128,12,128]{3,1,2,0:T(8,128)} %fusion.59) | data formatting | bytes 6291456 | tf_op jit(solution)/shard_map/reshape | solution.py:197
  198.1 4.5 add_bitcast_fusion
  216.7 4.3 fusion.21
  221.3 10.7 %multiply_reduce_fusion.7 = (f32[512]{0:T(512)S(1)}, f32[512]{0:T(512)S(1)}, f32[512,1536]{1,0:T(8,128)}, f32[512,1536]{1,0:T(8,128)}, f32[512,1536]{1,0:T(8,128)}) fusion(f32[1536]{0:T(1024)S(1)} %copy-done.112, f32[512,1536]{1,0:T(8,128)} %fusion.21, f32[512,1792]{1,0:T(8,128)S(1)} %copy-done.1, f32[1536]{0:T(1024)S(1)} %copy-done.97, ...), kind=kOutput, calls=%fused_computation.89 | convolution fusion | flops 2426928128 | bytes 31477760 | tf_op jit(solution)/shard_map/dot_general | solution.py:47
  234.6 7.7 %fusion.271 = f32[512,1536]{1,0:T(8,128)} fusion(bf16[1536,1536]{1,0:T(8,128)(2,1)} %bitcast.342, f32[512,1536]{1,0:T(8,128)} %get-tuple-element.191, f32[512]{0:T(512)S(1)} %bitcast.365, f32[1536]{0:T(1024)S(1)} %copy-done.112), kind=kOutput, calls=%fused_computation.556 | convolution fusion | flops 2418278400 | bytes 11018240 | tf_op jit(solution)/shard_map/dot_general | solution.py:47
  242.3 4.9 multiply_reduce_fusion.4
  252.1 4.3 fusion.294
  289.3 5.3 fusion.56
  300.8 4.9 copy.79
  309.8 4.7 fusion.116
  317.9 5.8 %collective-permute-done.14 = bf16[768,1536]{1,0:T(8,128)(2,1)} collective-permute-done((bf16[768,1536]{1,0:T(8,128)(2,1)}, bf16[768,1536]{1,0:T(8,128)(2,1)}, u32[]{:S(2)}, u32[]{:S(2)}) %collective-permute-start.14) | collective-permute-done | bytes 2359328 | tf_op jit(solution)/shard_map/ppermute | solution.py:119
  357.2 4.8 collective-permute-done.18
  377.2 6.7 %collective-permute-start.32 = (f32[8,128]{1,0:T(8,128)S(1)}, f32[8,128]{1,0:T(8,128)S(1)}, u32[]{:S(2)}, u32[]{:S(2)}) collective-permute-start(f32[8,128]{1,0:T(8,128)S(1)} %select_maximum_fusion.1), channel_id=1, source_target_pairs={{0,32},{1,97},{32,0},{33,65},{64,96},{65,33},{96,64},{97,1},{2,34}... | collective-permute-start | bytes 12296 | tf_op jit(solution)/shard_map/ppermute | solution.py:119
  388.2 5.8 %collective-permute-done.20 = bf16[192,1536]{1,0:T(8,128)(2,1)S(1)} collective-permute-done((bf16[192,1536]{1,0:T(8,128)(2,1)S(1)}, bf16[192,1536]{1,0:T(8,128)(2,1)S(1)}, u32[]{:S(2)}, u32[]{:S(2)}) %collective-permute-start.20) | collective-permute-done | bytes 589856 | tf_op jit(solution)/shard_map/ppermute | solution.py:119
  402.7 6.9 %select_convert_fusion = bf16[1536,3328]{1,0:T(8,128)(2,1)S(1)} fusion(s32[1536]{0:T(1024)S(1)} %copy-done.115, s32[3328]{0:T(1024)S(1)} %copy-done.103, s32[3328]{0:T(1024)S(1)} %copy-done.104, pred[3328]{0:T(1024)(128)(4,1)S(1)} %copy-done.135, s32[1536]{0:T(1024)S(1)} %copy-done.116, f32[8,256]{1,0:T(8,128)S(1)} %slice-done.18, ...), kind=kOutput, calls=%fused_computation | convolution fusion | flops 265852928 | bytes 10372352 | tf_op jit(solution)/shard_map/dot_general | solution.py:53
  420.0 5.8 %fusion.295 = f32[528,1536]{1,0:T(8,128)S(1)} fusion(bf16[528,1920]{1,0:T(8,128)(2,1)S(1)} %fusion.53, bf16[1536,1920]{1,0:T(8,128)(2,1)} %all-gather.3.cloned.1.call-done), kind=kOutput, calls=%fused_computation.569 | convolution fusion | flops 3114270720 | bytes 11169792 | tf_op jit(solution)/shard_map/dot_general | solution.py:47
  442.0 8.8 %collective-permute-done.31 = bf16[48,1536]{1,0:T(8,128)(2,1)S(1)} collective-permute-done((bf16[48,1536]{1,0:T(8,128)(2,1)S(1)}, bf16[48,1536]{1,0:T(8,128)(2,1)S(1)}, u32[]{:S(2)}, u32[]{:S(2)}) %collective-permute-start.31) | collective-permute-done | bytes 147488 | tf_op jit(solution)/shard_map/ppermute | solution.py:119
  461.9 6.0 %collective-permute-done.34 = bf16[384,896]{1,0:T(8,128)(2,1)S(1)} collective-permute-done((bf16[384,896]{1,0:T(8,128)(2,1)S(1)}, bf16[384,896]{1,0:T(8,128)(2,1)S(1)}, u32[]{:S(2)}, u32[]{:S(2)}) %collective-permute-start.34) | collective-permute-done | bytes 688160 | tf_op jit(solution)/shard_map/ppermute | solution.py:119
  472.6 17.5 %collective-permute-start.40 = (f32[8,128]{1,0:T(8,128)S(1)}, f32[8,128]{1,0:T(8,128)S(1)}, u32[]{:S(2)}, u32[]{:S(2)}) collective-permute-start(f32[8,128]{1,0:T(8,128)S(1)} %add.1010), channel_id=1, source_target_pairs={{0,8},{1,25},{8,0},{9,17},{16,24},{17,9},{24,16},{25,1},{2,10},{3,... | collective-permute-start | bytes 12296 | tf_op jit(solution)/shard_map/ppermute | solution.py:119
  492.1 5.4 collective-permute-start.51
  501.6 4.3 collective-permute-done.45
  509.5 10.3 %collective-permute-start.55 = (f32[8,128]{1,0:T(8,128)S(1)}, f32[8,128]{1,0:T(8,128)S(1)}, u32[]{:S(2)}, u32[]{:S(2)}) collective-permute-start(f32[8,128]{1,0:T(8,128)S(1)} %add.1051), channel_id=1, source_target_pairs={{0,1},{1,0},{2,3},{3,2},{4,5},{5,4},{6,7},{7,6},{8,9},{9,8},{10,11... | collective-permute-start | bytes 12296 | tf_op jit(solution)/shard_map/ppermute | solution.py:86
  (760 shorter events, 297.6 us)
Async XLA Ops:
  7.2 81.9 %all-gather.3.cloned.1.call-start = ((), (), s32[]{:S(2)}) async-start(), calls=%async_computation | async-start | bytes 5990400 | tf_op jit(solution)/shard_map/all_gather | solution.py:308
  14.1 194.8 %all-gather.5.cloned.1.call-start = ((), (), s32[]{:S(2)}) async-start(), calls=%async_computation.1 | async-start | bytes 9584640 | tf_op jit(solution)/shard_map/all_gather | solution.py:310
  22.1 11.7 %collective-permute-start = (bf16[2,128,1536]{2,1,0:T(8,128)(2,1)S(1)}, bf16[2,128,1536]{2,1,0:T(8,128)(2,1)S(1)}, u32[]{:S(2)}, u32[]{:S(2)}) collective-permute-start(bf16[2,128,1536]{2,1,0:T(8,128)(2,1)S(1)} %get-tuple-element.211), channel_id=1, source_target_pairs={{0,0},{1,16},{8,8},{9,24},{16,1},{17,17},{24,9},{25,25},{2,2},{3,1... | collective-permute-start | bytes 2359304 | tf_op jit(solution)/shard_map/ppermute | solution.py:93
  22.8 19.7 %collective-permute-start.1 = (bf16[2,128,1536]{2,1,0:T(8,128)(2,1)S(1)}, bf16[2,128,1536]{2,1,0:T(8,128)(2,1)S(1)}, u32[]{:S(2)}, u32[]{:S(2)}) collective-permute-start(bf16[2,128,1536]{2,1,0:T(8,128)(2,1)S(1)} %get-tuple-element.212), channel_id=1, source_target_pairs={{0,8},{1,24},{8,0},{9,16},{16,9},{17,25},{24,1},{25,17},{2,10},{3,... | collective-permute-start | bytes 2359304 | tf_op jit(solution)/shard_map/ppermute | solution.py:93
  130.0 68.1 %collective-permute-start.7 = (f32[1544,128]{1,0:T(8,128)}, f32[1544,128]{1,0:T(8,128)}, u32[]{:S(2)}, u32[]{:S(2)}) collective-permute-start(f32[1544,128]{1,0:T(8,128)} %pad_maximum_fusion.8), channel_id=1, source_target_pairs={{0,96},{1,97},{2,98},{3,99},{4,100},{5,101},{6,102},{7,103},{8,104... | collective-permute-start | bytes 2371592 | tf_op jit(solution)/shard_map/ppermute | solution.py:106
  135.2 57.1 %collective-permute-start.6 = (f32[1544,128]{1,0:T(8,128)}, f32[1544,128]{1,0:T(8,128)}, u32[]{:S(2)}, u32[]{:S(2)}) collective-permute-start(f32[1544,128]{1,0:T(8,128)} %pad_maximum_fusion.8), channel_id=1, source_target_pairs={{0,64},{32,96},{1,65},{33,97},{2,66},{34,98},{3,67},{35,99},{4,68}... | collective-permute-start | bytes 2371592 | tf_op jit(solution)/shard_map/ppermute | solution.py:106
  137.4 58.0 %collective-permute-start.5 = (f32[1544,128]{1,0:T(8,128)}, f32[1544,128]{1,0:T(8,128)}, u32[]{:S(2)}, u32[]{:S(2)}) collective-permute-start(f32[1544,128]{1,0:T(8,128)} %pad_maximum_fusion.8), channel_id=1, source_target_pairs={{0,32},{32,64},{64,96},{1,33},{33,65},{65,97},{2,34},{34,66},{66,9... | collective-permute-start | bytes 2371592 | tf_op jit(solution)/shard_map/ppermute | solution.py:106
  270.3 45.9 %collective-permute-start.17 = (bf16[1552,128]{1,0:T(8,128)(2,1)}, bf16[1552,128]{1,0:T(8,128)(2,1)}, u32[]{:S(2)}, u32[]{:S(2)}) collective-permute-start(bf16[1552,128]{1,0:T(8,128)(2,1)} %pad_maximum_fusion.11), channel_id=1, source_target_pairs={{96,0},{97,1},{98,2},{99,3},{100,4},{101,5},{102,6},{103,7},{104,8... | collective-permute-start | bytes 1191944 | tf_op jit(solution)/shard_map/ppermute | solution.py:106
  271.9 42.7 %collective-permute-start.16 = (bf16[1552,128]{1,0:T(8,128)(2,1)}, bf16[1552,128]{1,0:T(8,128)(2,1)}, u32[]{:S(2)}, u32[]{:S(2)}) collective-permute-start(bf16[1552,128]{1,0:T(8,128)(2,1)} %pad_maximum_fusion.11), channel_id=1, source_target_pairs={{64,0},{96,32},{65,1},{97,33},{66,2},{98,34},{67,3},{99,35},{68,4}... | collective-permute-start | bytes 1191944 | tf_op jit(solution)/shard_map/ppermute | solution.py:106
  273.2 42.2 %collective-permute-start.15 = (bf16[1552,128]{1,0:T(8,128)(2,1)}, bf16[1552,128]{1,0:T(8,128)(2,1)}, u32[]{:S(2)}, u32[]{:S(2)}) collective-permute-start(bf16[1552,128]{1,0:T(8,128)(2,1)} %pad_maximum_fusion.11), channel_id=1, source_target_pairs={{32,0},{64,32},{96,64},{33,1},{65,33},{97,65},{34,2},{66,34},{98,6... | collective-permute-start | bytes 1191944 | tf_op jit(solution)/shard_map/ppermute | solution.py:106
  294.6 29.2 %collective-permute-start.14 = (bf16[768,1536]{1,0:T(8,128)(2,1)}, bf16[768,1536]{1,0:T(8,128)(2,1)}, u32[]{:S(2)}, u32[]{:S(2)}) collective-permute-start(bf16[768,1536]{1,0:T(8,128)(2,1)} %convolution_convert_fusion), channel_id=1, source_target_pairs={{0,2},{1,7},{2,0},{3,5},{4,6},{5,3},{6,4},{7,1},{8,10},{9,15},{10,... | collective-permute-start | bytes 7077896 | tf_op jit(solution)/shard_map/ppermute | solution.py:119
  298.0 29.7 %collective-permute-start.13 = (bf16[768,1536]{1,0:T(8,128)(2,1)}, bf16[768,1536]{1,0:T(8,128)(2,1)}, u32[]{:S(2)}, u32[]{:S(2)}) collective-permute-start(bf16[768,1536]{1,0:T(8,128)(2,1)} %convolution_convert_fusion.1), channel_id=1, source_target_pairs={{0,8},{1,25},{8,0},{9,17},{16,24},{17,9},{24,16},{25,1},{2,10},{3,... | collective-permute-start | bytes 7077896 | tf_op jit(solution)/shard_map/ppermute | solution.py:119
  346.3 15.7 %collective-permute-start.18 = (bf16[384,1536]{1,0:T(8,128)(2,1)}, bf16[384,1536]{1,0:T(8,128)(2,1)}, u32[]{:S(2)}, u32[]{:S(2)}) collective-permute-start(bf16[384,1536]{1,0:T(8,128)(2,1)} %slice.1218), channel_id=1, source_target_pairs={{0,24},{1,9},{8,16},{9,1},{16,8},{17,25},{24,0},{25,17},{2,26},{3,... | collective-permute-start | bytes 3538952 | tf_op jit(solution)/shard_map/ppermute | solution.py:119
  349.9 15.7 %collective-permute-start.19 = (bf16[384,1536]{1,0:T(8,128)(2,1)}, bf16[384,1536]{1,0:T(8,128)(2,1)S(1)}, u32[]{:S(2)}, u32[]{:S(2)}) collective-permute-start(bf16[384,1536]{1,0:T(8,128)(2,1)} %slice.1217), channel_id=1, source_target_pairs={{0,6},{1,3},{2,4},{3,1},{4,2},{5,7},{6,0},{7,5},{8,14},{9,11},{10,... | collective-permute-start | bytes 3538952 | tf_op jit(solution)/shard_map/ppermute | solution.py:119
  377.2 61.7 %collective-permute-start.32 = (f32[8,128]{1,0:T(8,128)S(1)}, f32[8,128]{1,0:T(8,128)S(1)}, u32[]{:S(2)}, u32[]{:S(2)}) collective-permute-start(f32[8,128]{1,0:T(8,128)S(1)} %select_maximum_fusion.1), channel_id=1, source_target_pairs={{0,32},{1,97},{32,0},{33,65},{64,96},{65,33},{96,64},{97,1},{2,34}... | collective-permute-start | bytes 12296 | tf_op jit(solution)/shard_map/ppermute | solution.py:119
  400.7 14.8 %collective-permute-start.22 = (bf16[96,1536]{1,0:T(8,128)(2,1)S(1)}, bf16[96,1536]{1,0:T(8,128)(2,1)S(1)}, u32[]{:S(2)}, u32[]{:S(2)}) collective-permute-start(bf16[96,1536]{1,0:T(8,128)(2,1)S(1)} %slice.1226), channel_id=1, source_target_pairs={{0,6},{1,3},{2,4},{3,1},{4,2},{5,7},{6,0},{7,5},{8,14},{9,11},{10,... | collective-permute-start | bytes 884744 | tf_op jit(solution)/shard_map/ppermute | solution.py:119
  402.1 13.5 %collective-permute-start.23 = (bf16[96,1536]{1,0:T(8,128)(2,1)S(1)}, bf16[96,1536]{1,0:T(8,128)(2,1)S(1)}, u32[]{:S(2)}, u32[]{:S(2)}) collective-permute-start(bf16[96,1536]{1,0:T(8,128)(2,1)S(1)} %slice.1225), channel_id=1, source_target_pairs={{0,24},{1,9},{8,16},{9,1},{16,8},{17,25},{24,0},{25,17},{2,26},{3,... | collective-permute-start | bytes 884744 | tf_op jit(solution)/shard_map/ppermute | solution.py:119
  425.8 12.6 %collective-permute-start.24 = (f32[16,1536]{1,0:T(8,128)S(1)}, f32[16,1536]{1,0:T(8,128)S(1)}, u32[]{:S(2)}, u32[]{:S(2)}) collective-permute-start(f32[16,1536]{1,0:T(8,128)S(1)} %slice.879), channel_id=1, source_target_pairs={{32,0},{64,32},{96,64},{33,1},{65,33},{97,65},{34,2},{66,34},{98,6... | collective-permute-start | bytes 294920 | tf_op jit(solution)/shard_map/ppermute | solution.py:106
  427.1 14.9 %collective-permute-start.30 = (bf16[48,1536]{1,0:T(8,128)(2,1)S(1)}, bf16[48,1536]{1,0:T(8,128)(2,1)S(1)}, u32[]{:S(2)}, u32[]{:S(2)}) collective-permute-start(bf16[48,1536]{1,0:T(8,128)(2,1)S(1)} %slice.1230), channel_id=1, source_target_pairs={{0,32},{1,97},{32,0},{33,65},{64,96},{65,33},{96,64},{97,1},{2,34}... | collective-permute-start | bytes 442376 | tf_op jit(solution)/shard_map/ppermute | solution.py:119
  427.6 23.2 %collective-permute-start.28 = (bf16[768,1024]{1,0:T(8,128)(2,1)S(1)}, bf16[768,1024]{1,0:T(8,128)(2,1)S(1)}, u32[]{:S(2)}, u32[]{:S(2)}) collective-permute-start(bf16[768,1024]{1,0:T(8,128)(2,1)S(1)} %convolution_convert_fusion.2), channel_id=1, source_target_pairs={{0,32},{1,97},{32,0},{33,65},{64,96},{65,33},{96,64},{97,1},{2,34}... | collective-permute-start | bytes 4718600 | tf_op jit(solution)/shard_map/ppermute | solution.py:119
  431.7 19.2 %collective-permute-start.29 = (bf16[768,896]{1,0:T(8,128)(2,1)S(1)}, bf16[768,896]{1,0:T(8,128)(2,1)S(1)}, u32[]{:S(2)}, u32[]{:S(2)}) collective-permute-start(bf16[768,896]{1,0:T(8,128)(2,1)S(1)} %add_convert_fusion.1), channel_id=1, source_target_pairs={{0,2},{1,7},{2,0},{3,5},{4,6},{5,3},{6,4},{7,1},{8,10},{9,15},{10,... | collective-permute-start | bytes 4128776 | tf_op jit(solution)/shard_map/ppermute | solution.py:119
  438.4 12.4 %collective-permute-start.31 = (bf16[48,1536]{1,0:T(8,128)(2,1)S(1)}, bf16[48,1536]{1,0:T(8,128)(2,1)S(1)}, u32[]{:S(2)}, u32[]{:S(2)}) collective-permute-start(bf16[48,1536]{1,0:T(8,128)(2,1)S(1)} %slice.1229), channel_id=1, source_target_pairs={{0,32},{1,97},{32,0},{33,65},{64,96},{65,33},{96,64},{97,1},{2,34}... | collective-permute-start | bytes 442376 | tf_op jit(solution)/shard_map/ppermute | solution.py:119
  440.0 17.7 %collective-permute-start.10 = (f32[256,1536]{1,0:T(8,128)S(1)}, f32[256,1536]{1,0:T(8,128)S(1)}, u32[]{:S(2)}, u32[]{:S(2)}) collective-permute-start(f32[256,1536]{1,0:T(8,128)S(1)} %copy-done.66), channel_id=1, source_target_pairs={{0,1},{1,0},{2,3},{3,2},{4,5},{5,4},{6,7},{7,6},{8,9},{9,8},{10,11... | collective-permute-start | bytes 4718600 | tf_op jit(solution)/shard_map/ppermute | solution.py:86
  442.0 14.9 %collective-permute-start.25 = (f32[256,1536]{1,0:T(8,128)S(1)}, f32[256,1536]{1,0:T(8,128)S(1)}, u32[]{:S(2)}, u32[]{:S(2)}) collective-permute-start(f32[256,1536]{1,0:T(8,128)S(1)} %slice_select_fusion), channel_id=1, source_target_pairs={{0,1},{1,0},{2,3},{3,2},{4,5},{5,4},{6,7},{7,6},{8,9},{9,8},{10,11... | collective-permute-start | bytes 4718600 | tf_op jit(solution)/shard_map/ppermute | solution.py:86
  456.9 12.2 %collective-permute-start.33 = (bf16[384,1024]{1,0:T(8,128)(2,1)S(1)}, bf16[384,1024]{1,0:T(8,128)(2,1)S(1)}, u32[]{:S(2)}, u32[]{:S(2)}) collective-permute-start(bf16[384,1024]{1,0:T(8,128)(2,1)S(1)} %slice.1219), channel_id=1, source_target_pairs={{0,96},{1,33},{32,64},{33,1},{64,32},{65,97},{96,0},{97,65},{2,98}... | collective-permute-start | bytes 2359304 | tf_op jit(solution)/shard_map/ppermute | solution.py:119
  461.3 28.8 %collective-permute-start.11 = (bf16[128,1536]{1,0:T(8,128)(2,1)S(1)}, bf16[128,1536]{1,0:T(8,128)(2,1)S(1)}, u32[]{:S(2)}, u32[]{:S(2)}) collective-permute-start(bf16[128,1536]{1,0:T(8,128)(2,1)S(1)} %get-tuple-element.218), channel_id=1, source_target_pairs={{0,0},{1,16},{8,8},{9,24},{16,1},{17,17},{24,9},{25,25},{2,2},{3,1... | collective-permute-start | bytes 1179656 | tf_op jit(solution)/shard_map/ppermute | solution.py:93
  467.9 22.1 %collective-permute-start.12 = (bf16[128,1536]{1,0:T(8,128)(2,1)S(1)}, bf16[128,1536]{1,0:T(8,128)(2,1)S(1)}, u32[]{:S(2)}, u32[]{:S(2)}) collective-permute-start(bf16[128,1536]{1,0:T(8,128)(2,1)S(1)} %get-tuple-element.219), channel_id=1, source_target_pairs={{0,8},{1,24},{8,0},{9,16},{16,9},{17,25},{24,1},{25,17},{2,10},{3,... | collective-permute-start | bytes 1179656 | tf_op jit(solution)/shard_map/ppermute | solution.py:93
  469.5 21.7 %collective-permute-start.38 = (bf16[192,1024]{1,0:T(8,128)(2,1)S(1)}, bf16[192,1024]{1,0:T(8,128)(2,1)S(1)}, u32[]{:S(2)}, u32[]{:S(2)}) collective-permute-start(bf16[192,1024]{1,0:T(8,128)(2,1)S(1)} %slice.1223), channel_id=1, source_target_pairs={{0,2},{1,7},{2,0},{3,5},{4,6},{5,3},{6,4},{7,1},{8,10},{9,15},{10,... | collective-permute-start | bytes 1179656 | tf_op jit(solution)/shard_map/ppermute | solution.py:119
  470.4 20.8 %collective-permute-start.39 = (bf16[192,896]{1,0:T(8,128)(2,1)S(1)}, bf16[192,896]{1,0:T(8,128)(2,1)S(1)}, u32[]{:S(2)}, u32[]{:S(2)}) collective-permute-start(bf16[192,896]{1,0:T(8,128)(2,1)S(1)} %slice.1224), channel_id=1, source_target_pairs={{0,32},{1,97},{32,0},{33,65},{64,96},{65,33},{96,64},{97,1},{2,34}... | collective-permute-start | bytes 1032200 | tf_op jit(solution)/shard_map/ppermute | solution.py:119
  472.6 18.6 %collective-permute-start.40 = (f32[8,128]{1,0:T(8,128)S(1)}, f32[8,128]{1,0:T(8,128)S(1)}, u32[]{:S(2)}, u32[]{:S(2)}) collective-permute-start(f32[8,128]{1,0:T(8,128)S(1)} %add.1010), channel_id=1, source_target_pairs={{0,8},{1,25},{8,0},{9,17},{16,24},{17,9},{24,16},{25,1},{2,10},{3,... | collective-permute-start | bytes 12296 | tf_op jit(solution)/shard_map/ppermute | solution.py:119
  492.1 15.6 %collective-permute-start.51 = (f32[24,1536]{1,0:T(8,128)S(1)}, f32[24,1536]{1,0:T(8,128)S(1)}, u32[]{:S(2)}, u32[]{:S(2)}) collective-permute-start(f32[24,1536]{1,0:T(8,128)S(1)} %convert_add_fusion.21), channel_id=1, source_target_pairs={{0,0},{1,64},{32,32},{33,96},{64,1},{65,65},{96,33},{97,97},{2,2},... | collective-permute-start | bytes 442376 | tf_op jit(solution)/shard_map/ppermute | solution.py:102
  525.3 11.2 %collective-permute-start.53 = (f32[12]{0:T(128)S(1)}, f32[12]{0:T(128)S(1)}, u32[]{:S(2)}, u32[]{:S(2)}) collective-permute-start(f32[12]{0:T(128)S(1)} %bitcast_divide_fusion), channel_id=1, source_target_pairs={{1,0},{4,1},{7,2},{10,3},{13,4},{16,5},{19,6},{22,7},{25,8},{28,9}... | collective-permute-start | bytes 152 | tf_op jit(solution)/shard_map/ppermute | solution.py:578
  (215 other events, 1894.1 us)
Sparse Core Ops, SparseCore 0:
  14.2 74.8 all-gather.2
  92.5 102.8 all-gather.4

commit v4 on v3

--- a/solution.py
+++ b/solution.py
@@ -153,7 +153,6 @@
     def __init__(self, sends, keeps, orders):
         self.sends = [v.astype(BF16) for v in sends]
         self.keeps, self.orders, self.step = keeps, orders, 0
-        self.start()
 
     def start(self):
         self.arrived = [
@@ -190,11 +189,12 @@
 
 
 def by_pair(value):
-    return value.reshape(CHUNKS, CHUNK, PAIRS, LANES).transpose(0, 2, 1, 3)
+    pairs = [value[:, p * LANES : (p + 1) * LANES] for p in range(PAIRS)]
+    return jnp.stack(pairs).reshape(PAIRS, CHUNKS, CHUNK, LANES)
 
 
 def from_pairs(value):
-    return value.transpose(0, 2, 1, 3).reshape(TOKENS, HALF)
+    return jnp.concatenate([value[p].reshape(TOKENS, LANES) for p in range(PAIRS)], axis=1)
 
 
 def one_head(value):
@@ -203,7 +203,7 @@
 
 
 def decays(cl):
-    heads = cl[:, :HALF_HEADS].reshape(CHUNKS, CHUNK, PAIRS, 2).transpose(0, 2, 3, 1)
+    heads = cl[:, :HALF_HEADS].T.reshape(PAIRS, 2, CHUNKS, CHUNK).transpose(0, 2, 1, 3)
     causal = iota((CHUNK, CHUNK), 0) >= iota((CHUNK, CHUNK), 1)
     differ = jnp.where(causal, heads[..., :, None] - heads[..., None, :], 0.0)
     return jnp.where(causal, jnp.exp(differ), 0.0)
@@ -384,9 +384,9 @@
     incoming = combine(pack_full(local[CHUNKS], piece_decay), 1, unpack_full)
     decay = decays(cl)
     scores = jnp.einsum("ktn,ksn->kts", c_proj, b_proj, precision=PRECISE)
-    mixes = (scores[:, None, None] * decay).astype(BF16)
+    mixes = (scores[None, :, None] * decay).astype(BF16)
     u_pairs = one_head(by_pair(u_low.astype(BF16)))
-    y_chunk = from_pairs(product("kpjts,kpjsc->kptc", mixes, u_pairs))
+    y_chunk = from_pairs(product("pkjts,pkjsc->pktc", mixes, u_pairs))
 
     starts = jnp.stack([between(0, k) * incoming + local[k] for k in range(CHUNKS)])
     state_end = between(0, CHUNKS) * incoming + local[CHUNKS]
@@ -398,7 +398,7 @@
     gate = mm(normed[:TOKENS], w_gate)
     gate_sig = sigmoid(gate)
     gate_silu = gate * gate_sig
-    d_gated = mm(cot, w_out, NT)
+    (d_gated,) = lax.optimization_barrier((mm(cot, w_out, NT),))
     g = mixed * gate_silu
     e = d_gated * gate_gain
     sums = jnp.concatenate(
@@ -443,11 +443,12 @@
         [mm(normed_gate[:middle, :TOKENS], d_gate), mm(gated_b[:middle], cot)],
         [order_gate, order_out],
     )
+    first.start()
 
     dy_pairs = by_pair(dy_low.astype(BF16))
-    du_chunk = from_pairs(product("kpjts,kpjtc->kpsc", mixes, one_head(dy_pairs)))
-    both = product("kptc,kpjsc->kpjts", dy_pairs, u_pairs)
-    d_scores = jnp.sum(decay * both, axis=(1, 2)).astype(BF16)
+    du_chunk = from_pairs(product("pkjts,pkjtc->pksc", mixes, one_head(dy_pairs)))
+    both = product("pktc,pkjsc->pkjts", dy_pairs, u_pairs)
+    d_scores = jnp.sum(decay * both, axis=(0, 2)).astype(BF16)
     db_chunk = product("kts,ktn->ksn", d_scores, c_low)
     dc_chunk = product("kts,ksn->ktn", d_scores, b_low)
 
@@ -497,14 +498,9 @@
     y_of, x_of, z_of = block_order(order_b)
     row_at = rows_of((y_of * 4 + x_of) * 4 + z_of)[:, None]
     device_of, slot_of = row_at // 12, row_at % 12
-    conv_x = d_conv[:, :HALF]
-    conv_full = jnp.concatenate(
-        [ordered(first_core, conv_x, jnp.zeros_like(conv_x), axis=1), d_conv[:, HALF:]], axis=1
-    )
     slot_pick = (slot_of == iota((1536, 8), 1)).astype(F32)
-    conv_cols = iota((1536, CONV), 1)
-    conv_spread = jnp.where(conv_cols // 26 == device_of, exact(slot_pick, conv_full), 0.0)
-    fold = (iota((CONV, LANES), 0) % 26 + HALF_HEADS == iota((CONV, LANES), 1)).astype(BF16)
+    conv_spread = jnp.where(conv_at // 26 == device_of, exact(slot_pick, d_conv), 0.0)
+    fold = (conv_at.T % 26 + HALF_HEADS == iota((ACT, LANES), 1)).astype(BF16)
     gain_at = WIDTH + core * HALF + iota((1536, HALF), 1)
     gain_spread = jnp.where((gain_at // 36 == device_of) & (slot_of == 5), d_gate_gain[None, :], 0.0)
     gain_fold = (
@@ -524,7 +520,9 @@
         [order_a, order_b],
     )
 
-    d_normed = mm(d_crit, w_crit, NT)
+    second.sends, d_crit_late = lax.optimization_barrier((second.sends, d_crit))
+    second.start()
+    d_normed = mm(d_crit_late, w_crit, NT)
     d_halo = along_y(d_normed[TOKENS:], -1)
     d_normed = d_normed[:TOKENS] + mm(d_gate, w_gate, NT)
     d_normed = jnp.concatenate(
@@ -538,13 +536,16 @@
     d_tokens = own_inv * d_own - (own_inv * own_inv * own_inv) * own * jnp.mean(
         own * d_own, axis=1, keepdims=True
     )
-    input_grad = to_owner((own_cot.astype(F32) + d_tokens).astype(BF16)).astype(F32)
+    input_grad = to_owner((own_cot.astype(F32) + d_tokens).astype(BF16))
 
     head_own = jnp.pad(d_head, ((0, 5), (0, 0)))
     for step in range(6):
         head_got = exchange(head_own, CHIPS[step // 2], step % 2)
         head_own, head_got = wait([second, first] if step < 2 else [second], head_own, head_got)
         head_own = head_own + head_got
+        if step == 4:
+            head_own, input_grad = lax.optimization_barrier((head_own, input_grad))
+    input_grad = input_grad.astype(F32)
     head_other = swap_cores(head_own)
     rows_a, rows_b = second.totals
     gate_rows, out_rows_grad = first.totals

time: 552 us -> 518 us (0.938)
  local copies, waits for them, and re-layouts: 93.1 us -> 57.2 us
  waiting for transfers between devices: 99.2 us -> 131 us
  matrix products: 149 us -> 129 us
  other arithmetic: 81.4 us -> 75.4 us
    ppermute x8, waiting for transfers between devices: 1.89 us -> 23 us  [along_y(): lax.ppermute(value, 'y', [(y, y + steps) for y in range(4) if 0 <= y + st...]
    transpose x4 -> x1, local copies, waits for them, and re-layouts: 13.1 us -> 0.03 us  [decays(): cl[:, :HALF_HEADS].T.reshape(PAIRS, 2, CHUNKS, CHUNK).transpose(0, 2, 1, 3)]
    reshape x4 -> x1, local copies, waits for them, and re-layouts: 13 us -> 0.02 us  [decays(): cl[:, :HALF_HEADS].T.reshape(PAIRS, 2, CHUNKS, CHUNK).transpose(0, 2, 1, 3)]
    ppermute x30, waiting for transfers between devices: 46.2 us -> 58.6 us  [exchange(): return lax.ppermute(value, axes, pairs)]
    unnamed x352 -> x412, local copies, waits for them, and re-layouts: 21.5 us -> 30.4 us
    dot_general x5, matrix products: 16.5 us -> 9.95 us  [product(): return jnp.einsum(terms, a, b, preferred_element_type=F32)]
    convert_element_type x2 -> x0, local copies, waits for them, and re-layouts: 5.58 us -> none  [the longest x1 2.98 us: on_device(): u_pairs = one_head(by_pair(u_low.astype(BF16)))]
  transfers between devices with their start and end apart: 58 -> 58, of which waited for: 22 -> 22; matrix products, arithmetic and copies ran while one was open for 40% -> 33% of each run, Pallas kernels for 0% -> 0%
where the time goes in v4:
time: 518 us; the launch traced here: 512 us
  waiting for transfers between devices  131 us (25%)
  matrix products  129 us (25%)
  starting transfers between devices  102 us (20%)
  other arithmetic  75.4 us (15%)
  local copies, waits for them, and re-layouts  57.2 us (11%)
  between operations  17.9 us (3%)
    dot_general x23, matrix products, mm(): lax.dot_general(a.astype(BF16), b.astype(BF16), (dims, ((), ())), preferr...  86.7 us
    ppermute x30, waiting for transfers between devices, exchange(): return lax.ppermute(value, axes, pairs)  58.6 us
    ppermute x30, starting transfers between devices, exchange(): return lax.ppermute(value, axes, pairs)  47 us
    unnamed x412, local copies, waits for them, and re-layouts  30.4 us
    all_gather x1, waiting for transfers between devices, on_device(): w_crit = lax.all_gather(in_rows_low[:, :CRIT], CHIPS, axis=0, tiled=True)  28.8 us
    ppermute x8, waiting for transfers between devices, along_y(): lax.ppermute(value, 'y', [(y, y + steps) for y in range(4) if 0 <= y + st...  23 us
    ppermute x8, starting transfers between devices, along_y(): lax.ppermute(value, 'y', [(y, y + steps) for y in range(4) if 0 <= y + st...  17.7 us
    dot_general x9, matrix products, exact(): lax.dot_general(a, b, (dims, ((), ())), precision=PRECISE, preferred_elem...  16.3 us
  transfers between devices with their start and end apart: 58, of which 22 were waited for; matrix products, arithmetic and copies ran while one was open for 33% of the time, Pallas kernels for 0%

profile of v4, /device:TPU:7, one launch (start us, length us, event | category | flops | bytes accessed | tf_op | source)
XLA Modules:
  0.0 512.5 jit_solution(14739361665827713168)
XLA Ops:
  15.7 5.1 collective-permute-start.8
  32.1 11.0 %collective-permute-done.1 = bf16[2,128,1536]{2,1,0:T(8,128)(2,1)S(1)} collective-permute-done((bf16[2,128,1536]{2,1,0:T(8,128)(2,1)S(1)}, bf16[2,128,1536]{2,1,0:T(8,128)(2,1)S(1)}, u32[]{:S(2)}, u32[]{:S(2)}) %collective-permute-start.1) | collective-permute-done | bytes 786464 | tf_op jit(solution)/shard_map/ppermute | solution.py:93
  58.7 28.8 %all-gather.3.cloned.1.call-done = bf16[1536,1920]{1,0:T(8,128)(2,1)} async-done(((bf16[24,1920]{1,0:T(8,128)(2,1)}), bf16[1536,1920]{1,0:T(8,128)(2,1)}) %all-gather.3.cloned.1.call-update) | async-done | bytes 5898256 | tf_op jit(solution)/shard_map/all_gather | solution.py:308
  87.5 3.7 fusion.297
  91.7 6.4 %fusion.300 = f32[528,1920]{1,0:T(8,128)S(1)} fusion(bf16[528,1536]{1,0:T(8,128)(2,1)S(1)} %fusion.29, bf16[1536,1920]{1,0:T(8,128)(2,1)} %all-gather.3.cloned.1.call-done), kind=kOutput, calls=%fused_computation.622 | convolution fusion | flops 3114270720 | bytes 11575296 | tf_op jit(solution)/shard_map/dot_general | solution.py:47
  103.1 4.3 fusion.55
  107.6 8.8 %fusion.26 = (f32[512,1792]{1,0:T(8,128)S(1)}, f32[512,1792]{1,0:T(8,128)}) fusion(f32[512,1792]{1,0:T(8,128)} %slice.996, f32[1792]{0:T(1024)S(1)} %get-tuple-element.175, f32[8,1792]{1,0:T(8,128)S(1)} %slice.995, f32[1792]{0:T(1024)S(1)} %get-tuple-element.176, f32[1792]{0:T(1024)S(1)} %get-tuple-element.177, f32[1792]{0:T(1024)S(1)} %get-tuple-element.178, ...), kind=kLoop, calls=%fused_computation.54 | loop fusion | flops 13762560 | bytes 11103232 | tf_op jit(solution)/shard_map/mul | solution.py:355
  128.0 5.1 %collective-permute-start.7 = (f32[1544,128]{1,0:T(8,128)}, f32[1544,128]{1,0:T(8,128)}, u32[]{:S(2)}, u32[]{:S(2)}) collective-permute-start(f32[1544,128]{1,0:T(8,128)} %pad_maximum_fusion.8), channel_id=1, source_target_pairs={{0,96},{1,97},{2,98},{3,99},{4,100},{5,101},{6,102},{7,103},{8,104... | collective-permute-start | bytes 2371592 | tf_op jit(solution)/shard_map/ppermute | solution.py:106
  150.1 4.6 fusion.48
  154.8 4.2 fusion.49
  159.1 4.3 fusion.50
  166.2 3.8 fusion.96
  170.8 22.1 %collective-permute-done.5 = f32[1544,128]{1,0:T(8,128)} collective-permute-done((f32[1544,128]{1,0:T(8,128)}, f32[1544,128]{1,0:T(8,128)}, u32[]{:S(2)}, u32[]{:S(2)}) %collective-permute-start.5) | collective-permute-done | bytes 790560 | tf_op jit(solution)/shard_map/ppermute | solution.py:106
  193.8 4.0 add_bitcast_fusion
  209.5 4.3 fusion.86
  216.0 9.8 %multiply_reduce_fusion.7 = (f32[512]{0:T(512)S(1)}, f32[512]{0:T(512)S(1)}, f32[512,1536]{1,0:T(8,128)}, f32[512,1536]{1,0:T(8,128)}, f32[512,1536]{1,0:T(8,128)}) fusion(f32[512,1536]{1,0:T(8,128)} %fusion.86, f32[1536]{0:T(1024)S(1)} %fusion.96, f32[512,1792]{1,0:T(8,128)S(1)} %copy-done.1, f32[1536]{0:T(1024)S(1)} %copy-done.104, ...), kind=kOutput, calls=%fused_computation.87 | convolution fusion | flops 2426928128 | bytes 31477760 | tf_op jit(solution)/shard_map/dot_general | solution.py:47
  228.7 5.7 %fusion.275 = f32[512,1536]{1,0:T(8,128)S(1)} fusion(bf16[1536,1536]{1,0:T(8,128)(2,1)} %bitcast.379, f32[512,1536]{1,0:T(8,128)} %get-tuple-element.201, f32[512]{0:T(512)S(1)} %bitcast.465, f32[1536]{0:T(1024)S(1)} %fusion.96), kind=kOutput, calls=%fused_computation.609 | convolution fusion | flops 2418278400 | bytes 11018240 | tf_op jit(solution)/shard_map/dot_general | solution.py:47
  289.1 12.4 %collective-permute-done.14 = bf16[768,1536]{1,0:T(8,128)(2,1)} collective-permute-done((bf16[768,1536]{1,0:T(8,128)(2,1)}, bf16[768,1536]{1,0:T(8,128)(2,1)}, u32[]{:S(2)}, u32[]{:S(2)}) %collective-permute-start.14) | collective-permute-done | bytes 2359328 | tf_op jit(solution)/shard_map/ppermute | solution.py:119
  301.6 4.4 collective-permute-done.13
  306.0 3.8 convert_add_fusion.1
  329.1 9.7 %collective-permute-done.18 = bf16[384,1536]{1,0:T(8,128)(2,1)S(1)} collective-permute-done((bf16[384,1536]{1,0:T(8,128)(2,1)S(1)}, bf16[384,1536]{1,0:T(8,128)(2,1)S(1)}, u32[]{:S(2)}, u32[]{:S(2)}) %collective-permute-start.18) | collective-permute-done | bytes 1179680 | tf_op jit(solution)/shard_map/ppermute | solution.py:119
  349.9 6.2 %collective-permute-start.28 = (f32[8,128]{1,0:T(8,128)S(1)}, f32[8,128]{1,0:T(8,128)S(1)}, u32[]{:S(2)}, u32[]{:S(2)}) collective-permute-start(f32[8,128]{1,0:T(8,128)S(1)} %select_maximum_fusion.1), channel_id=1, source_target_pairs={{0,32},{1,97},{32,0},{33,65},{64,96},{65,33},{96,64},{97,1},{2,34}... | collective-permute-start | bytes 12296 | tf_op jit(solution)/shard_map/ppermute | solution.py:119
  360.2 5.8 %collective-permute-done.20 = bf16[192,1536]{1,0:T(8,128)(2,1)S(1)} collective-permute-done((bf16[192,1536]{1,0:T(8,128)(2,1)S(1)}, bf16[192,1536]{1,0:T(8,128)(2,1)S(1)}, u32[]{:S(2)}, u32[]{:S(2)}) %collective-permute-start.20) | collective-permute-done | bytes 589856 | tf_op jit(solution)/shard_map/ppermute | solution.py:119
  374.1 4.0 select_convert_fusion
  386.6 5.8 %fusion.304 = f32[528,1536]{1,0:T(8,128)S(1)} fusion(bf16[528,1920]{1,0:T(8,128)(2,1)S(1)} %fusion.56, bf16[1536,1920]{1,0:T(8,128)(2,1)} %all-gather.3.cloned.1.call-done), kind=kOutput, calls=%fused_computation.626 | convolution fusion | flops 3114270720 | bytes 11169792 | tf_op jit(solution)/shard_map/dot_general | solution.py:47
  406.3 10.9 %collective-permute-done.27 = bf16[48,1536]{1,0:T(8,128)(2,1)S(1)} collective-permute-done((bf16[48,1536]{1,0:T(8,128)(2,1)S(1)}, bf16[48,1536]{1,0:T(8,128)(2,1)S(1)}, u32[]{:S(2)}, u32[]{:S(2)}) %collective-permute-start.27) | collective-permute-done | bytes 147488 | tf_op jit(solution)/shard_map/ppermute | solution.py:119
  427.4 6.9 %collective-permute-done.30 = bf16[384,896]{1,0:T(8,128)(2,1)S(1)} collective-permute-done((bf16[384,896]{1,0:T(8,128)(2,1)S(1)}, bf16[384,896]{1,0:T(8,128)(2,1)S(1)}, u32[]{:S(2)}, u32[]{:S(2)}) %collective-permute-start.30) | collective-permute-done | bytes 688160 | tf_op jit(solution)/shard_map/ppermute | solution.py:119
  439.9 15.2 %collective-permute-start.36 = (f32[8,128]{1,0:T(8,128)S(1)}, f32[8,128]{1,0:T(8,128)S(1)}, u32[]{:S(2)}, u32[]{:S(2)}) collective-permute-start(f32[8,128]{1,0:T(8,128)S(1)} %add.1010), channel_id=1, source_target_pairs={{0,8},{1,25},{8,0},{9,17},{16,24},{17,9},{24,16},{25,1},{2,10},{3,... | collective-permute-start | bytes 12296 | tf_op jit(solution)/shard_map/ppermute | solution.py:119
  458.6 4.0 collective-permute-start.51
  467.3 4.4 collective-permute-done.41
  476.3 8.4 %collective-permute-start.55 = (f32[8,128]{1,0:T(8,128)S(1)}, f32[8,128]{1,0:T(8,128)S(1)}, u32[]{:S(2)}, u32[]{:S(2)}) collective-permute-start(f32[8,128]{1,0:T(8,128)S(1)} %add.1057), channel_id=1, source_target_pairs={{0,1},{1,0},{2,3},{3,2},{4,5},{5,4},{6,7},{7,6},{8,9},{9,8},{10,11... | collective-permute-start | bytes 12296 | tf_op jit(solution)/shard_map/ppermute | solution.py:86
  490.1 5.6 %collective-permute-start.53 = (f32[12]{0:T(128)S(1)}, f32[12]{0:T(128)S(1)}, u32[]{:S(2)}, u32[]{:S(2)}) collective-permute-start(f32[12]{0:T(128)S(1)} %bitcast_divide_fusion), channel_id=1, source_target_pairs={{1,0},{4,1},{7,2},{10,3},{13,4},{16,5},{19,6},{22,7},{25,8},{28,9}... | collective-permute-start | bytes 152 | tf_op jit(solution)/shard_map/ppermute | solution.py:579
  (815 shorter events, 250.8 us)
Async XLA Ops:
  7.2 80.3 %all-gather.3.cloned.1.call-start = ((), (), s32[]{:S(2)}) async-start(), calls=%async_computation | async-start | bytes 5990400 | tf_op jit(solution)/shard_map/all_gather | solution.py:308
  14.1 189.9 %all-gather.5.cloned.1.call-start = ((), (), s32[]{:S(2)}) async-start(), calls=%async_computation.1 | async-start | bytes 9584640 | tf_op jit(solution)/shard_map/all_gather | solution.py:310
  15.7 31.5 %collective-permute-start.8 = (bf16[24,1536]{1,0:T(8,128)(2,1)}, bf16[24,1536]{1,0:T(8,128)(2,1)}, u32[]{:S(2)}, u32[]{:S(2)}) collective-permute-start(bf16[24,1536]{1,0:T(8,128)(2,1)} %convert.150), channel_id=1, source_target_pairs={{0,0},{1,64},{32,32},{33,96},{64,1},{65,65},{96,33},{97,97},{2,2},... | collective-permute-start | bytes 221192 | tf_op jit(solution)/shard_map/ppermute | solution.py:102
  23.5 19.7 %collective-permute-start.1 = (bf16[2,128,1536]{2,1,0:T(8,128)(2,1)S(1)}, bf16[2,128,1536]{2,1,0:T(8,128)(2,1)S(1)}, u32[]{:S(2)}, u32[]{:S(2)}) collective-permute-start(bf16[2,128,1536]{2,1,0:T(8,128)(2,1)S(1)} %get-tuple-element.270), channel_id=1, source_target_pairs={{0,8},{1,24},{8,0},{9,16},{16,9},{17,25},{24,1},{25,17},{2,10},{3,... | collective-permute-start | bytes 2359304 | tf_op jit(solution)/shard_map/ppermute | solution.py:93
  128.0 65.8 %collective-permute-start.7 = (f32[1544,128]{1,0:T(8,128)}, f32[1544,128]{1,0:T(8,128)}, u32[]{:S(2)}, u32[]{:S(2)}) collective-permute-start(f32[1544,128]{1,0:T(8,128)} %pad_maximum_fusion.8), channel_id=1, source_target_pairs={{0,96},{1,97},{2,98},{3,99},{4,100},{5,101},{6,102},{7,103},{8,104... | collective-permute-start | bytes 2371592 | tf_op jit(solution)/shard_map/ppermute | solution.py:106
  133.2 36.8 %collective-permute-start.6 = (f32[1544,128]{1,0:T(8,128)}, f32[1544,128]{1,0:T(8,128)}, u32[]{:S(2)}, u32[]{:S(2)}) collective-permute-start(f32[1544,128]{1,0:T(8,128)} %pad_maximum_fusion.8), channel_id=1, source_target_pairs={{0,64},{32,96},{1,65},{33,97},{2,66},{34,98},{3,67},{35,99},{4,68}... | collective-permute-start | bytes 2371592 | tf_op jit(solution)/shard_map/ppermute | solution.py:106
  135.4 57.6 %collective-permute-start.5 = (f32[1544,128]{1,0:T(8,128)}, f32[1544,128]{1,0:T(8,128)}, u32[]{:S(2)}, u32[]{:S(2)}) collective-permute-start(f32[1544,128]{1,0:T(8,128)} %pad_maximum_fusion.8), channel_id=1, source_target_pairs={{0,32},{32,64},{64,96},{1,33},{33,65},{65,97},{2,34},{34,66},{66,9... | collective-permute-start | bytes 2371592 | tf_op jit(solution)/shard_map/ppermute | solution.py:106
  248.9 38.3 %collective-permute-start.17 = (bf16[1552,128]{1,0:T(8,128)(2,1)}, bf16[1552,128]{1,0:T(8,128)(2,1)}, u32[]{:S(2)}, u32[]{:S(2)}) collective-permute-start(bf16[1552,128]{1,0:T(8,128)(2,1)} %pad_maximum_fusion.11), channel_id=1, source_target_pairs={{96,0},{97,1},{98,2},{99,3},{100,4},{101,5},{102,6},{103,7},{104,8... | collective-permute-start | bytes 1191944 | tf_op jit(solution)/shard_map/ppermute | solution.py:106
  250.2 35.3 %collective-permute-start.16 = (bf16[1552,128]{1,0:T(8,128)(2,1)}, bf16[1552,128]{1,0:T(8,128)(2,1)S(1)}, u32[]{:S(2)}, u32[]{:S(2)}) collective-permute-start(bf16[1552,128]{1,0:T(8,128)(2,1)} %pad_maximum_fusion.11), channel_id=1, source_target_pairs={{64,0},{96,32},{65,1},{97,33},{66,2},{98,34},{67,3},{99,35},{68,4}... | collective-permute-start | bytes 1191944 | tf_op jit(solution)/shard_map/ppermute | solution.py:106
  251.5 34.9 %collective-permute-start.15 = (bf16[1552,128]{1,0:T(8,128)(2,1)}, bf16[1552,128]{1,0:T(8,128)(2,1)}, u32[]{:S(2)}, u32[]{:S(2)}) collective-permute-start(bf16[1552,128]{1,0:T(8,128)(2,1)} %pad_maximum_fusion.11), channel_id=1, source_target_pairs={{32,0},{64,32},{96,64},{33,1},{65,33},{97,65},{34,2},{66,34},{98,6... | collective-permute-start | bytes 1191944 | tf_op jit(solution)/shard_map/ppermute | solution.py:106
  272.3 29.3 %collective-permute-start.14 = (bf16[768,1536]{1,0:T(8,128)(2,1)}, bf16[768,1536]{1,0:T(8,128)(2,1)}, u32[]{:S(2)}, u32[]{:S(2)}) collective-permute-start(bf16[768,1536]{1,0:T(8,128)(2,1)} %convolution_convert_fusion), channel_id=1, source_target_pairs={{0,2},{1,7},{2,0},{3,5},{4,6},{5,3},{6,4},{7,1},{8,10},{9,15},{10,... | collective-permute-start | bytes 7077896 | tf_op jit(solution)/shard_map/ppermute | solution.py:119
  276.3 29.7 %collective-permute-start.13 = (bf16[768,1536]{1,0:T(8,128)(2,1)}, bf16[768,1536]{1,0:T(8,128)(2,1)}, u32[]{:S(2)}, u32[]{:S(2)}) collective-permute-start(bf16[768,1536]{1,0:T(8,128)(2,1)} %convolution_convert_fusion.1), channel_id=1, source_target_pairs={{0,8},{1,25},{8,0},{9,17},{16,24},{17,9},{24,16},{25,1},{2,10},{3,... | collective-permute-start | bytes 7077896 | tf_op jit(solution)/shard_map/ppermute | solution.py:119
  323.5 15.4 %collective-permute-start.18 = (bf16[384,1536]{1,0:T(8,128)(2,1)S(1)}, bf16[384,1536]{1,0:T(8,128)(2,1)S(1)}, u32[]{:S(2)}, u32[]{:S(2)}) collective-permute-start(bf16[384,1536]{1,0:T(8,128)(2,1)S(1)} %slice.1450), channel_id=1, source_target_pairs={{0,24},{1,9},{8,16},{9,1},{16,8},{17,25},{24,0},{25,17},{2,26},{3,... | collective-permute-start | bytes 3538952 | tf_op jit(solution)/shard_map/ppermute | solution.py:119
  323.5 15.8 %collective-permute-start.19 = (bf16[384,1536]{1,0:T(8,128)(2,1)}, bf16[384,1536]{1,0:T(8,128)(2,1)S(1)}, u32[]{:S(2)}, u32[]{:S(2)}) collective-permute-start(bf16[384,1536]{1,0:T(8,128)(2,1)} %slice.1449), channel_id=1, source_target_pairs={{0,6},{1,3},{2,4},{3,1},{4,2},{5,7},{6,0},{7,5},{8,14},{9,11},{10,... | collective-permute-start | bytes 3538952 | tf_op jit(solution)/shard_map/ppermute | solution.py:119
  349.9 53.7 %collective-permute-start.28 = (f32[8,128]{1,0:T(8,128)S(1)}, f32[8,128]{1,0:T(8,128)S(1)}, u32[]{:S(2)}, u32[]{:S(2)}) collective-permute-start(f32[8,128]{1,0:T(8,128)S(1)} %select_maximum_fusion.1), channel_id=1, source_target_pairs={{0,32},{1,97},{32,0},{33,65},{64,96},{65,33},{96,64},{97,1},{2,34}... | collective-permute-start | bytes 12296 | tf_op jit(solution)/shard_map/ppermute | solution.py:119
  384.7 21.6 %collective-permute-start.26 = (bf16[48,1536]{1,0:T(8,128)(2,1)S(1)}, bf16[48,1536]{1,0:T(8,128)(2,1)S(1)}, u32[]{:S(2)}, u32[]{:S(2)}) collective-permute-start(bf16[48,1536]{1,0:T(8,128)(2,1)S(1)} %slice.1462), channel_id=1, source_target_pairs={{0,32},{1,97},{32,0},{33,65},{64,96},{65,33},{96,64},{97,1},{2,34}... | collective-permute-start | bytes 442376 | tf_op jit(solution)/shard_map/ppermute | solution.py:119
  392.4 10.7 %collective-permute-start.43 = (f32[16,1536]{1,0:T(8,128)S(1)}, f32[16,1536]{1,0:T(8,128)S(1)}, u32[]{:S(2)}, u32[]{:S(2)}) collective-permute-start(f32[16,1536]{1,0:T(8,128)S(1)} %slice.1141), channel_id=1, source_target_pairs={{32,0},{64,32},{96,64},{33,1},{65,33},{97,65},{34,2},{66,34},{98,6... | collective-permute-start | bytes 294920 | tf_op jit(solution)/shard_map/ppermute | solution.py:106
  393.7 23.5 %collective-permute-start.25 = (bf16[768,896]{1,0:T(8,128)(2,1)S(1)}, bf16[768,896]{1,0:T(8,128)(2,1)S(1)}, u32[]{:S(2)}, u32[]{:S(2)}) collective-permute-start(bf16[768,896]{1,0:T(8,128)(2,1)S(1)} %add_convert_fusion.1), channel_id=1, source_target_pairs={{0,2},{1,7},{2,0},{3,5},{4,6},{5,3},{6,4},{7,1},{8,10},{9,15},{10,... | collective-permute-start | bytes 4128776 | tf_op jit(solution)/shard_map/ppermute | solution.py:119
  394.8 22.4 %collective-permute-start.24 = (bf16[768,1024]{1,0:T(8,128)(2,1)S(1)}, bf16[768,1024]{1,0:T(8,128)(2,1)S(1)}, u32[]{:S(2)}, u32[]{:S(2)}) collective-permute-start(bf16[768,1024]{1,0:T(8,128)(2,1)S(1)} %convolution_convert_fusion.2), channel_id=1, source_target_pairs={{0,32},{1,97},{32,0},{33,65},{64,96},{65,33},{96,64},{97,1},{2,34}... | collective-permute-start | bytes 4718600 | tf_op jit(solution)/shard_map/ppermute | solution.py:119
  403.2 14.1 %collective-permute-start.27 = (bf16[48,1536]{1,0:T(8,128)(2,1)S(1)}, bf16[48,1536]{1,0:T(8,128)(2,1)S(1)}, u32[]{:S(2)}, u32[]{:S(2)}) collective-permute-start(bf16[48,1536]{1,0:T(8,128)(2,1)S(1)} %slice.1461), channel_id=1, source_target_pairs={{0,32},{1,97},{32,0},{33,65},{64,96},{65,33},{96,64},{97,1},{2,34}... | collective-permute-start | bytes 442376 | tf_op jit(solution)/shard_map/ppermute | solution.py:119
  404.8 19.6 %collective-permute-start.10 = (f32[256,1536]{1,0:T(8,128)S(1)}, f32[256,1536]{1,0:T(8,128)S(1)}, u32[]{:S(2)}, u32[]{:S(2)}) collective-permute-start(f32[256,1536]{1,0:T(8,128)S(1)} %copy-done.62), channel_id=1, source_target_pairs={{0,1},{1,0},{2,3},{3,2},{4,5},{5,4},{6,7},{7,6},{8,9},{9,8},{10,11... | collective-permute-start | bytes 4718600 | tf_op jit(solution)/shard_map/ppermute | solution.py:86
  406.3 17.3 %collective-permute-start.44 = (f32[256,1536]{1,0:T(8,128)S(1)}, f32[256,1536]{1,0:T(8,128)S(1)}, u32[]{:S(2)}, u32[]{:S(2)}) collective-permute-start(f32[256,1536]{1,0:T(8,128)S(1)} %slice_select_fusion), channel_id=1, source_target_pairs={{0,1},{1,0},{2,3},{3,2},{4,5},{5,4},{6,7},{7,6},{8,9},{9,8},{10,11... | collective-permute-start | bytes 4718600 | tf_op jit(solution)/shard_map/ppermute | solution.py:86
  423.6 11.1 %collective-permute-start.29 = (bf16[384,1024]{1,0:T(8,128)(2,1)S(1)}, bf16[384,1024]{1,0:T(8,128)(2,1)S(1)}, u32[]{:S(2)}, u32[]{:S(2)}) collective-permute-start(bf16[384,1024]{1,0:T(8,128)(2,1)S(1)} %slice.1451), channel_id=1, source_target_pairs={{0,96},{1,33},{32,64},{33,1},{64,32},{65,97},{96,0},{97,65},{2,98}... | collective-permute-start | bytes 2359304 | tf_op jit(solution)/shard_map/ppermute | solution.py:119
  425.5 11.8 %collective-permute-start.45 = (bf16[128,1536]{1,0:T(8,128)(2,1)S(1)}, bf16[128,1536]{1,0:T(8,128)(2,1)S(1)}, u32[]{:S(2)}, u32[]{:S(2)}) collective-permute-start(bf16[128,1536]{1,0:T(8,128)(2,1)S(1)} %get-tuple-element.272), channel_id=1, source_target_pairs={{0,0},{1,16},{8,8},{9,24},{16,1},{17,17},{24,9},{25,25},{2,2},{3,1... | collective-permute-start | bytes 1179656 | tf_op jit(solution)/shard_map/ppermute | solution.py:93
  426.3 13.5 %collective-permute-start.46 = (bf16[128,1536]{1,0:T(8,128)(2,1)S(1)}, bf16[128,1536]{1,0:T(8,128)(2,1)S(1)}, u32[]{:S(2)}, u32[]{:S(2)}) collective-permute-start(bf16[128,1536]{1,0:T(8,128)(2,1)S(1)} %get-tuple-element.273), channel_id=1, source_target_pairs={{0,8},{1,24},{8,0},{9,16},{16,9},{17,25},{24,1},{25,17},{2,10},{3,... | collective-permute-start | bytes 1179656 | tf_op jit(solution)/shard_map/ppermute | solution.py:93
  426.7 28.4 %collective-permute-start.11 = (bf16[128,1536]{1,0:T(8,128)(2,1)S(1)}, bf16[128,1536]{1,0:T(8,128)(2,1)S(1)}, u32[]{:S(2)}, u32[]{:S(2)}) collective-permute-start(bf16[128,1536]{1,0:T(8,128)(2,1)S(1)} %get-tuple-element.276), channel_id=1, source_target_pairs={{0,0},{1,16},{8,8},{9,24},{16,1},{17,17},{24,9},{25,25},{2,2},{3,1... | collective-permute-start | bytes 1179656 | tf_op jit(solution)/shard_map/ppermute | solution.py:93
  434.3 20.9 %collective-permute-start.12 = (bf16[128,1536]{1,0:T(8,128)(2,1)S(1)}, bf16[128,1536]{1,0:T(8,128)(2,1)S(1)}, u32[]{:S(2)}, u32[]{:S(2)}) collective-permute-start(bf16[128,1536]{1,0:T(8,128)(2,1)S(1)} %get-tuple-element.277), channel_id=1, source_target_pairs={{0,8},{1,24},{8,0},{9,16},{16,9},{17,25},{24,1},{25,17},{2,10},{3,... | collective-permute-start | bytes 1179656 | tf_op jit(solution)/shard_map/ppermute | solution.py:93
  435.1 22.8 %collective-permute-start.34 = (bf16[192,1024]{1,0:T(8,128)(2,1)S(1)}, bf16[192,1024]{1,0:T(8,128)(2,1)S(1)}, u32[]{:S(2)}, u32[]{:S(2)}) collective-permute-start(bf16[192,1024]{1,0:T(8,128)(2,1)S(1)} %slice.1455), channel_id=1, source_target_pairs={{0,2},{1,7},{2,0},{3,5},{4,6},{5,3},{6,4},{7,1},{8,10},{9,15},{10,... | collective-permute-start | bytes 1179656 | tf_op jit(solution)/shard_map/ppermute | solution.py:119
  437.2 20.7 %collective-permute-start.35 = (bf16[192,896]{1,0:T(8,128)(2,1)S(1)}, bf16[192,896]{1,0:T(8,128)(2,1)S(1)}, u32[]{:S(2)}, u32[]{:S(2)}) collective-permute-start(bf16[192,896]{1,0:T(8,128)(2,1)S(1)} %slice.1456), channel_id=1, source_target_pairs={{0,32},{1,97},{32,0},{33,65},{64,96},{65,33},{96,64},{97,1},{2,34}... | collective-permute-start | bytes 1032200 | tf_op jit(solution)/shard_map/ppermute | solution.py:119
  439.9 18.0 %collective-permute-start.36 = (f32[8,128]{1,0:T(8,128)S(1)}, f32[8,128]{1,0:T(8,128)S(1)}, u32[]{:S(2)}, u32[]{:S(2)}) collective-permute-start(f32[8,128]{1,0:T(8,128)S(1)} %add.1010), channel_id=1, source_target_pairs={{0,8},{1,25},{8,0},{9,17},{16,24},{17,9},{24,16},{25,1},{2,10},{3,... | collective-permute-start | bytes 12296 | tf_op jit(solution)/shard_map/ppermute | solution.py:119
  458.6 15.5 %collective-permute-start.51 = (f32[24,1536]{1,0:T(8,128)S(1)}, f32[24,1536]{1,0:T(8,128)S(1)}, u32[]{:S(2)}, u32[]{:S(2)}) collective-permute-start(f32[24,1536]{1,0:T(8,128)S(1)} %convert_add_fusion.21), channel_id=1, source_target_pairs={{0,0},{1,64},{32,32},{33,96},{64,1},{65,65},{96,33},{97,97},{2,2},... | collective-permute-start | bytes 442376 | tf_op jit(solution)/shard_map/ppermute | solution.py:102
  490.1 11.2 %collective-permute-start.53 = (f32[12]{0:T(128)S(1)}, f32[12]{0:T(128)S(1)}, u32[]{:S(2)}, u32[]{:S(2)}) collective-permute-start(f32[12]{0:T(128)S(1)} %bitcast_divide_fusion), channel_id=1, source_target_pairs={{1,0},{4,1},{7,2},{10,3},{13,4},{16,5},{19,6},{22,7},{25,8},{28,9}... | collective-permute-start | bytes 152 | tf_op jit(solution)/shard_map/ppermute | solution.py:579
  (218 other events, 1814.5 us)
Sparse Core Ops, SparseCore 0:
  14.3 73.1 all-gather.2
  90.9 102.6 all-gather.4

commit v5 on v4

--- a/solution.py
+++ b/solution.py
@@ -305,7 +305,18 @@
     theirs = jnp.where(first_core, halves[1], halves[0])
     in_rows_low = ordered(first_core, mine, swap_cores(theirs)).astype(BF16)
     out_rows_low = cross_halves(out_master).astype(BF16)
-    w_crit = lax.all_gather(in_rows_low[:, :CRIT], CHIPS, axis=0, tiled=True)
+    order_a, order_b = ("y", "z", "x"), ("z", "y", "x")
+    block = in_rows_low[:, :CRIT]
+    for turn in (1, 0):
+        block = jnp.concatenate([block, exchange(block, "x", turn)], axis=0)
+    block_a, block_b = block[:, :PART], block[:, PART:]
+    for at in (1, 0):
+        for turn in (1, 0):
+            got_a, got_b = exchange(block_a, order_a[at], turn), exchange(block_b, order_b[at], turn)
+            if at or turn:
+                block_a = jnp.concatenate([block_a, got_a], axis=0)
+                block_b = jnp.concatenate([block_b, got_b], axis=0)
+    w_a, w_b = (block_a, got_a), (block_b, got_b)
     rest_low = jnp.concatenate([in_rows_low[:, CRIT:], out_rows_low], axis=1)
     w_rest = lax.all_gather(rest_low, CHIPS, axis=0, tiled=True)
     w_gate = w_rest[:, :HALF]
@@ -315,14 +326,18 @@
         .transpose(1, 2, 0, 3, 4)
         .reshape(HALF, WIDTH)
     )
-    smalls = w_crit[:, ACT:]
-    device_at, slot_at = iota((1536, 1), 0) // 12, iota((1536, 1), 0) % 12
+    smalls = jnp.concatenate([w[:, ACT - PART :] for w in w_b], axis=0)
+    rows_a, rows_b = in_rows(order_a), in_rows(order_b)
+    device_at, slot_at = rows_b[:, None] // 12, rows_b[:, None] % 12
 
     def gather_small(columns, width, slots):
         unfold = (HALF_HEADS + columns % width == iota((LANES, columns.shape[1]), 0)).astype(BF16)
         wide = jnp.where(device_at == columns // width, mm(smalls, unfold), 0.0)
         return mm((slot_at == slots).astype(BF16), wide, TN)
 
+    gain_ab = gather_small(
+        jnp.concatenate([rows_a, rows_b])[None], 36, 5 + iota((1, 8), 1)
+    )[0]
     norm_gain = gather_small(iota((1, WIDTH), 1), 36, 5 + iota((1, 8), 1))[0]
     gate_gain = gather_small(WIDTH + core * HALF + iota((1, HALF), 1), 36, 5 + iota((1, 8), 1))[0]
     conv_at = iota((1, ACT), 1)
@@ -342,11 +357,23 @@
     own_in, own_cot = own_both[0], own_both[1]
     tokens, cot = all_both[0], all_both[1]
     halo = along_y(tokens[TOKENS - HALO :], 1)
-    extended = jnp.concatenate([tokens, halo], axis=0).astype(F32)
+    raw = jnp.concatenate([tokens, halo], axis=0)
+    pick_a, pick_b = pick(rows_a), pick(rows_b)
+    raw_a, raw_b = mm(raw, pick_a, NT), mm(raw, pick_b, NT)
+    extended = raw.astype(F32)
     inv = lax.rsqrt(jnp.mean(extended * extended, axis=1, keepdims=True) + NORM_EPS)
     normed = (extended * inv * norm_gain).astype(BF16)
-
-    crit = mm(normed, w_crit)
+    normed_a = (raw_a * inv * gain_ab[:WIDTH]).astype(BF16)
+    normed_b = (raw_b * inv * gain_ab[WIDTH:]).astype(BF16)
+    middle = WIDTH // 2
+
+    crit = jnp.concatenate(
+        [
+            mm(v[:, :middle], w[0]) + mm(v[:, middle:], w[1])
+            for v, w in ((normed_a, w_a), (normed_b, w_b))
+        ],
+        axis=1,
+    )
     ext = jnp.concatenate([crit[TOKENS + 8 :, :ACT], crit[:TOKENS, :ACT]], axis=0)
     preact = conv_weights[KERNEL] + sum(
         conv_weights[k] * ext[5 + k : 5 + k + TOKENS] for k in range(KERNEL)
@@ -432,12 +459,8 @@
         return jnp.where(even_x, jnp.stack([back0, back1]), jnp.stack([back1, back0]))
 
     order_gate, order_out = ("x", "z", "y"), ("z", "x", "y")
-    order_a, order_b = ("y", "z", "x"), ("z", "y", "x")
     normed_gate = mm(pick(in_rows(order_gate)), normed, NT).astype(BF16)
-    normed_a = mm(pick(in_rows(order_a)), normed, NT).astype(BF16)
-    normed_b = mm(pick(in_rows(order_b)), normed, NT).astype(BF16)
     gated_b = mm(pick(out_rows(order_out)), gated_low, NT).astype(BF16)
-    middle = WIDTH // 2
     first = Halving(
         [mm(normed_gate[middle:, :TOKENS], d_gate), mm(gated_b[middle:], cot)],
         [mm(normed_gate[:middle, :TOKENS], d_gate), mm(gated_b[:middle], cot)],
@@ -495,9 +518,7 @@
     ).astype(BF16)
     (d_crit,) = wait([first], d_crit)
 
-    y_of, x_of, z_of = block_order(order_b)
-    row_at = rows_of((y_of * 4 + x_of) * 4 + z_of)[:, None]
-    device_of, slot_of = row_at // 12, row_at % 12
+    device_of, slot_of = device_at, slot_at
     slot_pick = (slot_of == iota((1536, 8), 1)).astype(F32)
     conv_spread = jnp.where(conv_at // 26 == device_of, exact(slot_pick, d_conv), 0.0)
     fold = (conv_at.T % 26 + HALF_HEADS == iota((ACT, LANES), 1)).astype(BF16)
@@ -512,17 +533,24 @@
 
     def part_b(rows):
         with_riders = jnp.pad(riders[rows], ((0, 0), (CRIT - PART - LANES, 0)))
-        return mm(normed_b[rows], crit_b) + with_riders
+        return mm(normed_b[:, rows], crit_b, TN) + with_riders
 
     second = Halving(
-        [mm(normed_a[middle:], d_crit[:, :PART]), part_b(slice(middle, None))],
-        [mm(normed_a[:middle], d_crit[:, :PART]), part_b(slice(0, middle))],
+        [mm(normed_a[:, middle:], d_crit[:, :PART], TN), part_b(slice(middle, None))],
+        [mm(normed_a[:, :middle], d_crit[:, :PART], TN), part_b(slice(0, middle))],
         [order_a, order_b],
     )
 
     second.sends, d_crit_late = lax.optimization_barrier((second.sends, d_crit))
     second.start()
-    d_normed = mm(d_crit_late, w_crit, NT)
+    d_normed = 0.0
+    for part, w, choose in (
+        (d_crit_late[:, :PART], w_a, pick_a),
+        (d_crit_late[:, PART:], w_b, pick_b),
+    ):
+        there = jnp.concatenate([mm(part, w[0], NT), mm(part, w[1], NT)], axis=1)
+        high = rounded(there)
+        d_normed = d_normed + mm(high, choose) + mm(there - high, choose)
     d_halo = along_y(d_normed[TOKENS:], -1)
     d_normed = d_normed[:TOKENS] + mm(d_gate, w_gate, NT)
     d_normed = jnp.concatenate(
@@ -547,10 +575,10 @@
             head_own, input_grad = lax.optimization_barrier((head_own, input_grad))
     input_grad = input_grad.astype(F32)
     head_other = swap_cores(head_own)
-    rows_a, rows_b = second.totals
+    share_a, share_b = second.totals
     gate_rows, out_rows_grad = first.totals
 
-    rows = jnp.concatenate([rows_a, rows_b, gate_rows], axis=1)
+    rows = jnp.concatenate([share_a, share_b, gate_rows], axis=1)
     mine = jnp.where(first_core, rows[:12], rows[12:])
     theirs = jnp.where(first_core, rows[12:], rows[:12])
     theirs = swap_cores(theirs)

time: 518 us -> 564 us (1.089)
  waiting for transfers between devices: 131 us -> 100 us
  starting transfers between devices: 102 us -> 131 us
  matrix products: 129 us -> 157 us
  other arithmetic: 75.4 us -> 87 us
    all_gather x1 -> x0, waiting for transfers between devices: 28.8 us -> none  [on_device(): w_crit = lax.all_gather(in_rows_low[:, :CRIT], CHIPS, axis=0, tiled=True)]
    dot_general x23 -> x34, matrix products: 86.7 us -> 114 us  [mm(): lax.dot_general(a.astype(BF16), b.astype(BF16), (dims, ((), ())), preferr...]
    ppermute x30 -> x40, starting transfers between devices: 47 us -> 63.2 us  [exchange(): return lax.ppermute(value, axes, pairs)]
    ppermute x30 -> x40, waiting for transfers between devices: 58.6 us -> 71.5 us  [exchange(): return lax.ppermute(value, axes, pairs)]
    ppermute x6, waiting for transfers between devices: 11 us -> 0.02 us  [regroup(): return lax.ppermute(value, ('x', 'c'), pairs)]
    concatenate x1 -> x12, other arithmetic: 0.02 us -> 8.52 us  [the longest x3 4.19 us: on_device(): block_a = jnp.concatenate([block_a, got_a], axis=0)]
    unnamed x412 -> x499, local copies, waits for them, and re-layouts: 30.4 us -> 30.7 us
  transfers between devices with their start and end apart: 58 -> 67, of which waited for: 22 -> 26; matrix products, arithmetic and copies ran while one was open for 33% -> 39% of each run, Pallas kernels for 0% -> 0%
where the time goes in v5:
time: 564 us; the launch traced here: 556 us
  matrix products  157 us (28%)
  starting transfers between devices  131 us (23%)
  waiting for transfers between devices  100 us (18%)
  other arithmetic  87 us (15%)
  local copies, waits for them, and re-layouts  61.4 us (11%)
  between operations  18.7 us (3%)
    dot_general x34, matrix products, mm(): lax.dot_general(a.astype(BF16), b.astype(BF16), (dims, ((), ())), preferr...  114 us
    ppermute x40, waiting for transfers between devices, exchange(): return lax.ppermute(value, axes, pairs)  71.5 us
    ppermute x40, starting transfers between devices, exchange(): return lax.ppermute(value, axes, pairs)  63.2 us
    unnamed x499, local copies, waits for them, and re-layouts  30.7 us
    ppermute x8, starting transfers between devices, along_y(): lax.ppermute(value, 'y', [(y, y + steps) for y in range(4) if 0 <= y + st...  22.9 us
    ppermute x7, starting transfers between devices, swap_cores(): return lax.ppermute(value, 'c', [(0, 1), (1, 0)])  21.7 us
    ppermute x8, waiting for transfers between devices, along_y(): lax.ppermute(value, 'y', [(y, y + steps) for y in range(4) if 0 <= y + st...  19.6 us
    dot_general x9, matrix products, exact(): lax.dot_general(a, b, (dims, ((), ())), precision=PRECISE, preferred_elem...  17.5 us
  transfers between devices with their start and end apart: 67, of which 26 were waited for; matrix products, arithmetic and copies ran while one was open for 39% of the time, Pallas kernels for 0%

profile of v5, /device:TPU:7, one launch (start us, length us, event | category | flops | bytes accessed | tf_op | source)
XLA Modules:
  0.0 556.0 jit_solution(13281212711365654416)
XLA Ops:
  8.8 5.4 collective-permute-start.18
  35.2 7.6 %collective-permute-done.3 = bf16[24,1920]{1,0:T(8,128)(2,1)S(1)} collective-permute-done((bf16[24,1920]{1,0:T(8,128)(2,1)S(1)}, bf16[24,1920]{1,0:T(8,128)(2,1)S(1)}, u32[]{:S(2)}, u32[]{:S(2)}) %collective-permute-start.3) | collective-permute-done | bytes 92192 | tf_op jit(solution)/shard_map/ppermute | solution.py:119
  44.2 4.2 collective-permute-done.4
  71.8 4.9 collective-permute-done.7
  92.2 6.6 %collective-permute-done.8 = bf16[768,896]{1,0:T(8,128)(2,1)S(1)} collective-permute-done((bf16[768,896]{1,0:T(8,128)(2,1)S(1)}, bf16[768,896]{1,0:T(8,128)(2,1)S(1)}, u32[]{:S(2)}, u32[]{:S(2)}) %collective-permute-start.8) | collective-permute-done | bytes 1376288 | tf_op jit(solution)/shard_map/ppermute | solution.py:119
  100.0 4.9 fusion.69
  137.7 4.6 fusion.323
  147.6 4.5 fusion.64
  170.8 4.7 collective-permute-start.17
  175.5 8.7 %collective-permute-start.16 = (f32[1544,128]{1,0:T(8,128)}, f32[1544,128]{1,0:T(8,128)S(1)}, u32[]{:S(2)}, u32[]{:S(2)}) collective-permute-start(f32[1544,128]{1,0:T(8,128)} %pad_maximum_fusion.13), channel_id=1, source_target_pairs={{0,64},{32,96},{1,65},{33,97},{2,66},{34,98},{3,67},{35,99},{4,68}... | collective-permute-start | bytes 2371592 | tf_op jit(solution)/shard_map/ppermute | solution.py:106
  197.2 15.3 %collective-permute-done.15 = f32[1544,128]{1,0:T(8,128)} collective-permute-done((f32[1544,128]{1,0:T(8,128)}, f32[1544,128]{1,0:T(8,128)}, u32[]{:S(2)}, u32[]{:S(2)}) %collective-permute-start.15) | collective-permute-done | bytes 790560 | tf_op jit(solution)/shard_map/ppermute | solution.py:106
  214.0 5.1 add_bitcast_fusion
  230.8 4.3 fusion.103
  236.4 10.0 %multiply_reduce_fusion.7 = (f32[512]{0:T(512)S(1)}, f32[512]{0:T(512)S(1)}, f32[512,1536]{1,0:T(8,128)}, f32[512,1536]{1,0:T(8,128)}, f32[512,1536]{1,0:T(8,128)}) fusion(f32[512,1536]{1,0:T(8,128)} %fusion.103, f32[1536]{0:T(1024)S(1)} %copy-done.158, f32[512,1792]{1,0:T(8,128)S(1)} %copy-done.3, f32[1536]{0:T(1024)S(1)} %copy-done.140, ...), kind=kOutput, calls=%fused_computation.108 | convolution fusion | flops 2426928128 | bytes 31477760 | tf_op jit(solution)/shard_map/dot_general | solution.py:47
  246.4 7.3 %collective-permute-start.19 = (f32[512,2]{0,1:T(2,128)S(1)}, f32[512,2]{0,1:T(2,128)S(1)}, u32[]{:S(2)}, u32[]{:S(2)}) collective-permute-start(f32[512,2]{0,1:T(2,128)S(1)} %pad_maximum_fusion.28), channel_id=1, source_target_pairs={{0,1},{1,0},{2,3},{3,2},{4,5},{5,4},{6,7},{7,6},{8,9},{9,8},{10,11... | collective-permute-start | bytes 12296 | tf_op jit(solution)/shard_map/ppermute | solution.py:86
  254.6 5.7 %fusion.301 = f32[512,1536]{1,0:T(8,128)S(1)} fusion(bf16[1536,1536]{1,0:T(8,128)(2,1)} %bitcast.376, f32[512,1536]{1,0:T(8,128)} %get-tuple-element.203, f32[512]{0:T(512)S(1)} %bitcast.462, f32[1536]{0:T(1024)S(1)} %copy-done.158), kind=kOutput, calls=%fused_computation.660 | convolution fusion | flops 2418278400 | bytes 11018240 | tf_op jit(solution)/shard_map/dot_general | solution.py:47
  304.0 4.3 collective-permute-start.23
  319.0 10.1 %collective-permute-done.24 = bf16[768,1536]{1,0:T(8,128)(2,1)} collective-permute-done((bf16[768,1536]{1,0:T(8,128)(2,1)}, bf16[768,1536]{1,0:T(8,128)(2,1)}, u32[]{:S(2)}, u32[]{:S(2)}) %collective-permute-start.24) | collective-permute-done | bytes 2359328 | tf_op jit(solution)/shard_map/ppermute | solution.py:119
  329.0 5.9 %collective-permute-done.23 = bf16[768,1536]{1,0:T(8,128)(2,1)} collective-permute-done((bf16[768,1536]{1,0:T(8,128)(2,1)}, bf16[768,1536]{1,0:T(8,128)(2,1)}, u32[]{:S(2)}, u32[]{:S(2)}) %collective-permute-start.23) | collective-permute-done | bytes 2359328 | tf_op jit(solution)/shard_map/ppermute | solution.py:119
  356.8 10.9 %collective-permute-done.28 = bf16[384,1536]{1,0:T(8,128)(2,1)S(1)} collective-permute-done((bf16[384,1536]{1,0:T(8,128)(2,1)S(1)}, bf16[384,1536]{1,0:T(8,128)(2,1)S(1)}, u32[]{:S(2)}, u32[]{:S(2)}) %collective-permute-start.28) | collective-permute-done | bytes 1179680 | tf_op jit(solution)/shard_map/ppermute | solution.py:119
  379.0 6.2 %collective-permute-start.38 = (f32[8,128]{1,0:T(8,128)S(1)}, f32[8,128]{1,0:T(8,128)S(1)}, u32[]{:S(2)}, u32[]{:S(2)}) collective-permute-start(f32[8,128]{1,0:T(8,128)S(1)} %select_maximum_fusion.1), channel_id=1, source_target_pairs={{0,32},{1,97},{32,0},{33,65},{64,96},{65,33},{96,64},{97,1},{2,34}... | collective-permute-start | bytes 12296 | tf_op jit(solution)/shard_map/ppermute | solution.py:119
  390.9 4.2 collective-permute-done.30
  402.9 4.1 select_convert_fusion.1
  418.5 4.6 fusion
  423.1 4.6 fusion.1
  438.4 4.7 fusion.3
  443.1 7.9 %add_add_fusion.1 = f32[528,1536]{1,0:T(8,128)S(1)} fusion(f32[528,1536]{1,0:T(8,128)} %fusion, f32[528,1536]{1,0:T(8,128)} %fusion.1, f32[528,1536]{1,0:T(8,128)} %fusion.3, s32[1536]{0:T(1024)S(1)} %copy-done.135, f32[528,768]{1,0:T(8,128)} %copy-done.211, f32[528,768]{1,0:T(8,128)} %copy-done.212), kind=kOutput, calls=%fused_computation.81 | convolution fusion | flops 2498641920 | bytes 16226304 | tf_op jit(solution)/shard_map/dot_general | solution.py:47
  472.1 7.1 %collective-permute-done.40 = bf16[384,896]{1,0:T(8,128)(2,1)S(1)} collective-permute-done((bf16[384,896]{1,0:T(8,128)(2,1)S(1)}, bf16[384,896]{1,0:T(8,128)(2,1)S(1)}, u32[]{:S(2)}, u32[]{:S(2)}) %collective-permute-start.40) | collective-permute-done | bytes 688160 | tf_op jit(solution)/shard_map/ppermute | solution.py:119
  484.6 13.6 %collective-permute-start.46 = (f32[8,128]{1,0:T(8,128)S(1)}, f32[8,128]{1,0:T(8,128)S(1)}, u32[]{:S(2)}, u32[]{:S(2)}) collective-permute-start(f32[8,128]{1,0:T(8,128)S(1)} %add.1038), channel_id=1, source_target_pairs={{0,8},{1,25},{8,0},{9,17},{16,24},{17,9},{24,16},{25,1},{2,10},{3,... | collective-permute-start | bytes 12296 | tf_op jit(solution)/shard_map/ppermute | solution.py:119
  502.0 5.1 collective-permute-start.61
  519.8 8.1 %collective-permute-start.65 = (f32[8,128]{1,0:T(8,128)S(1)}, f32[8,128]{1,0:T(8,128)S(1)}, u32[]{:S(2)}, u32[]{:S(2)}) collective-permute-start(f32[8,128]{1,0:T(8,128)S(1)} %add.1088), channel_id=1, source_target_pairs={{0,1},{1,0},{2,3},{3,2},{4,5},{5,4},{6,7},{7,6},{8,9},{9,8},{10,11... | collective-permute-start | bytes 12296 | tf_op jit(solution)/shard_map/ppermute | solution.py:86
  533.4 5.7 %collective-permute-start.63 = (f32[12]{0:T(128)S(1)}, f32[12]{0:T(128)S(1)}, u32[]{:S(2)}, u32[]{:S(2)}) collective-permute-start(f32[12]{0:T(128)S(1)} %bitcast_divide_fusion), channel_id=1, source_target_pairs={{1,0},{4,1},{7,2},{10,3},{13,4},{16,5},{19,6},{22,7},{25,8},{28,9}... | collective-permute-start | bytes 152 | tf_op jit(solution)/shard_map/ppermute | solution.py:607
  (943 shorter events, 326.6 us)
Async XLA Ops:
  7.2 218.2 %all-gather.2.cloned.1.call-start = ((), (), s32[]{:S(2)}) async-start(), calls=%async_computation | async-start | bytes 9584640 | tf_op jit(solution)/shard_map/all_gather | solution.py:321
  8.8 61.4 %collective-permute-start.18 = (bf16[24,1536]{1,0:T(8,128)(2,1)}, bf16[24,1536]{1,0:T(8,128)(2,1)}, u32[]{:S(2)}, u32[]{:S(2)}) collective-permute-start(bf16[24,1536]{1,0:T(8,128)(2,1)} %convert.150), channel_id=1, source_target_pairs={{0,0},{1,64},{32,32},{33,96},{64,1},{65,65},{96,33},{97,97},{2,2},... | collective-permute-start | bytes 221192 | tf_op jit(solution)/shard_map/ppermute | solution.py:102
  18.5 15.0 %collective-permute-start.2 = (bf16[12,3456]{1,0:T(8,128)(2,1)S(1)}, bf16[12,3456]{1,0:T(8,128)(2,1)S(1)}, u32[]{:S(2)}, u32[]{:S(2)}) collective-permute-start(bf16[12,3456]{1,0:T(8,128)(2,1)S(1)} %get-tuple-element.305), channel_id=1, source_target_pairs={{0,1},{1,0},{2,3},{3,2},{4,5},{5,4},{6,7},{7,6},{8,9},{9,8},{10,11... | collective-permute-start | bytes 248840 | tf_op jit(solution)/shard_map/ppermute | solution.py:86
  20.6 38.2 %collective-permute-start = (bf16[2,128,1536]{2,1,0:T(8,128)(2,1)S(1)}, bf16[2,128,1536]{2,1,0:T(8,128)(2,1)}, u32[]{:S(2)}, u32[]{:S(2)}) collective-permute-start(bf16[2,128,1536]{2,1,0:T(8,128)(2,1)S(1)} %get-tuple-element.271), channel_id=1, source_target_pairs={{0,0},{1,16},{8,8},{9,24},{16,1},{17,17},{24,9},{25,25},{2,2},{3,1... | collective-permute-start | bytes 2359304 | tf_op jit(solution)/shard_map/ppermute | solution.py:93
  22.1 36.7 %collective-permute-start.1 = (bf16[2,128,1536]{2,1,0:T(8,128)(2,1)S(1)}, bf16[2,128,1536]{2,1,0:T(8,128)(2,1)}, u32[]{:S(2)}, u32[]{:S(2)}) collective-permute-start(bf16[2,128,1536]{2,1,0:T(8,128)(2,1)S(1)} %get-tuple-element.272), channel_id=1, source_target_pairs={{0,8},{1,24},{8,0},{9,16},{16,9},{17,25},{24,1},{25,17},{2,10},{3,... | collective-permute-start | bytes 2359304 | tf_op jit(solution)/shard_map/ppermute | solution.py:93
  55.0 11.9 %collective-permute-start.12 = (bf16[192,1024]{1,0:T(8,128)(2,1)}, bf16[192,1024]{1,0:T(8,128)(2,1)S(1)}, u32[]{:S(2)}, u32[]{:S(2)}) collective-permute-start(bf16[192,1024]{1,0:T(8,128)(2,1)} %pad_maximum_fusion.20), channel_id=1, source_target_pairs={{0,2},{1,7},{2,0},{3,5},{4,6},{5,3},{6,4},{7,1},{8,10},{9,15},{10,... | collective-permute-start | bytes 1179656 | tf_op jit(solution)/shard_map/ppermute | solution.py:119
  61.1 24.8 %collective-permute-start.9 = (bf16[2,256,1536]{2,1,0:T(8,128)(2,1)S(1)}, bf16[2,256,1536]{2,1,0:T(8,128)(2,1)}, u32[]{:S(2)}, u32[]{:S(2)}) collective-permute-start(bf16[2,256,1536]{2,1,0:T(8,128)(2,1)S(1)} %maximum_select_fusion.1), channel_id=1, source_target_pairs={{0,1},{1,0},{2,3},{3,2},{4,5},{5,4},{6,7},{7,6},{8,9},{9,8},{10,11... | collective-permute-start | bytes 4718600 | tf_op jit(solution)/shard_map/ppermute | solution.py:86
  68.0 13.1 %collective-permute-start.13 = (bf16[384,1024]{1,0:T(8,128)(2,1)}, bf16[384,1024]{1,0:T(8,128)(2,1)}, u32[]{:S(2)}, u32[]{:S(2)}) collective-permute-start(bf16[384,1024]{1,0:T(8,128)(2,1)} %pad_maximum_fusion.14), channel_id=1, source_target_pairs={{0,96},{1,33},{32,64},{33,1},{64,32},{65,97},{96,0},{97,65},{2,98}... | collective-permute-start | bytes 2359304 | tf_op jit(solution)/shard_map/ppermute | solution.py:119
  78.9 20.0 %collective-permute-start.8 = (bf16[768,896]{1,0:T(8,128)(2,1)S(1)}, bf16[768,896]{1,0:T(8,128)(2,1)S(1)}, u32[]{:S(2)}, u32[]{:S(2)}) collective-permute-start(bf16[768,896]{1,0:T(8,128)(2,1)S(1)} %pad_maximum_fusion.12), channel_id=1, source_target_pairs={{0,2},{1,7},{2,0},{3,5},{4,6},{5,3},{6,4},{7,1},{8,10},{9,15},{10,... | collective-permute-start | bytes 4128776 | tf_op jit(solution)/shard_map/ppermute | solution.py:119
  83.5 68.5 %collective-permute-start.14 = (bf16[768,1024]{1,0:T(8,128)(2,1)}, bf16[768,1024]{1,0:T(8,128)(2,1)}, u32[]{:S(2)}, u32[]{:S(2)}) collective-permute-start(bf16[768,1024]{1,0:T(8,128)(2,1)} %pad_maximum_fusion.11), channel_id=1, source_target_pairs={{0,32},{1,97},{32,0},{33,65},{64,96},{65,33},{96,64},{97,1},{2,34}... | collective-permute-start | bytes 4718600 | tf_op jit(solution)/shard_map/ppermute | solution.py:119
  170.8 43.2 %collective-permute-start.17 = (f32[1544,128]{1,0:T(8,128)}, f32[1544,128]{1,0:T(8,128)}, u32[]{:S(2)}, u32[]{:S(2)}) collective-permute-start(f32[1544,128]{1,0:T(8,128)} %pad_maximum_fusion.13), channel_id=1, source_target_pairs={{0,96},{1,97},{2,98},{3,99},{4,100},{5,101},{6,102},{7,103},{8,104... | collective-permute-start | bytes 2371592 | tf_op jit(solution)/shard_map/ppermute | solution.py:106
  175.5 20.1 %collective-permute-start.16 = (f32[1544,128]{1,0:T(8,128)}, f32[1544,128]{1,0:T(8,128)S(1)}, u32[]{:S(2)}, u32[]{:S(2)}) collective-permute-start(f32[1544,128]{1,0:T(8,128)} %pad_maximum_fusion.13), channel_id=1, source_target_pairs={{0,64},{32,96},{1,65},{33,97},{2,66},{34,98},{3,67},{35,99},{4,68}... | collective-permute-start | bytes 2371592 | tf_op jit(solution)/shard_map/ppermute | solution.py:106
  184.2 28.3 %collective-permute-start.15 = (f32[1544,128]{1,0:T(8,128)}, f32[1544,128]{1,0:T(8,128)}, u32[]{:S(2)}, u32[]{:S(2)}) collective-permute-start(f32[1544,128]{1,0:T(8,128)} %pad_maximum_fusion.13), channel_id=1, source_target_pairs={{0,32},{32,64},{64,96},{1,33},{33,65},{65,97},{2,34},{34,66},{66,9... | collective-permute-start | bytes 2371592 | tf_op jit(solution)/shard_map/ppermute | solution.py:106
  275.9 41.2 %collective-permute-start.27 = (bf16[1552,128]{1,0:T(8,128)(2,1)}, bf16[1552,128]{1,0:T(8,128)(2,1)}, u32[]{:S(2)}, u32[]{:S(2)}) collective-permute-start(bf16[1552,128]{1,0:T(8,128)(2,1)} %pad_maximum_fusion.18), channel_id=1, source_target_pairs={{96,0},{97,1},{98,2},{99,3},{100,4},{101,5},{102,6},{103,7},{104,8... | collective-permute-start | bytes 1191944 | tf_op jit(solution)/shard_map/ppermute | solution.py:106
  277.2 38.2 %collective-permute-start.26 = (bf16[1552,128]{1,0:T(8,128)(2,1)}, bf16[1552,128]{1,0:T(8,128)(2,1)S(1)}, u32[]{:S(2)}, u32[]{:S(2)}) collective-permute-start(bf16[1552,128]{1,0:T(8,128)(2,1)} %pad_maximum_fusion.18), channel_id=1, source_target_pairs={{64,0},{96,32},{65,1},{97,33},{66,2},{98,34},{67,3},{99,35},{68,4}... | collective-permute-start | bytes 1191944 | tf_op jit(solution)/shard_map/ppermute | solution.py:106
  278.5 37.8 %collective-permute-start.25 = (bf16[1552,128]{1,0:T(8,128)(2,1)}, bf16[1552,128]{1,0:T(8,128)(2,1)}, u32[]{:S(2)}, u32[]{:S(2)}) collective-permute-start(bf16[1552,128]{1,0:T(8,128)(2,1)} %pad_maximum_fusion.18), channel_id=1, source_target_pairs={{32,0},{64,32},{96,64},{33,1},{65,33},{97,65},{34,2},{66,34},{98,6... | collective-permute-start | bytes 1191944 | tf_op jit(solution)/shard_map/ppermute | solution.py:106
  299.7 29.3 %collective-permute-start.24 = (bf16[768,1536]{1,0:T(8,128)(2,1)}, bf16[768,1536]{1,0:T(8,128)(2,1)}, u32[]{:S(2)}, u32[]{:S(2)}) collective-permute-start(bf16[768,1536]{1,0:T(8,128)(2,1)} %convolution_convert_fusion), channel_id=1, source_target_pairs={{0,2},{1,7},{2,0},{3,5},{4,6},{5,3},{6,4},{7,1},{8,10},{9,15},{10,... | collective-permute-start | bytes 7077896 | tf_op jit(solution)/shard_map/ppermute | solution.py:119
  304.0 30.9 %collective-permute-start.23 = (bf16[768,1536]{1,0:T(8,128)(2,1)}, bf16[768,1536]{1,0:T(8,128)(2,1)}, u32[]{:S(2)}, u32[]{:S(2)}) collective-permute-start(bf16[768,1536]{1,0:T(8,128)(2,1)} %convolution_convert_fusion.1), channel_id=1, source_target_pairs={{0,8},{1,25},{8,0},{9,17},{16,24},{17,9},{24,16},{25,1},{2,10},{3,... | collective-permute-start | bytes 7077896 | tf_op jit(solution)/shard_map/ppermute | solution.py:119
  352.3 15.4 %collective-permute-start.28 = (bf16[384,1536]{1,0:T(8,128)(2,1)S(1)}, bf16[384,1536]{1,0:T(8,128)(2,1)S(1)}, u32[]{:S(2)}, u32[]{:S(2)}) collective-permute-start(bf16[384,1536]{1,0:T(8,128)(2,1)S(1)} %slice.1481), channel_id=1, source_target_pairs={{0,24},{1,9},{8,16},{9,1},{16,8},{17,25},{24,0},{25,17},{2,26},{3,... | collective-permute-start | bytes 3538952 | tf_op jit(solution)/shard_map/ppermute | solution.py:119
  352.4 16.0 %collective-permute-start.29 = (bf16[384,1536]{1,0:T(8,128)(2,1)}, bf16[384,1536]{1,0:T(8,128)(2,1)S(1)}, u32[]{:S(2)}, u32[]{:S(2)}) collective-permute-start(bf16[384,1536]{1,0:T(8,128)(2,1)} %slice.1480), channel_id=1, source_target_pairs={{0,6},{1,3},{2,4},{3,1},{4,2},{5,7},{6,0},{7,5},{8,14},{9,11},{10,... | collective-permute-start | bytes 3538952 | tf_op jit(solution)/shard_map/ppermute | solution.py:119
  379.0 78.6 %collective-permute-start.38 = (f32[8,128]{1,0:T(8,128)S(1)}, f32[8,128]{1,0:T(8,128)S(1)}, u32[]{:S(2)}, u32[]{:S(2)}) collective-permute-start(f32[8,128]{1,0:T(8,128)S(1)} %select_maximum_fusion.1), channel_id=1, source_target_pairs={{0,32},{1,97},{32,0},{33,65},{64,96},{65,33},{96,64},{97,1},{2,34}... | collective-permute-start | bytes 12296 | tf_op jit(solution)/shard_map/ppermute | solution.py:119
  427.7 34.7 %collective-permute-start.36 = (bf16[48,1536]{1,0:T(8,128)(2,1)S(1)}, bf16[48,1536]{1,0:T(8,128)(2,1)S(1)}, u32[]{:S(2)}, u32[]{:S(2)}) collective-permute-start(bf16[48,1536]{1,0:T(8,128)(2,1)S(1)} %slice.1493), channel_id=1, source_target_pairs={{0,32},{1,97},{32,0},{33,65},{64,96},{65,33},{96,64},{97,1},{2,34}... | collective-permute-start | bytes 442376 | tf_op jit(solution)/shard_map/ppermute | solution.py:119
  428.1 34.5 %collective-permute-start.35 = (bf16[768,896]{1,0:T(8,128)(2,1)S(1)}, bf16[768,896]{1,0:T(8,128)(2,1)S(1)}, u32[]{:S(2)}, u32[]{:S(2)}) collective-permute-start(bf16[768,896]{1,0:T(8,128)(2,1)S(1)} %add_convert_fusion.1), channel_id=1, source_target_pairs={{0,2},{1,7},{2,0},{3,5},{4,6},{5,3},{6,4},{7,1},{8,10},{9,15},{10,... | collective-permute-start | bytes 4128776 | tf_op jit(solution)/shard_map/ppermute | solution.py:119
  429.6 33.0 %collective-permute-start.34 = (bf16[768,1024]{1,0:T(8,128)(2,1)S(1)}, bf16[768,1024]{1,0:T(8,128)(2,1)S(1)}, u32[]{:S(2)}, u32[]{:S(2)}) collective-permute-start(bf16[768,1024]{1,0:T(8,128)(2,1)S(1)} %convolution_convert_fusion.2), channel_id=1, source_target_pairs={{0,32},{1,97},{32,0},{33,65},{64,96},{65,33},{96,64},{97,1},{2,34}... | collective-permute-start | bytes 4718600 | tf_op jit(solution)/shard_map/ppermute | solution.py:119
  467.7 12.0 %collective-permute-start.39 = (bf16[384,1024]{1,0:T(8,128)(2,1)S(1)}, bf16[384,1024]{1,0:T(8,128)(2,1)S(1)}, u32[]{:S(2)}, u32[]{:S(2)}) collective-permute-start(bf16[384,1024]{1,0:T(8,128)(2,1)S(1)} %slice.1482), channel_id=1, source_target_pairs={{0,96},{1,33},{32,64},{33,1},{64,32},{65,97},{96,0},{97,65},{2,98}... | collective-permute-start | bytes 2359304 | tf_op jit(solution)/shard_map/ppermute | solution.py:119
  470.8 13.6 %collective-permute-start.56 = (bf16[128,1536]{1,0:T(8,128)(2,1)S(1)}, bf16[128,1536]{1,0:T(8,128)(2,1)S(1)}, u32[]{:S(2)}, u32[]{:S(2)}) collective-permute-start(bf16[128,1536]{1,0:T(8,128)(2,1)S(1)} %get-tuple-element.275), channel_id=1, source_target_pairs={{0,8},{1,24},{8,0},{9,16},{16,9},{17,25},{24,1},{25,17},{2,10},{3,... | collective-permute-start | bytes 1179656 | tf_op jit(solution)/shard_map/ppermute | solution.py:93
  471.4 26.8 %collective-permute-start.21 = (bf16[128,1536]{1,0:T(8,128)(2,1)S(1)}, bf16[128,1536]{1,0:T(8,128)(2,1)S(1)}, u32[]{:S(2)}, u32[]{:S(2)}) collective-permute-start(bf16[128,1536]{1,0:T(8,128)(2,1)S(1)} %get-tuple-element.278), channel_id=1, source_target_pairs={{0,0},{1,16},{8,8},{9,24},{16,1},{17,17},{24,9},{25,25},{2,2},{3,1... | collective-permute-start | bytes 1179656 | tf_op jit(solution)/shard_map/ppermute | solution.py:93
  479.2 19.1 %collective-permute-start.22 = (bf16[128,1536]{1,0:T(8,128)(2,1)S(1)}, bf16[128,1536]{1,0:T(8,128)(2,1)S(1)}, u32[]{:S(2)}, u32[]{:S(2)}) collective-permute-start(bf16[128,1536]{1,0:T(8,128)(2,1)S(1)} %get-tuple-element.279), channel_id=1, source_target_pairs={{0,8},{1,24},{8,0},{9,16},{16,9},{17,25},{24,1},{25,17},{2,10},{3,... | collective-permute-start | bytes 1179656 | tf_op jit(solution)/shard_map/ppermute | solution.py:93
  480.1 21.3 %collective-permute-start.44 = (bf16[192,1024]{1,0:T(8,128)(2,1)S(1)}, bf16[192,1024]{1,0:T(8,128)(2,1)S(1)}, u32[]{:S(2)}, u32[]{:S(2)}) collective-permute-start(bf16[192,1024]{1,0:T(8,128)(2,1)S(1)} %slice.1486), channel_id=1, source_target_pairs={{0,2},{1,7},{2,0},{3,5},{4,6},{5,3},{6,4},{7,1},{8,10},{9,15},{10,... | collective-permute-start | bytes 1179656 | tf_op jit(solution)/shard_map/ppermute | solution.py:119
  481.6 19.8 %collective-permute-start.45 = (bf16[192,896]{1,0:T(8,128)(2,1)S(1)}, bf16[192,896]{1,0:T(8,128)(2,1)S(1)}, u32[]{:S(2)}, u32[]{:S(2)}) collective-permute-start(bf16[192,896]{1,0:T(8,128)(2,1)S(1)} %slice.1487), channel_id=1, source_target_pairs={{0,32},{1,97},{32,0},{33,65},{64,96},{65,33},{96,64},{97,1},{2,34}... | collective-permute-start | bytes 1032200 | tf_op jit(solution)/shard_map/ppermute | solution.py:119
  484.6 16.8 %collective-permute-start.46 = (f32[8,128]{1,0:T(8,128)S(1)}, f32[8,128]{1,0:T(8,128)S(1)}, u32[]{:S(2)}, u32[]{:S(2)}) collective-permute-start(f32[8,128]{1,0:T(8,128)S(1)} %add.1038), channel_id=1, source_target_pairs={{0,8},{1,25},{8,0},{9,17},{16,24},{17,9},{24,16},{25,1},{2,10},{3,... | collective-permute-start | bytes 12296 | tf_op jit(solution)/shard_map/ppermute | solution.py:119
  502.0 15.4 %collective-permute-start.61 = (f32[24,1536]{1,0:T(8,128)S(1)}, f32[24,1536]{1,0:T(8,128)S(1)}, u32[]{:S(2)}, u32[]{:S(2)}) collective-permute-start(f32[24,1536]{1,0:T(8,128)S(1)} %convert_add_fusion.21), channel_id=1, source_target_pairs={{0,0},{1,64},{32,32},{33,96},{64,1},{65,65},{96,33},{97,97},{2,2},... | collective-permute-start | bytes 442376 | tf_op jit(solution)/shard_map/ppermute | solution.py:102
  (269 other events, 2125.1 us)
Sparse Core Ops, SparseCore 0:
  71.9 83.4 all-gather.1

commit v6 on v4

--- a/solution.py
+++ b/solution.py
@@ -305,12 +305,11 @@
     theirs = jnp.where(first_core, halves[1], halves[0])
     in_rows_low = ordered(first_core, mine, swap_cores(theirs)).astype(BF16)
     out_rows_low = cross_halves(out_master).astype(BF16)
-    w_crit = lax.all_gather(in_rows_low[:, :CRIT], CHIPS, axis=0, tiled=True)
-    rest_low = jnp.concatenate([in_rows_low[:, CRIT:], out_rows_low], axis=1)
-    w_rest = lax.all_gather(rest_low, CHIPS, axis=0, tiled=True)
-    w_gate = w_rest[:, :HALF]
+    w_in = lax.all_gather(in_rows_low, CHIPS, axis=0, tiled=True)
+    w_crit = w_in[:, :CRIT]
+    w_gate = w_in[:, CRIT:]
     w_out = (
-        w_rest[:, HALF:]
+        lax.all_gather(out_rows_low, CHIPS, axis=0, tiled=True)
         .reshape(2, 2, 16, ROWS, WIDTH)
         .transpose(1, 2, 0, 3, 4)
         .reshape(HALF, WIDTH)
@@ -543,9 +542,6 @@
         head_got = exchange(head_own, CHIPS[step // 2], step % 2)
         head_own, head_got = wait([second, first] if step < 2 else [second], head_own, head_got)
         head_own = head_own + head_got
-        if step == 4:
-            head_own, input_grad = lax.optimization_barrier((head_own, input_grad))
-    input_grad = input_grad.astype(F32)
     head_other = swap_cores(head_own)
     rows_a, rows_b = second.totals
     gate_rows, out_rows_grad = first.totals
@@ -553,7 +549,8 @@
     rows = jnp.concatenate([rows_a, rows_b, gate_rows], axis=1)
     mine = jnp.where(first_core, rows[:12], rows[12:])
     theirs = jnp.where(first_core, rows[12:], rows[:12])
-    theirs = swap_cores(theirs)
+    theirs, input_grad = lax.optimization_barrier((swap_cores(theirs), input_grad))
+    input_grad = input_grad.astype(F32)
     h0 = jnp.where(first_core, mine, theirs)
     h1 = jnp.where(first_core, theirs, mine)
     in_share = jnp.concatenate(

time: 518 us -> 583 us (1.13)
  waiting for transfers between devices: 131 us -> 181 us
  starting transfers between devices: 102 us -> 111 us
    all_gather x2, waiting for transfers between devices: 28.8 us -> 106 us  [the longest x1 78.4 us: on_device(): w_in = lax.all_gather(in_rows_low, CHIPS, axis=0, tiled=True)]
    ppermute x8, waiting for transfers between devices: 23 us -> 2.02 us  [along_y(): lax.ppermute(value, 'y', [(y, y + steps) for y in range(4) if 0 <= y + st...]
    ppermute x7, starting transfers between devices: 16.2 us -> 25.4 us  [swap_cores(): return lax.ppermute(value, 'c', [(0, 1), (1, 0)])]
    ppermute x30, waiting for transfers between devices: 58.6 us -> 51.2 us  [exchange(): return lax.ppermute(value, axes, pairs)]
    unnamed x412 -> x386, local copies, waits for them, and re-layouts: 30.4 us -> 24.3 us
  transfers between devices with their start and end apart: 58 -> 58, of which waited for: 22 -> 23; matrix products, arithmetic and copies ran while one was open for 33% -> 23% of each run, Pallas kernels for 0% -> 0%
where the time goes in v6:
time: 583 us; the launch traced here: 574 us
  waiting for transfers between devices  181 us (31%)
  matrix products  126 us (22%)
  starting transfers between devices  111 us (19%)
  other arithmetic  77.5 us (13%)
  local copies, waits for them, and re-layouts  61.3 us (11%)
  between operations  17.8 us (3%)
    dot_general x23, matrix products, mm(): lax.dot_general(a.astype(BF16), b.astype(BF16), (dims, ((), ())), preferr...  85.3 us
    all_gather x1, waiting for transfers between devices, on_device(): w_in = lax.all_gather(in_rows_low, CHIPS, axis=0, tiled=True)  78.4 us
    ppermute x30, waiting for transfers between devices, exchange(): return lax.ppermute(value, axes, pairs)  51.2 us
    ppermute x30, starting transfers between devices, exchange(): return lax.ppermute(value, axes, pairs)  44.7 us
    all_gather x1, waiting for transfers between devices, on_device(): lax.all_gather(out_rows_low, CHIPS, axis=0, tiled=True)  27.3 us
    ppermute x7, starting transfers between devices, swap_cores(): return lax.ppermute(value, 'c', [(0, 1), (1, 0)])  25.4 us
    unnamed x386, local copies, waits for them, and re-layouts  24.3 us
    ppermute x8, starting transfers between devices, along_y(): lax.ppermute(value, 'y', [(y, y + steps) for y in range(4) if 0 <= y + st...  18.3 us
  transfers between devices with their start and end apart: 58, of which 23 were waited for; matrix products, arithmetic and copies ran while one was open for 23% of the time, Pallas kernels for 0%

profile of v6, /device:TPU:7, one launch (start us, length us, event | category | flops | bytes accessed | tf_op | source)
XLA Modules:
  0.0 574.4 jit_solution(6276002514236055492)
XLA Ops:
  8.2 5.4 collective-permute-start.8
  33.5 11.5 %collective-permute-done.1 = bf16[2,128,1536]{2,1,0:T(8,128)(2,1)S(1)} collective-permute-done((bf16[2,128,1536]{2,1,0:T(8,128)(2,1)S(1)}, bf16[2,128,1536]{2,1,0:T(8,128)(2,1)S(1)}, u32[]{:S(2)}, u32[]{:S(2)}) %collective-permute-start.1) | collective-permute-done | bytes 786464 | tf_op jit(solution)/shard_map/ppermute | solution.py:93
  45.6 4.5 collective-permute-start.3
  59.4 27.3 %all-gather.5.cloned.1.call-done = bf16[1536,1536]{1,0:T(8,128)(2,1)} async-done(((bf16[24,1536]{1,0:T(8,128)(2,1)}), bf16[1536,1536]{1,0:T(8,128)(2,1)}) %all-gather.5.cloned.1.call-update) | async-done | bytes 4718608 | tf_op jit(solution)/shard_map/all_gather | solution.py:312
  91.9 4.3 fusion.90
  96.2 78.4 %all-gather.3.cloned.1.call-done = bf16[1536,3456]{1,0:T(8,128)(2,1)} async-done(((bf16[24,3456]{1,0:T(8,128)(2,1)}), bf16[1536,3456]{1,0:T(8,128)(2,1)}) %all-gather.3.cloned.1.call-update) | async-done | bytes 10616848 | tf_op jit(solution)/shard_map/all_gather | solution.py:308
  178.8 4.7 fusion.52
  194.6 4.9 fusion.59
  202.3 8.7 %fusion.30 = (f32[512,1792]{1,0:T(8,128)S(1)}, f32[512,1792]{1,0:T(8,128)}) fusion(f32[512,1792]{1,0:T(8,128)} %slice.989, f32[1792]{0:T(1024)S(1)} %get-tuple-element.175, f32[8,1792]{1,0:T(8,128)S(1)} %slice.988, f32[1792]{0:T(1024)S(1)} %get-tuple-element.176, f32[1792]{0:T(1024)S(1)} %get-tuple-element.177, f32[1792]{0:T(1024)S(1)} %get-tuple-element.178, ...), kind=kLoop, calls=%fused_computation.58 | loop fusion | flops 13762560 | bytes 11103232 | tf_op jit(solution)/shard_map/mul | solution.py:354
  220.2 5.4 collective-permute-start.7
  230.3 4.4 fusion.53
  234.7 4.3 fusion.54
  258.4 4.4 fusion.100
  268.2 5.1 add_bitcast_fusion
  278.2 12.0 %multiply_reduce_fusion.7 = (f32[512]{0:T(512)S(1)}, f32[512]{0:T(512)S(1)}, f32[512,1536]{1,0:T(8,128)}, f32[512,1536]{1,0:T(8,128)}, f32[512,1536]{1,0:T(8,128)}) fusion(f32[512,1536]{1,0:T(8,128)} %fusion.90, f32[1536]{0:T(1024)S(1)} %copy-done.105, f32[512,1792]{1,0:T(8,128)S(1)} %copy-done.1, f32[1536]{0:T(1024)S(1)} %copy-done.95, ...), kind=kOutput, calls=%fused_computation.91 | convolution fusion | flops 2426928128 | bytes 31473664 | tf_op jit(solution)/shard_map/dot_general | solution.py:47
  292.4 5.7 fusion.279
  298.5 5.4 multiply_reduce_fusion.4
  352.9 12.8 %collective-permute-done.14 = bf16[768,1536]{1,0:T(8,128)(2,1)} collective-permute-done((bf16[768,1536]{1,0:T(8,128)(2,1)}, bf16[768,1536]{1,0:T(8,128)(2,1)}, u32[]{:S(2)}, u32[]{:S(2)}) %collective-permute-start.14) | collective-permute-done | bytes 2359328 | tf_op jit(solution)/shard_map/ppermute | solution.py:119
  365.6 4.1 collective-permute-done.13
  369.8 3.8 convert_add_fusion.1
  392.6 10.6 %collective-permute-done.18 = bf16[384,1536]{1,0:T(8,128)(2,1)S(1)} collective-permute-done((bf16[384,1536]{1,0:T(8,128)(2,1)}, bf16[384,1536]{1,0:T(8,128)(2,1)S(1)}, u32[]{:S(2)}, u32[]{:S(2)}) %collective-permute-start.18) | collective-permute-done | bytes 1179680 | tf_op jit(solution)/shard_map/ppermute | solution.py:119
  414.1 5.4 collective-permute-start.28
  423.6 5.8 %collective-permute-done.20 = bf16[192,1536]{1,0:T(8,128)(2,1)S(1)} collective-permute-done((bf16[192,1536]{1,0:T(8,128)(2,1)S(1)}, bf16[192,1536]{1,0:T(8,128)(2,1)S(1)}, u32[]{:S(2)}, u32[]{:S(2)}) %collective-permute-start.20) | collective-permute-done | bytes 589856 | tf_op jit(solution)/shard_map/ppermute | solution.py:119
  437.8 4.0 select_convert_fusion
  466.6 11.3 %collective-permute-start.10 = (f32[256,1536]{1,0:T(8,128)S(1)}, f32[256,1536]{1,0:T(8,128)S(1)}, u32[]{:S(2)}, u32[]{:S(2)}) collective-permute-start(f32[256,1536]{1,0:T(8,128)S(1)} %copy-done.56), channel_id=1, source_target_pairs={{0,1},{1,0},{2,3},{3,2},{4,5},{5,4},{6,7},{7,6},{8,9},{9,8},{10,11... | collective-permute-start | bytes 4718600 | tf_op jit(solution)/shard_map/ppermute | solution.py:86
  488.3 7.5 %collective-permute-done.30 = bf16[384,896]{1,0:T(8,128)(2,1)S(1)} collective-permute-done((bf16[384,896]{1,0:T(8,128)(2,1)S(1)}, bf16[384,896]{1,0:T(8,128)(2,1)S(1)}, u32[]{:S(2)}, u32[]{:S(2)}) %collective-permute-start.30) | collective-permute-done | bytes 688160 | tf_op jit(solution)/shard_map/ppermute | solution.py:119
  497.6 4.1 collective-permute-start.35
  501.9 12.5 %collective-permute-start.36 = (f32[8,128]{1,0:T(8,128)S(1)}, f32[8,128]{1,0:T(8,128)S(1)}, u32[]{:S(2)}, u32[]{:S(2)}) collective-permute-start(f32[8,128]{1,0:T(8,128)S(1)} %add.1010), channel_id=1, source_target_pairs={{0,8},{1,25},{8,0},{9,17},{16,24},{17,9},{24,16},{25,1},{2,10},{3,... | collective-permute-start | bytes 12296 | tf_op jit(solution)/shard_map/ppermute | solution.py:119
  519.1 6.2 %collective-permute-start.51 = (f32[24,1536]{1,0:T(8,128)S(1)}, f32[24,1536]{1,0:T(8,128)S(1)}, u32[]{:S(2)}, u32[]{:S(2)}) collective-permute-start(f32[24,1536]{1,0:T(8,128)S(1)} %convert_add_fusion.21), channel_id=1, source_target_pairs={{0,0},{1,64},{32,32},{33,96},{64,1},{65,65},{96,33},{97,97},{2,2},... | collective-permute-start | bytes 442376 | tf_op jit(solution)/shard_map/ppermute | solution.py:102
  530.8 4.4 collective-permute-done.41
  538.8 8.1 %collective-permute-start.55 = (f32[8,128]{1,0:T(8,128)S(1)}, f32[8,128]{1,0:T(8,128)S(1)}, u32[]{:S(2)}, u32[]{:S(2)}) collective-permute-start(f32[8,128]{1,0:T(8,128)S(1)} %add.1057), channel_id=1, source_target_pairs={{0,1},{1,0},{2,3},{3,2},{4,5},{5,4},{6,7},{7,6},{8,9},{9,8},{10,11... | collective-permute-start | bytes 12296 | tf_op jit(solution)/shard_map/ppermute | solution.py:86
  552.3 5.3 collective-permute-start.53
  (782 shorter events, 254.3 us)
Async XLA Ops:
  7.2 79.5 %all-gather.5.cloned.1.call-start = ((), (), s32[]{:S(2)}) async-start(), calls=%async_computation.1 | async-start | bytes 4792320 | tf_op jit(solution)/shard_map/all_gather | solution.py:312
  16.2 158.4 %all-gather.3.cloned.1.call-start = ((), (), s32[]{:S(2)}) async-start(), calls=%async_computation | async-start | bytes 10782720 | tf_op jit(solution)/shard_map/all_gather | solution.py:308
  25.5 19.5 %collective-permute-start.1 = (bf16[2,128,1536]{2,1,0:T(8,128)(2,1)S(1)}, bf16[2,128,1536]{2,1,0:T(8,128)(2,1)S(1)}, u32[]{:S(2)}, u32[]{:S(2)}) collective-permute-start(bf16[2,128,1536]{2,1,0:T(8,128)(2,1)S(1)} %get-tuple-element.270), channel_id=1, source_target_pairs={{0,8},{1,24},{8,0},{9,16},{16,9},{17,25},{24,1},{25,17},{2,10},{3,... | collective-permute-start | bytes 2359304 | tf_op jit(solution)/shard_map/ppermute | solution.py:93
  220.2 48.0 %collective-permute-start.7 = (f32[1544,128]{1,0:T(8,128)}, f32[1544,128]{1,0:T(8,128)}, u32[]{:S(2)}, u32[]{:S(2)}) collective-permute-start(f32[1544,128]{1,0:T(8,128)} %pad_maximum_fusion.8), channel_id=1, source_target_pairs={{0,96},{1,97},{2,98},{3,99},{4,100},{5,101},{6,102},{7,103},{8,104... | collective-permute-start | bytes 2371592 | tf_op jit(solution)/shard_map/ppermute | solution.py:106
  225.6 37.1 %collective-permute-start.6 = (f32[1544,128]{1,0:T(8,128)}, f32[1544,128]{1,0:T(8,128)}, u32[]{:S(2)}, u32[]{:S(2)}) collective-permute-start(f32[1544,128]{1,0:T(8,128)} %pad_maximum_fusion.8), channel_id=1, source_target_pairs={{0,64},{32,96},{1,65},{33,97},{2,66},{34,98},{3,67},{35,99},{4,68}... | collective-permute-start | bytes 2371592 | tf_op jit(solution)/shard_map/ppermute | solution.py:106
  227.8 37.7 %collective-permute-start.5 = (f32[1544,128]{1,0:T(8,128)}, f32[1544,128]{1,0:T(8,128)}, u32[]{:S(2)}, u32[]{:S(2)}) collective-permute-start(f32[1544,128]{1,0:T(8,128)} %pad_maximum_fusion.8), channel_id=1, source_target_pairs={{0,32},{32,64},{64,96},{1,33},{33,65},{65,97},{2,34},{34,66},{66,9... | collective-permute-start | bytes 2371592 | tf_op jit(solution)/shard_map/ppermute | solution.py:106
  312.7 38.3 %collective-permute-start.17 = (bf16[1552,128]{1,0:T(8,128)(2,1)}, bf16[1552,128]{1,0:T(8,128)(2,1)}, u32[]{:S(2)}, u32[]{:S(2)}) collective-permute-start(bf16[1552,128]{1,0:T(8,128)(2,1)} %pad_maximum_fusion.11), channel_id=1, source_target_pairs={{96,0},{97,1},{98,2},{99,3},{100,4},{101,5},{102,6},{103,7},{104,8... | collective-permute-start | bytes 1191944 | tf_op jit(solution)/shard_map/ppermute | solution.py:106
  314.0 35.3 %collective-permute-start.16 = (bf16[1552,128]{1,0:T(8,128)(2,1)}, bf16[1552,128]{1,0:T(8,128)(2,1)S(1)}, u32[]{:S(2)}, u32[]{:S(2)}) collective-permute-start(bf16[1552,128]{1,0:T(8,128)(2,1)} %pad_maximum_fusion.11), channel_id=1, source_target_pairs={{64,0},{96,32},{65,1},{97,33},{66,2},{98,34},{67,3},{99,35},{68,4}... | collective-permute-start | bytes 1191944 | tf_op jit(solution)/shard_map/ppermute | solution.py:106
  315.3 34.9 %collective-permute-start.15 = (bf16[1552,128]{1,0:T(8,128)(2,1)}, bf16[1552,128]{1,0:T(8,128)(2,1)}, u32[]{:S(2)}, u32[]{:S(2)}) collective-permute-start(bf16[1552,128]{1,0:T(8,128)(2,1)} %pad_maximum_fusion.11), channel_id=1, source_target_pairs={{32,0},{64,32},{96,64},{33,1},{65,33},{97,65},{34,2},{66,34},{98,6... | collective-permute-start | bytes 1191944 | tf_op jit(solution)/shard_map/ppermute | solution.py:106
  336.3 29.3 %collective-permute-start.14 = (bf16[768,1536]{1,0:T(8,128)(2,1)}, bf16[768,1536]{1,0:T(8,128)(2,1)}, u32[]{:S(2)}, u32[]{:S(2)}) collective-permute-start(bf16[768,1536]{1,0:T(8,128)(2,1)} %convolution_convert_fusion), channel_id=1, source_target_pairs={{0,2},{1,7},{2,0},{3,5},{4,6},{5,3},{6,4},{7,1},{8,10},{9,15},{10,... | collective-permute-start | bytes 7077896 | tf_op jit(solution)/shard_map/ppermute | solution.py:119
  340.3 29.5 %collective-permute-start.13 = (bf16[768,1536]{1,0:T(8,128)(2,1)}, bf16[768,1536]{1,0:T(8,128)(2,1)}, u32[]{:S(2)}, u32[]{:S(2)}) collective-permute-start(bf16[768,1536]{1,0:T(8,128)(2,1)} %convolution_convert_fusion.1), channel_id=1, source_target_pairs={{0,8},{1,25},{8,0},{9,17},{16,24},{17,9},{24,16},{25,1},{2,10},{3,... | collective-permute-start | bytes 7077896 | tf_op jit(solution)/shard_map/ppermute | solution.py:119
  387.6 15.6 %collective-permute-start.18 = (bf16[384,1536]{1,0:T(8,128)(2,1)}, bf16[384,1536]{1,0:T(8,128)(2,1)S(1)}, u32[]{:S(2)}, u32[]{:S(2)}) collective-permute-start(bf16[384,1536]{1,0:T(8,128)(2,1)} %slice.1445), channel_id=1, source_target_pairs={{0,24},{1,9},{8,16},{9,1},{16,8},{17,25},{24,0},{25,17},{2,26},{3,... | collective-permute-start | bytes 3538952 | tf_op jit(solution)/shard_map/ppermute | solution.py:119
  387.6 15.8 %collective-permute-start.19 = (bf16[384,1536]{1,0:T(8,128)(2,1)}, bf16[384,1536]{1,0:T(8,128)(2,1)S(1)}, u32[]{:S(2)}, u32[]{:S(2)}) collective-permute-start(bf16[384,1536]{1,0:T(8,128)(2,1)} %slice.1444), channel_id=1, source_target_pairs={{0,6},{1,3},{2,4},{3,1},{4,2},{5,7},{6,0},{7,5},{8,14},{9,11},{10,... | collective-permute-start | bytes 3538952 | tf_op jit(solution)/shard_map/ppermute | solution.py:119
  414.1 51.4 %collective-permute-start.28 = (f32[8,128]{1,0:T(8,128)S(1)}, f32[8,128]{1,0:T(8,128)S(1)}, u32[]{:S(2)}, u32[]{:S(2)}) collective-permute-start(f32[8,128]{1,0:T(8,128)S(1)} %select_maximum_fusion.1), channel_id=1, source_target_pairs={{0,32},{1,97},{32,0},{33,65},{64,96},{65,33},{96,64},{97,1},{2,34}... | collective-permute-start | bytes 12296 | tf_op jit(solution)/shard_map/ppermute | solution.py:119
  419.5 9.9 %collective-permute-start.20 = (bf16[192,1536]{1,0:T(8,128)(2,1)S(1)}, bf16[192,1536]{1,0:T(8,128)(2,1)S(1)}, u32[]{:S(2)}, u32[]{:S(2)}) collective-permute-start(bf16[192,1536]{1,0:T(8,128)(2,1)S(1)} %slice.1449), channel_id=1, source_target_pairs={{0,2},{1,7},{2,0},{3,5},{4,6},{5,3},{6,4},{7,1},{8,10},{9,15},{10,... | collective-permute-start | bytes 1769480 | tf_op jit(solution)/shard_map/ppermute | solution.py:119
  448.4 29.6 %collective-permute-start.26 = (bf16[48,1536]{1,0:T(8,128)(2,1)S(1)}, bf16[48,1536]{1,0:T(8,128)(2,1)S(1)}, u32[]{:S(2)}, u32[]{:S(2)}) collective-permute-start(bf16[48,1536]{1,0:T(8,128)(2,1)S(1)} %slice.1457), channel_id=1, source_target_pairs={{0,32},{1,97},{32,0},{33,65},{64,96},{65,33},{96,64},{97,1},{2,34}... | collective-permute-start | bytes 442376 | tf_op jit(solution)/shard_map/ppermute | solution.py:119
  451.3 26.6 %collective-permute-start.25 = (bf16[768,896]{1,0:T(8,128)(2,1)}, bf16[768,896]{1,0:T(8,128)(2,1)S(1)}, u32[]{:S(2)}, u32[]{:S(2)}) collective-permute-start(bf16[768,896]{1,0:T(8,128)(2,1)} %add_convert_fusion.1), channel_id=1, source_target_pairs={{0,2},{1,7},{2,0},{3,5},{4,6},{5,3},{6,4},{7,1},{8,10},{9,15},{10,... | collective-permute-start | bytes 4128776 | tf_op jit(solution)/shard_map/ppermute | solution.py:119
  452.3 25.6 %collective-permute-start.24 = (bf16[768,1024]{1,0:T(8,128)(2,1)S(1)}, bf16[768,1024]{1,0:T(8,128)(2,1)S(1)}, u32[]{:S(2)}, u32[]{:S(2)}) collective-permute-start(bf16[768,1024]{1,0:T(8,128)(2,1)S(1)} %convolution_convert_fusion.2), channel_id=1, source_target_pairs={{0,32},{1,97},{32,0},{33,65},{64,96},{65,33},{96,64},{97,1},{2,34}... | collective-permute-start | bytes 4718600 | tf_op jit(solution)/shard_map/ppermute | solution.py:119
  465.2 12.8 %collective-permute-start.27 = (bf16[48,1536]{1,0:T(8,128)(2,1)S(1)}, bf16[48,1536]{1,0:T(8,128)(2,1)S(1)}, u32[]{:S(2)}, u32[]{:S(2)}) collective-permute-start(bf16[48,1536]{1,0:T(8,128)(2,1)S(1)} %slice.1456), channel_id=1, source_target_pairs={{0,32},{1,97},{32,0},{33,65},{64,96},{65,33},{96,64},{97,1},{2,34}... | collective-permute-start | bytes 442376 | tf_op jit(solution)/shard_map/ppermute | solution.py:119
  466.6 19.1 %collective-permute-start.10 = (f32[256,1536]{1,0:T(8,128)S(1)}, f32[256,1536]{1,0:T(8,128)S(1)}, u32[]{:S(2)}, u32[]{:S(2)}) collective-permute-start(f32[256,1536]{1,0:T(8,128)S(1)} %copy-done.56), channel_id=1, source_target_pairs={{0,1},{1,0},{2,3},{3,2},{4,5},{5,4},{6,7},{7,6},{8,9},{9,8},{10,11... | collective-permute-start | bytes 4718600 | tf_op jit(solution)/shard_map/ppermute | solution.py:86
  484.1 11.8 %collective-permute-start.29 = (bf16[384,1024]{1,0:T(8,128)(2,1)S(1)}, bf16[384,1024]{1,0:T(8,128)(2,1)S(1)}, u32[]{:S(2)}, u32[]{:S(2)}) collective-permute-start(bf16[384,1024]{1,0:T(8,128)(2,1)S(1)} %slice.1446), channel_id=1, source_target_pairs={{0,96},{1,33},{32,64},{33,1},{64,32},{65,97},{96,0},{97,65},{2,98}... | collective-permute-start | bytes 2359304 | tf_op jit(solution)/shard_map/ppermute | solution.py:119
  485.7 10.2 %collective-permute-start.30 = (bf16[384,896]{1,0:T(8,128)(2,1)S(1)}, bf16[384,896]{1,0:T(8,128)(2,1)S(1)}, u32[]{:S(2)}, u32[]{:S(2)}) collective-permute-start(bf16[384,896]{1,0:T(8,128)(2,1)S(1)} %slice.1447), channel_id=1, source_target_pairs={{0,6},{1,3},{2,4},{3,1},{4,2},{5,7},{6,0},{7,5},{8,14},{9,11},{10,... | collective-permute-start | bytes 2064392 | tf_op jit(solution)/shard_map/ppermute | solution.py:119
  486.7 10.9 %collective-permute-start.49 = (bf16[128,1536]{1,0:T(8,128)(2,1)S(1)}, bf16[128,1536]{1,0:T(8,128)(2,1)S(1)}, u32[]{:S(2)}, u32[]{:S(2)}) collective-permute-start(bf16[128,1536]{1,0:T(8,128)(2,1)S(1)} %get-tuple-element.272), channel_id=1, source_target_pairs={{0,0},{1,16},{8,8},{9,24},{16,1},{17,17},{24,9},{25,25},{2,2},{3,1... | collective-permute-start | bytes 1179656 | tf_op jit(solution)/shard_map/ppermute | solution.py:93
  487.5 14.2 %collective-permute-start.50 = (bf16[128,1536]{1,0:T(8,128)(2,1)S(1)}, bf16[128,1536]{1,0:T(8,128)(2,1)S(1)}, u32[]{:S(2)}, u32[]{:S(2)}) collective-permute-start(bf16[128,1536]{1,0:T(8,128)(2,1)S(1)} %get-tuple-element.273), channel_id=1, source_target_pairs={{0,8},{1,24},{8,0},{9,16},{16,9},{17,25},{24,1},{25,17},{2,10},{3,... | collective-permute-start | bytes 1179656 | tf_op jit(solution)/shard_map/ppermute | solution.py:93
  487.6 26.8 %collective-permute-start.11 = (bf16[128,1536]{1,0:T(8,128)(2,1)S(1)}, bf16[128,1536]{1,0:T(8,128)(2,1)S(1)}, u32[]{:S(2)}, u32[]{:S(2)}) collective-permute-start(bf16[128,1536]{1,0:T(8,128)(2,1)S(1)} %get-tuple-element.276), channel_id=1, source_target_pairs={{0,0},{1,16},{8,8},{9,24},{16,1},{17,17},{24,9},{25,25},{2,2},{3,1... | collective-permute-start | bytes 1179656 | tf_op jit(solution)/shard_map/ppermute | solution.py:93
  495.9 18.5 %collective-permute-start.12 = (bf16[128,1536]{1,0:T(8,128)(2,1)S(1)}, bf16[128,1536]{1,0:T(8,128)(2,1)S(1)}, u32[]{:S(2)}, u32[]{:S(2)}) collective-permute-start(bf16[128,1536]{1,0:T(8,128)(2,1)S(1)} %get-tuple-element.277), channel_id=1, source_target_pairs={{0,8},{1,24},{8,0},{9,16},{16,9},{17,25},{24,1},{25,17},{2,10},{3,... | collective-permute-start | bytes 1179656 | tf_op jit(solution)/shard_map/ppermute | solution.py:93
  496.2 22.2 %collective-permute-start.34 = (bf16[192,1024]{1,0:T(8,128)(2,1)S(1)}, bf16[192,1024]{1,0:T(8,128)(2,1)S(1)}, u32[]{:S(2)}, u32[]{:S(2)}) collective-permute-start(bf16[192,1024]{1,0:T(8,128)(2,1)S(1)} %slice.1450), channel_id=1, source_target_pairs={{0,2},{1,7},{2,0},{3,5},{4,6},{5,3},{6,4},{7,1},{8,10},{9,15},{10,... | collective-permute-start | bytes 1179656 | tf_op jit(solution)/shard_map/ppermute | solution.py:119
  497.6 20.8 %collective-permute-start.35 = (bf16[192,896]{1,0:T(8,128)(2,1)S(1)}, bf16[192,896]{1,0:T(8,128)(2,1)S(1)}, u32[]{:S(2)}, u32[]{:S(2)}) collective-permute-start(bf16[192,896]{1,0:T(8,128)(2,1)S(1)} %slice.1451), channel_id=1, source_target_pairs={{0,32},{1,97},{32,0},{33,65},{64,96},{65,33},{96,64},{97,1},{2,34}... | collective-permute-start | bytes 1032200 | tf_op jit(solution)/shard_map/ppermute | solution.py:119
  501.9 16.5 %collective-permute-start.36 = (f32[8,128]{1,0:T(8,128)S(1)}, f32[8,128]{1,0:T(8,128)S(1)}, u32[]{:S(2)}, u32[]{:S(2)}) collective-permute-start(f32[8,128]{1,0:T(8,128)S(1)} %add.1010), channel_id=1, source_target_pairs={{0,8},{1,25},{8,0},{9,17},{16,24},{17,9},{24,16},{25,1},{2,10},{3,... | collective-permute-start | bytes 12296 | tf_op jit(solution)/shard_map/ppermute | solution.py:119
  519.1 17.9 %collective-permute-start.51 = (f32[24,1536]{1,0:T(8,128)S(1)}, f32[24,1536]{1,0:T(8,128)S(1)}, u32[]{:S(2)}, u32[]{:S(2)}) collective-permute-start(f32[24,1536]{1,0:T(8,128)S(1)} %convert_add_fusion.21), channel_id=1, source_target_pairs={{0,0},{1,64},{32,32},{33,96},{64,1},{65,65},{96,33},{97,97},{2,2},... | collective-permute-start | bytes 442376 | tf_op jit(solution)/shard_map/ppermute | solution.py:102
  551.1 10.6 %collective-permute-start.54 = (f32[12]{0:T(128)S(1)}, f32[12]{0:T(128)S(1)}, u32[]{:S(2)}, u32[]{:S(2)}) collective-permute-start(f32[12]{0:T(128)S(1)} %bitcast_divide_fusion), channel_id=1, source_target_pairs={{2,0},{5,1},{8,2},{11,3},{14,4},{17,5},{20,6},{23,7},{26,8},{29,9}... | collective-permute-start | bytes 152 | tf_op jit(solution)/shard_map/ppermute | solution.py:576
  552.3 11.2 %collective-permute-start.53 = (f32[12]{0:T(128)S(1)}, f32[12]{0:T(128)S(1)}, u32[]{:S(2)}, u32[]{:S(2)}) collective-permute-start(f32[12]{0:T(128)S(1)} %bitcast_divide_fusion), channel_id=1, source_target_pairs={{1,0},{4,1},{7,2},{10,3},{13,4},{16,5},{19,6},{22,7},{25,8},{28,9}... | collective-permute-start | bytes 152 | tf_op jit(solution)/shard_map/ppermute | solution.py:576
  (203 other events, 2932.8 us)
Sparse Core Ops, SparseCore 0:
  16.3 70.3 all-gather.4
  90.2 84.4 all-gather.2

commit v7 on v6

--- a/solution.py
+++ b/solution.py
@@ -305,6 +305,11 @@
     theirs = jnp.where(first_core, halves[1], halves[0])
     in_rows_low = ordered(first_core, mine, swap_cores(theirs)).astype(BF16)
     out_rows_low = cross_halves(out_master).astype(BF16)
+    both = jnp.stack([block_in, cotangent], axis=1)
+    flipped = both[::-1]
+    got = [regroup(jnp.where(even_x, both, flipped)[k], k) for k in range(2)]
+    own_both = ordered(even_x, got[0], got[1], axis=1)
+    out_rows_low, own_both = lax.optimization_barrier((out_rows_low, own_both))
     w_in = lax.all_gather(in_rows_low, CHIPS, axis=0, tiled=True)
     w_crit = w_in[:, :CRIT]
     w_gate = w_in[:, CRIT:]
@@ -333,10 +338,6 @@
     )
     decay_rate = -jnp.exp(head_half[0])
 
-    both = jnp.stack([block_in, cotangent], axis=1)
-    flipped = both[::-1]
-    got = [regroup(jnp.where(even_x, both, flipped)[k], k) for k in range(2)]
-    own_both = ordered(even_x, got[0], got[1], axis=1)
     all_both = ordered(first_core, own_both, swap_cores(own_both), axis=1)
     own_in, own_cot = own_both[0], own_both[1]
     tokens, cot = all_both[0], all_both[1]
@@ -535,13 +536,16 @@
     d_tokens = own_inv * d_own - (own_inv * own_inv * own_inv) * own * jnp.mean(
         own * d_own, axis=1, keepdims=True
     )
-    input_grad = to_owner((own_cot.astype(F32) + d_tokens).astype(BF16))
+    returning = (own_cot.astype(F32) + d_tokens).astype(BF16)
 
     head_own = jnp.pad(d_head, ((0, 5), (0, 0)))
     for step in range(6):
         head_got = exchange(head_own, CHIPS[step // 2], step % 2)
         head_own, head_got = wait([second, first] if step < 2 else [second], head_own, head_got)
         head_own = head_own + head_got
+        if step == 3:
+            head_own, returning = lax.optimization_barrier((head_own, returning))
+            input_grad = to_owner(returning)
     head_other = swap_cores(head_own)
     rows_a, rows_b = second.totals
     gate_rows, out_rows_grad = first.totals

time: 583 us -> 614 us (1.053)
  waiting for transfers between devices: 181 us -> 195 us
  matrix products: 126 us -> 137 us
  starting transfers between devices: 111 us -> 121 us
    all_gather x1, waiting for transfers between devices: 27.3 us -> 49.9 us  [on_device(): lax.all_gather(out_rows_low, CHIPS, axis=0, tiled=True)]
    dot_general x23, matrix products: 85.3 us -> 96.1 us  [mm(): lax.dot_general(a.astype(BF16), b.astype(BF16), (dims, ((), ())), preferr...]
    ppermute x30, waiting for transfers between devices: 51.2 us -> 43.4 us  [exchange(): return lax.ppermute(value, axes, pairs)]
    ppermute x3, starting transfers between devices: 7.88 us -> 14.7 us  [on_device(): lax.ppermute(gain_rows, ALL, [(3 * d + k, d) for d in range(128) if 3 * d...]
  transfers between devices with their start and end apart: 58 -> 58, of which waited for: 23 -> 21; matrix products, arithmetic and copies ran while one was open for 23% -> 22% of each run, Pallas kernels for 0% -> 0%
where the time goes in v7:
time: 614 us; the launch traced here: 605 us
  waiting for transfers between devices  195 us (32%)
  matrix products  137 us (22%)
  starting transfers between devices  121 us (20%)
  other arithmetic  75.6 us (12%)
  local copies, waits for them, and re-layouts  58.2 us (9%)
  between operations  17.8 us (3%)
    dot_general x23, matrix products, mm(): lax.dot_general(a.astype(BF16), b.astype(BF16), (dims, ((), ())), preferr...  96.1 us
    all_gather x1, waiting for transfers between devices, on_device(): w_in = lax.all_gather(in_rows_low, CHIPS, axis=0, tiled=True)  78.5 us
    all_gather x1, waiting for transfers between devices, on_device(): lax.all_gather(out_rows_low, CHIPS, axis=0, tiled=True)  49.9 us
    ppermute x30, starting transfers between devices, exchange(): return lax.ppermute(value, axes, pairs)  43.9 us
    ppermute x30, waiting for transfers between devices, exchange(): return lax.ppermute(value, axes, pairs)  43.4 us
    ppermute x7, starting transfers between devices, swap_cores(): return lax.ppermute(value, 'c', [(0, 1), (1, 0)])  26.9 us
    unnamed x386, local copies, waits for them, and re-layouts  25.2 us
    ppermute x8, starting transfers between devices, along_y(): lax.ppermute(value, 'y', [(y, y + steps) for y in range(4) if 0 <= y + st...  18.5 us
  transfers between devices with their start and end apart: 58, of which 21 were waited for; matrix products, arithmetic and copies ran while one was open for 22% of the time, Pallas kernels for 0%

profile of v7, /device:TPU:7, one launch (start us, length us, event | category | flops | bytes accessed | tf_op | source)
XLA Modules:
  0.0 604.9 jit_solution(4542306055727172110)
XLA Ops:
  10.7 9.3 %collective-permute-start = (bf16[24,1536]{1,0:T(8,128)(2,1)S(1)}, bf16[24,1536]{1,0:T(8,128)(2,1)S(1)}, u32[]{:S(2)}, u32[]{:S(2)}) collective-permute-start(bf16[24,1536]{1,0:T(8,128)(2,1)S(1)} %convert.150), channel_id=1, source_target_pairs={{0,0},{1,64},{32,32},{33,96},{64,1},{65,65},{96,33},{97,97},{2,2},... | collective-permute-start | bytes 221192 | tf_op jit(solution)/shard_map/ppermute | solution.py:102
  20.0 8.7 %collective-permute-done.2 = bf16[2,128,1536]{2,1,0:T(8,128)(2,1)S(1)} collective-permute-done((bf16[2,128,1536]{2,1,0:T(8,128)(2,1)S(1)}, bf16[2,128,1536]{2,1,0:T(8,128)(2,1)S(1)}, u32[]{:S(2)}, u32[]{:S(2)}) %collective-permute-start.2) | collective-permute-done | bytes 786464 | tf_op jit(solution)/shard_map/ppermute | solution.py:93
  30.5 5.0 collective-permute-start.3
  54.6 49.9 %all-gather.5.cloned.1.call-done = bf16[1536,1536]{1,0:T(8,128)(2,1)} async-done(((bf16[24,1536]{1,0:T(8,128)(2,1)}), bf16[1536,1536]{1,0:T(8,128)(2,1)}) %all-gather.5.cloned.1.call-update) | async-done | bytes 4718608 | tf_op jit(solution)/shard_map/all_gather | solution.py:317
  109.7 4.3 fusion.90
  114.0 78.5 %all-gather.3.cloned.1.call-done = bf16[1536,3456]{1,0:T(8,128)(2,1)} async-done(((bf16[24,3456]{1,0:T(8,128)(2,1)}), bf16[1536,3456]{1,0:T(8,128)(2,1)}) %all-gather.3.cloned.1.call-update) | async-done | bytes 10616848 | tf_op jit(solution)/shard_map/all_gather | solution.py:313
  196.7 4.5 fusion.52
  212.2 4.9 fusion.59
  220.0 8.5 %fusion.30 = (f32[512,1792]{1,0:T(8,128)S(1)}, f32[512,1792]{1,0:T(8,128)}) fusion(f32[512,1792]{1,0:T(8,128)} %slice.988, f32[1792]{0:T(1024)S(1)} %get-tuple-element.183, f32[8,1792]{1,0:T(8,128)S(1)} %slice.987, f32[1792]{0:T(1024)S(1)} %get-tuple-element.184, f32[1792]{0:T(1024)S(1)} %get-tuple-element.185, f32[1792]{0:T(1024)S(1)} %get-tuple-element.186, ...), kind=kLoop, calls=%fused_computation.58 | loop fusion | flops 13762560 | bytes 11103232 | tf_op jit(solution)/shard_map/mul | solution.py:355
  237.7 5.4 collective-permute-start.8
  247.8 12.6 %fusion.53 = bf16[1536,528]{0,1:T(8,128)(2,1)} fusion(bf16[528,1536]{1,0:T(8,128)(2,1)S(1)} %copy-done.54, s32[1536]{0:T(1024)S(1)} %copy-done.112), kind=kOutput, calls=%fused_computation.99 | convolution fusion | flops 2494586880 | bytes 3250176 | tf_op jit(solution)/shard_map/dot_general | solution.py:47
  260.4 4.2 fusion.54
  284.0 4.4 fusion.100
  293.9 5.1 add_bitcast_fusion
  303.8 12.0 %multiply_reduce_fusion.7 = (f32[512]{0:T(512)S(1)}, f32[512]{0:T(512)S(1)}, f32[512,1536]{1,0:T(8,128)}, f32[512,1536]{1,0:T(8,128)}, f32[512,1536]{1,0:T(8,128)}) fusion(f32[512,1536]{1,0:T(8,128)} %fusion.90, f32[1536]{0:T(1024)S(1)} %copy-done.107, f32[512,1792]{1,0:T(8,128)S(1)} %copy-done.1, f32[1536]{0:T(1024)S(1)} %copy-done.96, ...), kind=kOutput, calls=%fused_computation.91 | convolution fusion | flops 2426928128 | bytes 31473664 | tf_op jit(solution)/shard_map/dot_general | solution.py:47
  318.1 5.7 fusion.279
  324.1 5.4 multiply_reduce_fusion.4
  378.6 12.7 %collective-permute-done.14 = bf16[768,1536]{1,0:T(8,128)(2,1)} collective-permute-done((bf16[768,1536]{1,0:T(8,128)(2,1)}, bf16[768,1536]{1,0:T(8,128)(2,1)}, u32[]{:S(2)}, u32[]{:S(2)}) %collective-permute-start.14) | collective-permute-done | bytes 2359328 | tf_op jit(solution)/shard_map/ppermute | solution.py:119
  391.3 4.1 collective-permute-done.13
  418.3 10.6 %collective-permute-done.18 = bf16[384,1536]{1,0:T(8,128)(2,1)S(1)} collective-permute-done((bf16[384,1536]{1,0:T(8,128)(2,1)}, bf16[384,1536]{1,0:T(8,128)(2,1)S(1)}, u32[]{:S(2)}, u32[]{:S(2)}) %collective-permute-start.18) | collective-permute-done | bytes 1179680 | tf_op jit(solution)/shard_map/ppermute | solution.py:119
  439.8 5.4 collective-permute-start.28
  449.3 5.8 collective-permute-done.20
  479.2 5.6 fusion.8
  486.3 4.5 fusion.34
  492.0 9.4 %collective-permute-start.43 = (f32[256,1536]{1,0:T(8,128)S(1)}, f32[256,1536]{1,0:T(8,128)S(1)}, u32[]{:S(2)}, u32[]{:S(2)}) collective-permute-start(f32[256,1536]{1,0:T(8,128)S(1)} %slice_select_fusion), channel_id=1, source_target_pairs={{0,1},{1,0},{2,3},{3,2},{4,5},{5,4},{6,7},{7,6},{8,9},{9,8},{10,11... | collective-permute-start | bytes 4718600 | tf_op jit(solution)/shard_map/ppermute | solution.py:86
  512.8 4.9 collective-permute-done.12
  521.2 10.4 %collective-permute-start.36 = (f32[8,128]{1,0:T(8,128)S(1)}, f32[8,128]{1,0:T(8,128)S(1)}, u32[]{:S(2)}, u32[]{:S(2)}) collective-permute-start(f32[8,128]{1,0:T(8,128)S(1)} %add.1010), channel_id=1, source_target_pairs={{0,8},{1,25},{8,0},{9,17},{16,24},{17,9},{24,16},{25,1},{2,10},{3,... | collective-permute-start | bytes 12296 | tf_op jit(solution)/shard_map/ppermute | solution.py:119
  536.5 5.1 collective-permute-start.51
  545.1 4.4 collective-permute-done.38
  560.0 10.6 %collective-permute-start.55 = (f32[8,128]{1,0:T(8,128)S(1)}, f32[8,128]{1,0:T(8,128)S(1)}, u32[]{:S(2)}, u32[]{:S(2)}) collective-permute-start(f32[8,128]{1,0:T(8,128)S(1)} %add.1057), channel_id=1, source_target_pairs={{0,1},{1,0},{2,3},{3,2},{4,5},{5,4},{6,7},{7,6},{8,9},{9,8},{10,11... | collective-permute-start | bytes 12296 | tf_op jit(solution)/shard_map/ppermute | solution.py:86
  576.0 12.1 %collective-permute-start.53 = (f32[12]{0:T(128)S(1)}, f32[12]{0:T(128)S(1)}, u32[]{:S(2)}, u32[]{:S(2)}) collective-permute-start(f32[12]{0:T(128)S(1)} %bitcast_divide_fusion), channel_id=1, source_target_pairs={{1,0},{4,1},{7,2},{10,3},{13,4},{16,5},{19,6},{22,7},{25,8},{28,9}... | collective-permute-start | bytes 152 | tf_op jit(solution)/shard_map/ppermute | solution.py:580
  591.4 5.8 collective-permute-done.52
  (780 shorter events, 247.1 us)
Async XLA Ops:
  7.2 97.4 %all-gather.5.cloned.1.call-start = ((), (), s32[]{:S(2)}) async-start(), calls=%async_computation.1 | async-start | bytes 4792320 | tf_op jit(solution)/shard_map/all_gather | solution.py:317
  9.2 10.8 %collective-permute-start.1 = (bf16[2,128,1536]{2,1,0:T(8,128)(2,1)S(1)}, bf16[2,128,1536]{2,1,0:T(8,128)(2,1)S(1)}, u32[]{:S(2)}, u32[]{:S(2)}) collective-permute-start(bf16[2,128,1536]{2,1,0:T(8,128)(2,1)S(1)} %get-tuple-element.277), channel_id=1, source_target_pairs={{0,0},{1,16},{8,8},{9,24},{16,1},{17,17},{24,9},{25,25},{2,2},{3,1... | collective-permute-start | bytes 2359304 | tf_op jit(solution)/shard_map/ppermute | solution.py:93
  10.1 18.6 %collective-permute-start.2 = (bf16[2,128,1536]{2,1,0:T(8,128)(2,1)S(1)}, bf16[2,128,1536]{2,1,0:T(8,128)(2,1)S(1)}, u32[]{:S(2)}, u32[]{:S(2)}) collective-permute-start(bf16[2,128,1536]{2,1,0:T(8,128)(2,1)S(1)} %get-tuple-element.278), channel_id=1, source_target_pairs={{0,8},{1,24},{8,0},{9,16},{16,9},{17,25},{24,1},{25,17},{2,10},{3,... | collective-permute-start | bytes 2359304 | tf_op jit(solution)/shard_map/ppermute | solution.py:93
  10.7 18.6 %collective-permute-start = (bf16[24,1536]{1,0:T(8,128)(2,1)S(1)}, bf16[24,1536]{1,0:T(8,128)(2,1)S(1)}, u32[]{:S(2)}, u32[]{:S(2)}) collective-permute-start(bf16[24,1536]{1,0:T(8,128)(2,1)S(1)} %convert.150), channel_id=1, source_target_pairs={{0,0},{1,64},{32,32},{33,96},{64,1},{65,65},{96,33},{97,97},{2,2},... | collective-permute-start | bytes 221192 | tf_op jit(solution)/shard_map/ppermute | solution.py:102
  30.0 162.4 %all-gather.3.cloned.1.call-start = ((), (), s32[]{:S(2)}) async-start(), calls=%async_computation | async-start | bytes 10782720 | tf_op jit(solution)/shard_map/all_gather | solution.py:313
  237.7 56.2 %collective-permute-start.8 = (f32[1544,128]{1,0:T(8,128)}, f32[1544,128]{1,0:T(8,128)}, u32[]{:S(2)}, u32[]{:S(2)}) collective-permute-start(f32[1544,128]{1,0:T(8,128)} %pad_maximum_fusion.8), channel_id=1, source_target_pairs={{0,96},{1,97},{2,98},{3,99},{4,100},{5,101},{6,102},{7,103},{8,104... | collective-permute-start | bytes 2371592 | tf_op jit(solution)/shard_map/ppermute | solution.py:106
  243.1 45.3 %collective-permute-start.7 = (f32[1544,128]{1,0:T(8,128)}, f32[1544,128]{1,0:T(8,128)}, u32[]{:S(2)}, u32[]{:S(2)}) collective-permute-start(f32[1544,128]{1,0:T(8,128)} %pad_maximum_fusion.8), channel_id=1, source_target_pairs={{0,64},{32,96},{1,65},{33,97},{2,66},{34,98},{3,67},{35,99},{4,68}... | collective-permute-start | bytes 2371592 | tf_op jit(solution)/shard_map/ppermute | solution.py:106
  245.3 45.9 %collective-permute-start.6 = (f32[1544,128]{1,0:T(8,128)}, f32[1544,128]{1,0:T(8,128)}, u32[]{:S(2)}, u32[]{:S(2)}) collective-permute-start(f32[1544,128]{1,0:T(8,128)} %pad_maximum_fusion.8), channel_id=1, source_target_pairs={{0,32},{32,64},{64,96},{1,33},{33,65},{65,97},{2,34},{34,66},{66,9... | collective-permute-start | bytes 2371592 | tf_op jit(solution)/shard_map/ppermute | solution.py:106
  338.3 38.4 %collective-permute-start.17 = (bf16[1552,128]{1,0:T(8,128)(2,1)}, bf16[1552,128]{1,0:T(8,128)(2,1)}, u32[]{:S(2)}, u32[]{:S(2)}) collective-permute-start(bf16[1552,128]{1,0:T(8,128)(2,1)} %pad_maximum_fusion.11), channel_id=1, source_target_pairs={{96,0},{97,1},{98,2},{99,3},{100,4},{101,5},{102,6},{103,7},{104,8... | collective-permute-start | bytes 1191944 | tf_op jit(solution)/shard_map/ppermute | solution.py:106
  339.6 35.3 %collective-permute-start.16 = (bf16[1552,128]{1,0:T(8,128)(2,1)}, bf16[1552,128]{1,0:T(8,128)(2,1)S(1)}, u32[]{:S(2)}, u32[]{:S(2)}) collective-permute-start(bf16[1552,128]{1,0:T(8,128)(2,1)} %pad_maximum_fusion.11), channel_id=1, source_target_pairs={{64,0},{96,32},{65,1},{97,33},{66,2},{98,34},{67,3},{99,35},{68,4}... | collective-permute-start | bytes 1191944 | tf_op jit(solution)/shard_map/ppermute | solution.py:106
  340.9 35.0 %collective-permute-start.15 = (bf16[1552,128]{1,0:T(8,128)(2,1)}, bf16[1552,128]{1,0:T(8,128)(2,1)}, u32[]{:S(2)}, u32[]{:S(2)}) collective-permute-start(bf16[1552,128]{1,0:T(8,128)(2,1)} %pad_maximum_fusion.11), channel_id=1, source_target_pairs={{32,0},{64,32},{96,64},{33,1},{65,33},{97,65},{34,2},{66,34},{98,6... | collective-permute-start | bytes 1191944 | tf_op jit(solution)/shard_map/ppermute | solution.py:106
  362.0 29.3 %collective-permute-start.14 = (bf16[768,1536]{1,0:T(8,128)(2,1)}, bf16[768,1536]{1,0:T(8,128)(2,1)}, u32[]{:S(2)}, u32[]{:S(2)}) collective-permute-start(bf16[768,1536]{1,0:T(8,128)(2,1)} %convolution_convert_fusion), channel_id=1, source_target_pairs={{0,2},{1,7},{2,0},{3,5},{4,6},{5,3},{6,4},{7,1},{8,10},{9,15},{10,... | collective-permute-start | bytes 7077896 | tf_op jit(solution)/shard_map/ppermute | solution.py:119
  366.0 29.5 %collective-permute-start.13 = (bf16[768,1536]{1,0:T(8,128)(2,1)}, bf16[768,1536]{1,0:T(8,128)(2,1)}, u32[]{:S(2)}, u32[]{:S(2)}) collective-permute-start(bf16[768,1536]{1,0:T(8,128)(2,1)} %convolution_convert_fusion.1), channel_id=1, source_target_pairs={{0,8},{1,25},{8,0},{9,17},{16,24},{17,9},{24,16},{25,1},{2,10},{3,... | collective-permute-start | bytes 7077896 | tf_op jit(solution)/shard_map/ppermute | solution.py:119
  413.3 15.6 %collective-permute-start.18 = (bf16[384,1536]{1,0:T(8,128)(2,1)}, bf16[384,1536]{1,0:T(8,128)(2,1)S(1)}, u32[]{:S(2)}, u32[]{:S(2)}) collective-permute-start(bf16[384,1536]{1,0:T(8,128)(2,1)} %slice.1434), channel_id=1, source_target_pairs={{0,24},{1,9},{8,16},{9,1},{16,8},{17,25},{24,0},{25,17},{2,26},{3,... | collective-permute-start | bytes 3538952 | tf_op jit(solution)/shard_map/ppermute | solution.py:119
  413.3 15.8 %collective-permute-start.19 = (bf16[384,1536]{1,0:T(8,128)(2,1)}, bf16[384,1536]{1,0:T(8,128)(2,1)S(1)}, u32[]{:S(2)}, u32[]{:S(2)}) collective-permute-start(bf16[384,1536]{1,0:T(8,128)(2,1)} %slice.1433), channel_id=1, source_target_pairs={{0,6},{1,3},{2,4},{3,1},{4,2},{5,7},{6,0},{7,5},{8,14},{9,11},{10,... | collective-permute-start | bytes 3538952 | tf_op jit(solution)/shard_map/ppermute | solution.py:119
  439.8 52.2 %collective-permute-start.28 = (f32[8,128]{1,0:T(8,128)S(1)}, f32[8,128]{1,0:T(8,128)S(1)}, u32[]{:S(2)}, u32[]{:S(2)}) collective-permute-start(f32[8,128]{1,0:T(8,128)S(1)} %select_maximum_fusion.1), channel_id=1, source_target_pairs={{0,32},{1,97},{32,0},{33,65},{64,96},{65,33},{96,64},{97,1},{2,34}... | collective-permute-start | bytes 12296 | tf_op jit(solution)/shard_map/ppermute | solution.py:119
  445.2 9.9 %collective-permute-start.20 = (bf16[192,1536]{1,0:T(8,128)(2,1)S(1)}, bf16[192,1536]{1,0:T(8,128)(2,1)S(1)}, u32[]{:S(2)}, u32[]{:S(2)}) collective-permute-start(bf16[192,1536]{1,0:T(8,128)(2,1)S(1)} %slice.1438), channel_id=1, source_target_pairs={{0,2},{1,7},{2,0},{3,5},{4,6},{5,3},{6,4},{7,1},{8,10},{9,15},{10,... | collective-permute-start | bytes 1769480 | tf_op jit(solution)/shard_map/ppermute | solution.py:119
  446.9 9.9 %collective-permute-start.21 = (bf16[192,1536]{1,0:T(8,128)(2,1)S(1)}, bf16[192,1536]{1,0:T(8,128)(2,1)S(1)}, u32[]{:S(2)}, u32[]{:S(2)}) collective-permute-start(bf16[192,1536]{1,0:T(8,128)(2,1)S(1)} %slice.1437), channel_id=1, source_target_pairs={{0,8},{1,25},{8,0},{9,17},{16,24},{17,9},{24,16},{25,1},{2,10},{3,... | collective-permute-start | bytes 1769480 | tf_op jit(solution)/shard_map/ppermute | solution.py:119
  473.7 29.1 %collective-permute-start.26 = (bf16[48,1536]{1,0:T(8,128)(2,1)S(1)}, bf16[48,1536]{1,0:T(8,128)(2,1)S(1)}, u32[]{:S(2)}, u32[]{:S(2)}) collective-permute-start(bf16[48,1536]{1,0:T(8,128)(2,1)S(1)} %slice.1446), channel_id=1, source_target_pairs={{0,32},{1,97},{32,0},{33,65},{64,96},{65,33},{96,64},{97,1},{2,34}... | collective-permute-start | bytes 442376 | tf_op jit(solution)/shard_map/ppermute | solution.py:119
  475.6 27.4 %collective-permute-start.25 = (bf16[768,896]{1,0:T(8,128)(2,1)S(1)}, bf16[768,896]{1,0:T(8,128)(2,1)S(1)}, u32[]{:S(2)}, u32[]{:S(2)}) collective-permute-start(bf16[768,896]{1,0:T(8,128)(2,1)S(1)} %add_convert_fusion.1), channel_id=1, source_target_pairs={{0,2},{1,7},{2,0},{3,5},{4,6},{5,3},{6,4},{7,1},{8,10},{9,15},{10,... | collective-permute-start | bytes 4128776 | tf_op jit(solution)/shard_map/ppermute | solution.py:119
  476.7 26.3 %collective-permute-start.24 = (bf16[768,1024]{1,0:T(8,128)(2,1)S(1)}, bf16[768,1024]{1,0:T(8,128)(2,1)S(1)}, u32[]{:S(2)}, u32[]{:S(2)}) collective-permute-start(bf16[768,1024]{1,0:T(8,128)(2,1)S(1)} %convolution_convert_fusion.2), channel_id=1, source_target_pairs={{0,32},{1,97},{32,0},{33,65},{64,96},{65,33},{96,64},{97,1},{2,34}... | collective-permute-start | bytes 4718600 | tf_op jit(solution)/shard_map/ppermute | solution.py:119
  491.8 11.2 %collective-permute-start.27 = (bf16[48,1536]{1,0:T(8,128)(2,1)S(1)}, bf16[48,1536]{1,0:T(8,128)(2,1)S(1)}, u32[]{:S(2)}, u32[]{:S(2)}) collective-permute-start(bf16[48,1536]{1,0:T(8,128)(2,1)S(1)} %slice.1445), channel_id=1, source_target_pairs={{0,32},{1,97},{32,0},{33,65},{64,96},{65,33},{96,64},{97,1},{2,34}... | collective-permute-start | bytes 442376 | tf_op jit(solution)/shard_map/ppermute | solution.py:119
  492.0 14.2 %collective-permute-start.43 = (f32[256,1536]{1,0:T(8,128)S(1)}, f32[256,1536]{1,0:T(8,128)S(1)}, u32[]{:S(2)}, u32[]{:S(2)}) collective-permute-start(f32[256,1536]{1,0:T(8,128)S(1)} %slice_select_fusion), channel_id=1, source_target_pairs={{0,1},{1,0},{2,3},{3,2},{4,5},{5,4},{6,7},{7,6},{8,9},{9,8},{10,11... | collective-permute-start | bytes 4718600 | tf_op jit(solution)/shard_map/ppermute | solution.py:86
  504.0 17.2 %collective-permute-start.29 = (bf16[384,1024]{1,0:T(8,128)(2,1)S(1)}, bf16[384,1024]{1,0:T(8,128)(2,1)S(1)}, u32[]{:S(2)}, u32[]{:S(2)}) collective-permute-start(bf16[384,1024]{1,0:T(8,128)(2,1)S(1)} %slice.1435), channel_id=1, source_target_pairs={{0,96},{1,33},{32,64},{33,1},{64,32},{65,97},{96,0},{97,65},{2,98}... | collective-permute-start | bytes 2359304 | tf_op jit(solution)/shard_map/ppermute | solution.py:119
  506.1 15.1 %collective-permute-start.30 = (bf16[384,896]{1,0:T(8,128)(2,1)S(1)}, bf16[384,896]{1,0:T(8,128)(2,1)S(1)}, u32[]{:S(2)}, u32[]{:S(2)}) collective-permute-start(bf16[384,896]{1,0:T(8,128)(2,1)S(1)} %slice.1436), channel_id=1, source_target_pairs={{0,6},{1,3},{2,4},{3,1},{4,2},{5,7},{6,0},{7,5},{8,14},{9,11},{10,... | collective-permute-start | bytes 2064392 | tf_op jit(solution)/shard_map/ppermute | solution.py:119
  521.2 20.4 %collective-permute-start.36 = (f32[8,128]{1,0:T(8,128)S(1)}, f32[8,128]{1,0:T(8,128)S(1)}, u32[]{:S(2)}, u32[]{:S(2)}) collective-permute-start(f32[8,128]{1,0:T(8,128)S(1)} %add.1010), channel_id=1, source_target_pairs={{0,8},{1,25},{8,0},{9,17},{16,24},{17,9},{24,16},{25,1},{2,10},{3,... | collective-permute-start | bytes 12296 | tf_op jit(solution)/shard_map/ppermute | solution.py:119
  536.5 17.6 %collective-permute-start.51 = (f32[24,1536]{1,0:T(8,128)S(1)}, f32[24,1536]{1,0:T(8,128)S(1)}, u32[]{:S(2)}, u32[]{:S(2)}) collective-permute-start(f32[24,1536]{1,0:T(8,128)S(1)} %convert_add_fusion.21), channel_id=1, source_target_pairs={{0,0},{1,64},{32,32},{33,96},{64,1},{65,65},{96,33},{97,97},{2,2},... | collective-permute-start | bytes 442376 | tf_op jit(solution)/shard_map/ppermute | solution.py:102
  558.2 13.9 %collective-permute-start.49 = (bf16[128,1536]{1,0:T(8,128)(2,1)S(1)}, bf16[128,1536]{1,0:T(8,128)(2,1)S(1)}, u32[]{:S(2)}, u32[]{:S(2)}) collective-permute-start(bf16[128,1536]{1,0:T(8,128)(2,1)S(1)} %get-tuple-element.280), channel_id=1, source_target_pairs={{0,0},{1,16},{8,8},{9,24},{16,1},{17,17},{24,9},{25,25},{2,2},{3,1... | collective-permute-start | bytes 1179656 | tf_op jit(solution)/shard_map/ppermute | solution.py:93
  558.9 13.2 %collective-permute-start.50 = (bf16[128,1536]{1,0:T(8,128)(2,1)S(1)}, bf16[128,1536]{1,0:T(8,128)(2,1)S(1)}, u32[]{:S(2)}, u32[]{:S(2)}) collective-permute-start(bf16[128,1536]{1,0:T(8,128)(2,1)S(1)} %get-tuple-element.281), channel_id=1, source_target_pairs={{0,8},{1,24},{8,0},{9,16},{16,9},{17,25},{24,1},{25,17},{2,10},{3,... | collective-permute-start | bytes 1179656 | tf_op jit(solution)/shard_map/ppermute | solution.py:93
  560.0 11.4 %collective-permute-start.55 = (f32[8,128]{1,0:T(8,128)S(1)}, f32[8,128]{1,0:T(8,128)S(1)}, u32[]{:S(2)}, u32[]{:S(2)}) collective-permute-start(f32[8,128]{1,0:T(8,128)S(1)} %add.1057), channel_id=1, source_target_pairs={{0,1},{1,0},{2,3},{3,2},{4,5},{5,4},{6,7},{7,6},{8,9},{9,8},{10,11... | collective-permute-start | bytes 12296 | tf_op jit(solution)/shard_map/ppermute | solution.py:86
  574.7 16.7 %collective-permute-start.54 = (f32[12]{0:T(128)S(1)}, f32[12]{0:T(128)S(1)}, u32[]{:S(2)}, u32[]{:S(2)}) collective-permute-start(f32[12]{0:T(128)S(1)} %bitcast_divide_fusion), channel_id=1, source_target_pairs={{2,0},{5,1},{8,2},{11,3},{14,4},{17,5},{20,6},{23,7},{26,8},{29,9}... | collective-permute-start | bytes 152 | tf_op jit(solution)/shard_map/ppermute | solution.py:580
  576.0 15.4 %collective-permute-start.53 = (f32[12]{0:T(128)S(1)}, f32[12]{0:T(128)S(1)}, u32[]{:S(2)}, u32[]{:S(2)}) collective-permute-start(f32[12]{0:T(128)S(1)} %bitcast_divide_fusion), channel_id=1, source_target_pairs={{1,0},{4,1},{7,2},{10,3},{13,4},{16,5},{19,6},{22,7},{25,8},{28,9}... | collective-permute-start | bytes 152 | tf_op jit(solution)/shard_map/ppermute | solution.py:580
  (202 other events, 3145.8 us)
Sparse Core Ops, SparseCore 0:
  30.2 74.3 all-gather.4
  108.0 84.4 all-gather.2
